TPU v7x, 128 devices: a whole 4x4x4 slice. The times are simulated.
128 devices in a mesh: seq: 8 (over z, y_hi), head: 16 (over y_lo, x, core).
Axes of the slice: x: 4, y: 4 (y_hi: 2, y_lo: 2; y = y_hi * 2 + y_lo), z: 4, core: 2. Of those that a mesh axis runs over, the one named last changes fastest.
Arguments:
- video_q: bfloat16 [16384, 2048], P(('seq', 'head')), may hold values from -8 to 8
- video_k: bfloat16 [16384, 2048], P(('seq', 'head')), may hold values from -8 to 8
- video_v: bfloat16 [16384, 2048], P(('seq', 'head')), may hold values from -6 to 6
- video_cross_q: bfloat16 [16384, 2048], P(('seq', 'head')), may hold values from -8 to 8
- audio_q: bfloat16 [2048, 2048], P('seq', 'head'), may hold values from -8 to 8
- audio_k: bfloat16 [2048, 2048], P('seq', 'head'), may hold values from -8 to 8
- audio_v: bfloat16 [2048, 2048], P('seq', 'head'), may hold values from -6 to 6
- audio_cross_q: bfloat16 [2048, 2048], P('seq', 'head'), may hold values from -8 to 8
- out_weight: bfloat16 [2048, 3072], P('head'), may hold values from -0.125 to 0.125
Outputs:
- video_mixed: bfloat16 [16384, 3072], P(('seq', 'head'))
- audio_attn: bfloat16 [2048, 2048], P('seq', 'head')
All inputs are finite; a program needn't handle non-finite values.
Results may differ from a plain program's by a relative error of at most 0.015.
Values may be sent and summed in bfloat16 or wider, within the bound.
No kernel may reach another device: no remote copies, remote signals or barrier semaphores. Data moves between devices by JAX's collectives and lax.ppermute only.
A program may use at most 128 MiB of HBM per device.

v0:
```python
import jax
import jax.numpy as jnp
from jax import lax
from jax.sharding import PartitionSpec as P

HEAD_DIM = 128


def empty_state(row_count, head_count):
    return (
        jnp.full((row_count, head_count), -1e30, jnp.float32),
        jnp.zeros((row_count, head_count), jnp.float32),
        jnp.zeros((row_count, head_count, HEAD_DIM), jnp.float32),
    )


def attend_block(state, queries, key_block, value_block):
    running, denominator, accum = state
    scores = jnp.einsum(
        "qhd,khd->qhk", queries, key_block, preferred_element_type=jnp.float32
    ) * HEAD_DIM ** (-0.5)
    newest = jnp.maximum(running, jnp.max(scores, axis=2))
    factor = jnp.exp(running - newest)
    weights = jnp.exp(scores - newest[:, :, None])
    denominator = denominator * factor + jnp.sum(weights, axis=2)
    rounded = weights.astype(jnp.bfloat16)
    accum = accum * factor[:, :, None] + jnp.einsum(
        "qhk,khd->qhd", rounded, value_block, preferred_element_type=jnp.float32
    )
    return (newest, denominator, accum)


def attend(state, queries, key_rows, value_rows):
    head_count = queries.shape[1]
    key_count = key_rows.shape[0]
    key_heads = key_rows.reshape(key_count, head_count, HEAD_DIM)
    value_heads = value_rows.reshape(key_count, head_count, HEAD_DIM)
    block_rows = 1024

    def key_step(block_index, states):
        key_block = lax.dynamic_slice_in_dim(key_heads, block_index * block_rows, block_rows, 0)
        value_block = lax.dynamic_slice_in_dim(value_heads, block_index * block_rows, block_rows, 0)
        return attend_block(states, queries, key_block, value_block)

    return lax.fori_loop(0, key_count // block_rows, key_step, state)


def finish(state):
    running, denominator, accum = state
    result = accum / denominator[:, :, None]
    return result.reshape(result.shape[0], -1)


def local(
    video_q, video_k, video_v, video_cross_q, audio_q, audio_k, audio_v, audio_cross_q, out_weight
):
    video_query, video_key, video_value, video_cross = (
        lax.all_to_all(video_q, "head", split_axis=1, concat_axis=0, tiled=True),
        lax.all_to_all(video_k, "head", split_axis=1, concat_axis=0, tiled=True),
        lax.all_to_all(video_v, "head", split_axis=1, concat_axis=0, tiled=True),
        lax.all_to_all(video_cross_q, "head", split_axis=1, concat_axis=0, tiled=True),
    )
    video_count = video_query.shape[0]
    audio_count = audio_q.shape[0]
    head_count = video_query.shape[1] // HEAD_DIM
    video_heads = video_query.reshape(video_count, head_count, HEAD_DIM)
    video_cross_heads = video_cross.reshape(video_count, head_count, HEAD_DIM)
    audio_heads = audio_q.reshape(audio_count, head_count, HEAD_DIM)
    audio_cross_heads = audio_cross_q.reshape(audio_count, head_count, HEAD_DIM)
    states = (empty_state(video_count, head_count), empty_state(audio_count, head_count))
    shard_piece = (
        lax.all_gather(video_key, "seq", axis=0, tiled=True),
        lax.all_gather(video_value, "seq", axis=0, tiled=True),
    )
    video_self = attend(states[0], video_heads, shard_piece[0], shard_piece[1])
    audio_cross = attend(states[1], audio_cross_heads, shard_piece[0], shard_piece[1])
    states = (empty_state(audio_count, head_count), empty_state(video_count, head_count))
    shard_piece = (
        lax.all_gather(audio_k, "seq", axis=0, tiled=True),
        lax.all_gather(audio_v, "seq", axis=0, tiled=True),
    )
    audio_self = attend(states[0], audio_heads, shard_piece[0], shard_piece[1])
    video_to_audio = attend(states[1], video_cross_heads, shard_piece[0], shard_piece[1])
    video_attn = (finish(video_self) + finish(video_to_audio)).astype(jnp.bfloat16)
    audio_attn = (finish(audio_self) + finish(audio_cross)).astype(jnp.bfloat16)
    token_attn = lax.all_to_all(video_attn, "head", split_axis=0, concat_axis=1, tiled=True)
    video_mixed = jnp.dot(
        token_attn,
        lax.all_gather(out_weight, "head", axis=0, tiled=True),
        preferred_element_type=jnp.float32,
    ).astype(jnp.bfloat16)
    return (video_mixed, audio_attn)


def solution(mesh):
    return jax.shard_map(
        local,
        mesh=mesh,
        in_specs=(
            P(("seq", "head"), None),
            P(("seq", "head"), None),
            P(("seq", "head"), None),
            P(("seq", "head"), None),
            P("seq", "head"),
            P("seq", "head"),
            P("seq", "head"),
            P("seq", "head"),
            P("head", None),
        ),
        out_specs=(P(("seq", "head"), None), P("seq", "head")),
        check_vma=False,
    )
```

profile of v0, /device:TPU:64, one launch (start us, length us, event | category | flops | bytes accessed | tf_op | source)
XLA Modules:
  0.0 473.2 jit_solution(5774297512667467766)
XLA Ops:
  8.3 16.2 %all_to_all.86 = bf16[128,16,128]{2,0,1:T(8,128)(2,1)} all-to-all(bf16[128,16,128]{2,0,1:T(8,128)(2,1)S(1)} %copy_bitcast_fusion.1), channel_id=1, replica_groups=mesh['seq'=8,'head'=16] {'head'}, dimensions={1} | all-to-all | bytes 1048576 | tf_op jit(solution)/shard_map/all_to_all | solution.py:59
  25.8 14.1 %all_to_all.87 = bf16[128,16,128]{2,0,1:T(8,128)(2,1)} all-to-all(bf16[128,16,128]{2,0,1:T(8,128)(2,1)S(1)} %copy_bitcast_fusion), channel_id=1, replica_groups=mesh['seq'=8,'head'=16] {'head'}, dimensions={1} | all-to-all | bytes 1048576 | tf_op jit(solution)/shard_map/all_to_all | solution.py:60
  47.3 37.9 %all_gather.17 = bf16[2048,128]{1,0:T(8,128)(2,1)S(1)} all-gather(bf16[256,128]{1,0:T(8,128)(2,1)S(1)} %copy-done.15), channel_id=1, replica_groups=mesh['seq'=8,'head'=16] {'seq'}, dimensions={0}, use_global_device_ids=true | all-gather | bytes 589824 | tf_op jit(solution)/shard_map/all_gather | solution.py:79
  85.2 35.9 %all_gather.18 = bf16[2048,128]{1,0:T(8,128)(2,1)S(1)} all-gather(bf16[256,128]{1,0:T(8,128)(2,1)S(1)} %copy-done.16), channel_id=1, replica_groups=mesh['seq'=8,'head'=16] {'seq'}, dimensions={0}, use_global_device_ids=true | all-gather | bytes 589824 | tf_op jit(solution)/shard_map/all_gather | solution.py:80
  121.1 5.7 %all-to-all-start.3 = ((bf16[128,16,128]{0,2,1:T(8,128)(2,1)}), bf16[128,16,128]{0,2,1:T(8,128)(2,1)}, u32[]{:S(2)}, u32[]{:S(2)}) async-start(bf16[128,16,128]{0,2,1:T(8,128)(2,1)} %bitcast.11), calls=%async_computation.3 | async-start | bytes 1048576 | tf_op jit(solution)/shard_map/all_to_all | solution.py:61
  131.2 6.6 %all-to-all-done.3 = bf16[128,16,128]{0,2,1:T(8,128)(2,1)} async-done(((bf16[128,16,128]{0,2,1:T(8,128)(2,1)}), bf16[128,16,128]{0,2,1:T(8,128)(2,1)}, u32[]{:S(2)}, u32[]{:S(2)}) %all-to-all-start.3) | async-done | bytes 524320 | tf_op jit(solution)/shard_map/all_to_all | solution.py:61
  139.8 28.5 %while.73 = (s32[]{:T(128)}, f32[2048,1]{0,1:T(1,128)S(1)}, f32[2048,1]{0,1:T(1,128)}, f32[2048,1,128]{0,2,1:T(8,128)S(1)}, bf16[2048,1,128]{2,0,1:T(8,128)(2,1)...) while((s32[]{:T(128)}, f32[2048,1]{0,1:T(1,128)S(1)}, ...), condition=%wide.region_7.0_spmd.clone, body=%wide.region_4.0_spmd.clone.sunk | while | flops 1091315712 | bytes 62062848 | solution.py:45
  139.8 5.6 %multiply_reduce_fusion.5 = (f32[2048]{0:T(1024)S(1)}, f32[1024,2048]{1,0:T(8,128)}) fusion(bf16[2048,1,128]{2,0,1:T(8,128)(2,1)} %get-tuple-element.909, bf16[2048,1,128]{2,0,1:T(8,128)(2,1)} %get-tuple-element.908, s32[]{:T(128)S(6)} %select_n.41), kind=kOutput, calls=%fused_computation.29.clone.1 | convolution fusion | flops 541063168 | bytes 9183236 | tf_op jit(solution)/shard_map/while/body/eval_jaxpr/qhd,khd->qhk/dot_general | solution.py:19
  145.4 5.0 %fusion.128 = f32[2048]{0:T(1024)S(1)} fusion(f32[1024,2048]{1,0:T(8,128)} %get-tuple-element.857, f32[2048]{0:T(1024)S(1)} %bitcast.303), kind=kLoop, calls=%fused_computation.31.clone.1 | loop fusion | flops 6289408 | bytes 8404992 | tf_op jit(solution)/shard_map/while/body/eval_jaxpr/reduce_sum | solution.py:25
  154.1 5.6 %multiply_reduce_fusion.5 = (f32[2048]{0:T(1024)S(1)}, f32[1024,2048]{1,0:T(8,128)}) fusion(bf16[2048,1,128]{2,0,1:T(8,128)(2,1)} %get-tuple-element.909, bf16[2048,1,128]{2,0,1:T(8,128)(2,1)} %get-tuple-element.908, s32[]{:T(128)S(6)} %select_n.41), kind=kOutput, calls=%fused_computation.29.clone.1 | convolution fusion | flops 541063168 | bytes 9183236 | tf_op jit(solution)/shard_map/while/body/eval_jaxpr/qhd,khd->qhk/dot_general | solution.py:19
  159.7 4.9 %fusion.128 = f32[2048]{0:T(1024)S(1)} fusion(f32[1024,2048]{1,0:T(8,128)} %get-tuple-element.857, f32[2048]{0:T(1024)S(1)} %bitcast.303), kind=kLoop, calls=%fused_computation.31.clone.1 | loop fusion | flops 6289408 | bytes 8404992 | tf_op jit(solution)/shard_map/while/body/eval_jaxpr/reduce_sum | solution.py:25
  169.7 6.8 %all-gather.6.cloned.1.call-done = bf16[16384,128]{1,0:T(8,128)(2,1)} async-done(((bf16[2048,128]{1,0:T(8,128)(2,1)}), bf16[16384,128]{1,0:T(8,128)(2,1)}) %all-gather.6.cloned.1.call-update) | async-done | bytes 4194320 | tf_op jit(solution)/shard_map/all_gather | solution.py:73
  176.5 226.0 %while.72 = (s32[]{:T(128)}, f32[2048,1]{0,1:T(1,128)S(1)}, f32[2048,1]{0,1:T(1,128)S(1)}, f32[2048,1,128]{0,2,1:T(8,128)S(1)}, bf16[16384,1,128]{2,0,1:T(8,128)...) while((s32[]{:T(128)}, f32[2048,1]{0,1:T(1,128)S(1)}, ...), condition=%wide.region_3.0_spmd.clone, body=%wide.region_0.0_spmd.clone.sunk | while | flops 1091315712 | bytes 61997256 | solution.py:45
  176.5 5.5 %multiply_reduce_fusion.4 = (f32[2048]{0:T(1024)S(1)}, f32[1024,2048]{1,0:T(8,128)}) fusion(bf16[2048,1,128]{2,0,1:T(8,128)(2,1)S(1)} %get-tuple-element.942, bf16[16384,1,128]{2,0,1:T(8,128)(2,1)} %get-tuple-element.941, s32[]{:T(128)S(6)} %select_n.40), kind=kOutput, calls=%fused_computation.2.clone.1 | convolution fusion | flops 541063168 | bytes 9183236 | tf_op jit(solution)/shard_map/while/body/eval_jaxpr/qhd,khd->qhk/dot_general | solution.py:19
  182.0 4.9 %fusion.122 = f32[2048]{0:T(1024)S(1)} fusion(f32[1024,2048]{1,0:T(8,128)} %get-tuple-element.846, f32[2048]{0:T(1024)S(1)} %bitcast.305), kind=kLoop, calls=%fused_computation.4.clone.1 | loop fusion | flops 6289408 | bytes 8404992 | tf_op jit(solution)/shard_map/while/body/eval_jaxpr/reduce_sum | solution.py:25
  191.1 5.4 %multiply_reduce_fusion.4 = (f32[2048]{0:T(1024)S(1)}, f32[1024,2048]{1,0:T(8,128)}) fusion(bf16[2048,1,128]{2,0,1:T(8,128)(2,1)S(1)} %get-tuple-element.942, bf16[16384,1,128]{2,0,1:T(8,128)(2,1)} %get-tuple-element.941, s32[]{:T(128)S(6)} %select_n.40), kind=kOutput, calls=%fused_computation.2.clone.1 | convolution fusion | flops 541063168 | bytes 9183236 | tf_op jit(solution)/shard_map/while/body/eval_jaxpr/qhd,khd->qhk/dot_general | solution.py:19
  196.5 5.1 %fusion.122 = f32[2048]{0:T(1024)S(1)} fusion(f32[1024,2048]{1,0:T(8,128)} %get-tuple-element.846, f32[2048]{0:T(1024)S(1)} %bitcast.305), kind=kLoop, calls=%fused_computation.4.clone.1 | loop fusion | flops 6289408 | bytes 8404992 | tf_op jit(solution)/shard_map/while/body/eval_jaxpr/reduce_sum | solution.py:25
  205.4 5.4 %multiply_reduce_fusion.4 = (f32[2048]{0:T(1024)S(1)}, f32[1024,2048]{1,0:T(8,128)}) fusion(bf16[2048,1,128]{2,0,1:T(8,128)(2,1)S(1)} %get-tuple-element.942, bf16[16384,1,128]{2,0,1:T(8,128)(2,1)} %get-tuple-element.941, s32[]{:T(128)S(6)} %select_n.40), kind=kOutput, calls=%fused_computation.2.clone.1 | convolution fusion | flops 541063168 | bytes 9183236 | tf_op jit(solution)/shard_map/while/body/eval_jaxpr/qhd,khd->qhk/dot_general | solution.py:19
  210.8 5.1 %fusion.122 = f32[2048]{0:T(1024)S(1)} fusion(f32[1024,2048]{1,0:T(8,128)} %get-tuple-element.846, f32[2048]{0:T(1024)S(1)} %bitcast.305), kind=kLoop, calls=%fused_computation.4.clone.1 | loop fusion | flops 6289408 | bytes 8404992 | tf_op jit(solution)/shard_map/while/body/eval_jaxpr/reduce_sum | solution.py:25
  219.7 5.4 %multiply_reduce_fusion.4 = (f32[2048]{0:T(1024)S(1)}, f32[1024,2048]{1,0:T(8,128)}) fusion(bf16[2048,1,128]{2,0,1:T(8,128)(2,1)S(1)} %get-tuple-element.942, bf16[16384,1,128]{2,0,1:T(8,128)(2,1)} %get-tuple-element.941, s32[]{:T(128)S(6)} %select_n.40), kind=kOutput, calls=%fused_computation.2.clone.1 | convolution fusion | flops 541063168 | bytes 9183236 | tf_op jit(solution)/shard_map/while/body/eval_jaxpr/qhd,khd->qhk/dot_general | solution.py:19
  225.1 5.1 %fusion.122 = f32[2048]{0:T(1024)S(1)} fusion(f32[1024,2048]{1,0:T(8,128)} %get-tuple-element.846, f32[2048]{0:T(1024)S(1)} %bitcast.305), kind=kLoop, calls=%fused_computation.4.clone.1 | loop fusion | flops 6289408 | bytes 8404992 | tf_op jit(solution)/shard_map/while/body/eval_jaxpr/reduce_sum | solution.py:25
  234.1 5.4 %multiply_reduce_fusion.4 = (f32[2048]{0:T(1024)S(1)}, f32[1024,2048]{1,0:T(8,128)}) fusion(bf16[2048,1,128]{2,0,1:T(8,128)(2,1)S(1)} %get-tuple-element.942, bf16[16384,1,128]{2,0,1:T(8,128)(2,1)} %get-tuple-element.941, s32[]{:T(128)S(6)} %select_n.40), kind=kOutput, calls=%fused_computation.2.clone.1 | convolution fusion | flops 541063168 | bytes 9183236 | tf_op jit(solution)/shard_map/while/body/eval_jaxpr/qhd,khd->qhk/dot_general | solution.py:19
  239.6 5.1 %fusion.122 = f32[2048]{0:T(1024)S(1)} fusion(f32[1024,2048]{1,0:T(8,128)} %get-tuple-element.846, f32[2048]{0:T(1024)S(1)} %bitcast.305), kind=kLoop, calls=%fused_computation.4.clone.1 | loop fusion | flops 6289408 | bytes 8404992 | tf_op jit(solution)/shard_map/while/body/eval_jaxpr/reduce_sum | solution.py:25
  248.4 5.4 %multiply_reduce_fusion.4 = (f32[2048]{0:T(1024)S(1)}, f32[1024,2048]{1,0:T(8,128)}) fusion(bf16[2048,1,128]{2,0,1:T(8,128)(2,1)S(1)} %get-tuple-element.942, bf16[16384,1,128]{2,0,1:T(8,128)(2,1)} %get-tuple-element.941, s32[]{:T(128)S(6)} %select_n.40), kind=kOutput, calls=%fused_computation.2.clone.1 | convolution fusion | flops 541063168 | bytes 9183236 | tf_op jit(solution)/shard_map/while/body/eval_jaxpr/qhd,khd->qhk/dot_general | solution.py:19
  253.8 4.9 %fusion.122 = f32[2048]{0:T(1024)S(1)} fusion(f32[1024,2048]{1,0:T(8,128)} %get-tuple-element.846, f32[2048]{0:T(1024)S(1)} %bitcast.305), kind=kLoop, calls=%fused_computation.4.clone.1 | loop fusion | flops 6289408 | bytes 8404992 | tf_op jit(solution)/shard_map/while/body/eval_jaxpr/reduce_sum | solution.py:25
  262.4 5.4 %multiply_reduce_fusion.4 = (f32[2048]{0:T(1024)S(1)}, f32[1024,2048]{1,0:T(8,128)}) fusion(bf16[2048,1,128]{2,0,1:T(8,128)(2,1)S(1)} %get-tuple-element.942, bf16[16384,1,128]{2,0,1:T(8,128)(2,1)} %get-tuple-element.941, s32[]{:T(128)S(6)} %select_n.40), kind=kOutput, calls=%fused_computation.2.clone.1 | convolution fusion | flops 541063168 | bytes 9183236 | tf_op jit(solution)/shard_map/while/body/eval_jaxpr/qhd,khd->qhk/dot_general | solution.py:19
  267.8 4.9 %fusion.122 = f32[2048]{0:T(1024)S(1)} fusion(f32[1024,2048]{1,0:T(8,128)} %get-tuple-element.846, f32[2048]{0:T(1024)S(1)} %bitcast.305), kind=kLoop, calls=%fused_computation.4.clone.1 | loop fusion | flops 6289408 | bytes 8404992 | tf_op jit(solution)/shard_map/while/body/eval_jaxpr/reduce_sum | solution.py:25
  276.4 5.4 %multiply_reduce_fusion.4 = (f32[2048]{0:T(1024)S(1)}, f32[1024,2048]{1,0:T(8,128)}) fusion(bf16[2048,1,128]{2,0,1:T(8,128)(2,1)S(1)} %get-tuple-element.942, bf16[16384,1,128]{2,0,1:T(8,128)(2,1)} %get-tuple-element.941, s32[]{:T(128)S(6)} %select_n.40), kind=kOutput, calls=%fused_computation.2.clone.1 | convolution fusion | flops 541063168 | bytes 9183236 | tf_op jit(solution)/shard_map/while/body/eval_jaxpr/qhd,khd->qhk/dot_general | solution.py:19
  281.8 4.9 %fusion.122 = f32[2048]{0:T(1024)S(1)} fusion(f32[1024,2048]{1,0:T(8,128)} %get-tuple-element.846, f32[2048]{0:T(1024)S(1)} %bitcast.305), kind=kLoop, calls=%fused_computation.4.clone.1 | loop fusion | flops 6289408 | bytes 8404992 | tf_op jit(solution)/shard_map/while/body/eval_jaxpr/reduce_sum | solution.py:25
  290.4 5.4 %multiply_reduce_fusion.4 = (f32[2048]{0:T(1024)S(1)}, f32[1024,2048]{1,0:T(8,128)}) fusion(bf16[2048,1,128]{2,0,1:T(8,128)(2,1)S(1)} %get-tuple-element.942, bf16[16384,1,128]{2,0,1:T(8,128)(2,1)} %get-tuple-element.941, s32[]{:T(128)S(6)} %select_n.40), kind=kOutput, calls=%fused_computation.2.clone.1 | convolution fusion | flops 541063168 | bytes 9183236 | tf_op jit(solution)/shard_map/while/body/eval_jaxpr/qhd,khd->qhk/dot_general | solution.py:19
  295.9 4.9 %fusion.122 = f32[2048]{0:T(1024)S(1)} fusion(f32[1024,2048]{1,0:T(8,128)} %get-tuple-element.846, f32[2048]{0:T(1024)S(1)} %bitcast.305), kind=kLoop, calls=%fused_computation.4.clone.1 | loop fusion | flops 6289408 | bytes 8404992 | tf_op jit(solution)/shard_map/while/body/eval_jaxpr/reduce_sum | solution.py:25
  304.5 5.4 %multiply_reduce_fusion.4 = (f32[2048]{0:T(1024)S(1)}, f32[1024,2048]{1,0:T(8,128)}) fusion(bf16[2048,1,128]{2,0,1:T(8,128)(2,1)S(1)} %get-tuple-element.942, bf16[16384,1,128]{2,0,1:T(8,128)(2,1)} %get-tuple-element.941, s32[]{:T(128)S(6)} %select_n.40), kind=kOutput, calls=%fused_computation.2.clone.1 | convolution fusion | flops 541063168 | bytes 9183236 | tf_op jit(solution)/shard_map/while/body/eval_jaxpr/qhd,khd->qhk/dot_general | solution.py:19
  309.9 4.9 %fusion.122 = f32[2048]{0:T(1024)S(1)} fusion(f32[1024,2048]{1,0:T(8,128)} %get-tuple-element.846, f32[2048]{0:T(1024)S(1)} %bitcast.305), kind=kLoop, calls=%fused_computation.4.clone.1 | loop fusion | flops 6289408 | bytes 8404992 | tf_op jit(solution)/shard_map/while/body/eval_jaxpr/reduce_sum | solution.py:25
  318.5 5.4 %multiply_reduce_fusion.4 = (f32[2048]{0:T(1024)S(1)}, f32[1024,2048]{1,0:T(8,128)}) fusion(bf16[2048,1,128]{2,0,1:T(8,128)(2,1)S(1)} %get-tuple-element.942, bf16[16384,1,128]{2,0,1:T(8,128)(2,1)} %get-tuple-element.941, s32[]{:T(128)S(6)} %select_n.40), kind=kOutput, calls=%fused_computation.2.clone.1 | convolution fusion | flops 541063168 | bytes 9183236 | tf_op jit(solution)/shard_map/while/body/eval_jaxpr/qhd,khd->qhk/dot_general | solution.py:19
  323.9 4.9 %fusion.122 = f32[2048]{0:T(1024)S(1)} fusion(f32[1024,2048]{1,0:T(8,128)} %get-tuple-element.846, f32[2048]{0:T(1024)S(1)} %bitcast.305), kind=kLoop, calls=%fused_computation.4.clone.1 | loop fusion | flops 6289408 | bytes 8404992 | tf_op jit(solution)/shard_map/while/body/eval_jaxpr/reduce_sum | solution.py:25
  332.5 5.4 %multiply_reduce_fusion.4 = (f32[2048]{0:T(1024)S(1)}, f32[1024,2048]{1,0:T(8,128)}) fusion(bf16[2048,1,128]{2,0,1:T(8,128)(2,1)S(1)} %get-tuple-element.942, bf16[16384,1,128]{2,0,1:T(8,128)(2,1)} %get-tuple-element.941, s32[]{:T(128)S(6)} %select_n.40), kind=kOutput, calls=%fused_computation.2.clone.1 | convolution fusion | flops 541063168 | bytes 9183236 | tf_op jit(solution)/shard_map/while/body/eval_jaxpr/qhd,khd->qhk/dot_general | solution.py:19
  337.9 4.9 %fusion.122 = f32[2048]{0:T(1024)S(1)} fusion(f32[1024,2048]{1,0:T(8,128)} %get-tuple-element.846, f32[2048]{0:T(1024)S(1)} %bitcast.305), kind=kLoop, calls=%fused_computation.4.clone.1 | loop fusion | flops 6289408 | bytes 8404992 | tf_op jit(solution)/shard_map/while/body/eval_jaxpr/reduce_sum | solution.py:25
  346.5 5.4 %multiply_reduce_fusion.4 = (f32[2048]{0:T(1024)S(1)}, f32[1024,2048]{1,0:T(8,128)}) fusion(bf16[2048,1,128]{2,0,1:T(8,128)(2,1)S(1)} %get-tuple-element.942, bf16[16384,1,128]{2,0,1:T(8,128)(2,1)} %get-tuple-element.941, s32[]{:T(128)S(6)} %select_n.40), kind=kOutput, calls=%fused_computation.2.clone.1 | convolution fusion | flops 541063168 | bytes 9183236 | tf_op jit(solution)/shard_map/while/body/eval_jaxpr/qhd,khd->qhk/dot_general | solution.py:19
  351.9 4.9 %fusion.122 = f32[2048]{0:T(1024)S(1)} fusion(f32[1024,2048]{1,0:T(8,128)} %get-tuple-element.846, f32[2048]{0:T(1024)S(1)} %bitcast.305), kind=kLoop, calls=%fused_computation.4.clone.1 | loop fusion | flops 6289408 | bytes 8404992 | tf_op jit(solution)/shard_map/while/body/eval_jaxpr/reduce_sum | solution.py:25
  360.5 5.4 %multiply_reduce_fusion.4 = (f32[2048]{0:T(1024)S(1)}, f32[1024,2048]{1,0:T(8,128)}) fusion(bf16[2048,1,128]{2,0,1:T(8,128)(2,1)S(1)} %get-tuple-element.942, bf16[16384,1,128]{2,0,1:T(8,128)(2,1)} %get-tuple-element.941, s32[]{:T(128)S(6)} %select_n.40), kind=kOutput, calls=%fused_computation.2.clone.1 | convolution fusion | flops 541063168 | bytes 9183236 | tf_op jit(solution)/shard_map/while/body/eval_jaxpr/qhd,khd->qhk/dot_general | solution.py:19
  365.9 4.9 %fusion.122 = f32[2048]{0:T(1024)S(1)} fusion(f32[1024,2048]{1,0:T(8,128)} %get-tuple-element.846, f32[2048]{0:T(1024)S(1)} %bitcast.305), kind=kLoop, calls=%fused_computation.4.clone.1 | loop fusion | flops 6289408 | bytes 8404992 | tf_op jit(solution)/shard_map/while/body/eval_jaxpr/reduce_sum | solution.py:25
  374.5 5.4 %multiply_reduce_fusion.4 = (f32[2048]{0:T(1024)S(1)}, f32[1024,2048]{1,0:T(8,128)}) fusion(bf16[2048,1,128]{2,0,1:T(8,128)(2,1)S(1)} %get-tuple-element.942, bf16[16384,1,128]{2,0,1:T(8,128)(2,1)} %get-tuple-element.941, s32[]{:T(128)S(6)} %select_n.40), kind=kOutput, calls=%fused_computation.2.clone.1 | convolution fusion | flops 541063168 | bytes 9183236 | tf_op jit(solution)/shard_map/while/body/eval_jaxpr/qhd,khd->qhk/dot_general | solution.py:19
  379.9 4.9 %fusion.122 = f32[2048]{0:T(1024)S(1)} fusion(f32[1024,2048]{1,0:T(8,128)} %get-tuple-element.846, f32[2048]{0:T(1024)S(1)} %bitcast.305), kind=kLoop, calls=%fused_computation.4.clone.1 | loop fusion | flops 6289408 | bytes 8404992 | tf_op jit(solution)/shard_map/while/body/eval_jaxpr/reduce_sum | solution.py:25
  388.5 5.4 %multiply_reduce_fusion.4 = (f32[2048]{0:T(1024)S(1)}, f32[1024,2048]{1,0:T(8,128)}) fusion(bf16[2048,1,128]{2,0,1:T(8,128)(2,1)S(1)} %get-tuple-element.942, bf16[16384,1,128]{2,0,1:T(8,128)(2,1)} %get-tuple-element.941, s32[]{:T(128)S(6)} %select_n.40), kind=kOutput, calls=%fused_computation.2.clone.1 | convolution fusion | flops 541063168 | bytes 9183236 | tf_op jit(solution)/shard_map/while/body/eval_jaxpr/qhd,khd->qhk/dot_general | solution.py:19
  393.9 4.9 %fusion.122 = f32[2048]{0:T(1024)S(1)} fusion(f32[1024,2048]{1,0:T(8,128)} %get-tuple-element.846, f32[2048]{0:T(1024)S(1)} %bitcast.305), kind=kLoop, calls=%fused_computation.4.clone.1 | loop fusion | flops 6289408 | bytes 8404992 | tf_op jit(solution)/shard_map/while/body/eval_jaxpr/reduce_sum | solution.py:25
  406.4 4.3 all-to-all-start.4
  410.7 46.2 %while.75 = (s32[]{:T(128)}, f32[256,1]{0,1:T(1,128)S(1)}, f32[256,1]{0,1:T(1,128)S(1)}, f32[256,1,128]{0,2,1:T(8,128)S(1)}, bf16[16384,1,128]{2,0,1:T(8,128)(2,...) while((s32[]{:T(128)}, f32[256,1]{0,1:T(1,128)S(1)}, ...), condition=%wide.region_15.0_spmd.clone, body=%wide.region_12.0_spmd.clone.sunk | while | flops 135890176 | bytes 4014255 | solution.py:45
  459.4 7.3 %convolution_convert_fusion = bf16[128,3072]{1,0:T(8,128)(2,1)} fusion(bf16[128,2048]{0,1:T(8,128)(2,1)S(1)} %bitcast.307, bf16[2048,3072]{1,0:T(8,128)(2,1)} %all-gather.8.cloned.1.call-done), kind=kOutput, calls=%fused_computation.100 | convolution fusion | flops 1611005952 | bytes 13893632 | tf_op jit(solution)/shard_map/dot_general | solution.py:87
  (295 shorter events, 137.3 us)
Async XLA Ops:
  7.2 1.0 copy-start
  7.2 39.2 %copy-start.9 = (bf16[128,2048]{1,0:T(8,128)(2,1)S(1)}, bf16[128,2048]{1,0:T(8,128)(2,1)}, u32[]{:S(2)}) copy-start(bf16[128,2048]{1,0:T(8,128)(2,1)} %param.20) | copy-start | bytes 1572868
  7.2 40.2 %copy-start.15 = (bf16[256,128]{1,0:T(8,128)(2,1)S(1)}, bf16[256,128]{1,0:T(8,128)(2,1)}, u32[]{:S(2)}) copy-start(bf16[256,128]{1,0:T(8,128)(2,1)} %param.22) | copy-start | bytes 196612
  7.2 78.0 %copy-start.16 = (bf16[256,128]{1,0:T(8,128)(2,1)S(1)}, bf16[256,128]{1,0:T(8,128)(2,1)}, u32[]{:S(2)}) copy-start(bf16[256,128]{1,0:T(8,128)(2,1)} %param.23) | copy-start | bytes 196612
  7.2 119.7 %copy-start.7 = (bf16[256,128]{1,0:T(8,128)(2,1)S(1)}, bf16[256,128]{1,0:T(8,128)(2,1)}, u32[]{:S(2)}) copy-start(bf16[256,128]{1,0:T(8,128)(2,1)} %param.21) | copy-start | bytes 196612
  7.2 162.4 %all-gather.4.cloned.1.call-start = ((), (), s32[]{:S(2)}) async-start(), calls=%async_computation.5 | async-start | bytes 4718592 | tf_op jit(solution)/shard_map/all_gather | solution.py:72
  24.6 151.9 %all-gather.6.cloned.1.call-start = ((), (), s32[]{:S(2)}) async-start(), calls=%async_computation.6 | async-start | bytes 4718592 | tf_op jit(solution)/shard_map/all_gather | solution.py:73
  42.0 79.1 %all-to-all-start.1 = ((bf16[128,16,128]{0,2,1:T(8,128)(2,1)}), bf16[128,16,128]{0,2,1:T(8,128)(2,1)S(1)}, u32[]{:S(2)}, u32[]{:S(2)}) async-start(bf16[128,16,128]{0,2,1:T(8,128)(2,1)} %bitcast.3), calls=%async_computation.1 | async-start | bytes 1048576 | tf_op jit(solution)/shard_map/all_to_all | solution.py:58
  45.6 413.8 %all-gather.8.cloned.1.call-start = ((), (), s32[]{:S(2)}) async-start(), calls=%async_computation.7 | async-start | bytes 13369344 | tf_op jit(solution)/shard_map/all_gather | solution.py:89
  121.1 5.8 %copy-start.6 = (bf16[128,16,128]{0,2,1:T(8,128)(2,1)}, bf16[128,16,128]{0,2,1:T(8,128)(2,1)S(1)}, u32[]{:S(2)}) copy-start(bf16[128,16,128]{0,2,1:T(8,128)(2,1)S(1)} %all-to-all-done.1) | copy-start | bytes 1572868
  121.1 16.7 %all-to-all-start.3 = ((bf16[128,16,128]{0,2,1:T(8,128)(2,1)}), bf16[128,16,128]{0,2,1:T(8,128)(2,1)}, u32[]{:S(2)}, u32[]{:S(2)}) async-start(bf16[128,16,128]{0,2,1:T(8,128)(2,1)} %bitcast.11), calls=%async_computation.3 | async-start | bytes 1048576 | tf_op jit(solution)/shard_map/all_to_all | solution.py:61
  128.9 0.8 copy-start.4
  128.9 0.8 copy-start.19
  128.9 0.9 copy-start.3
  139.8 36.6 %copy-start.10 = (f32[2048,1]{0,1:T(1,128)S(1)}, f32[2048,1]{0,1:T(1,128)}, u32[]{:S(2)}) copy-start(f32[2048,1]{0,1:T(1,128)} %custom-call.1) | copy-start | bytes 24580
  139.8 10.6 %copy-start.11 = (f32[2048,1]{0,1:T(1,128)S(1)}, f32[2048,1]{0,1:T(1,128)}, u32[]{:S(2)}) copy-start(f32[2048,1]{0,1:T(1,128)} %get-tuple-element.895) | copy-start | bytes 24580 | tf_op jit(solution)/shard_map/while
  145.4 5.8 %copy-start.1 = (f32[1024,2048]{1,0:T(8,128)S(1)}, f32[1024,2048]{1,0:T(8,128)}, u32[]{:S(2)}) copy-start(f32[1024,2048]{1,0:T(8,128)} %get-tuple-element.857) | copy-start | bytes 25165828 | tf_op jit(solution)/shard_map/while
  150.4 3.6 copy-start.12
  154.0 10.5 %copy-start.11 = (f32[2048,1]{0,1:T(1,128)S(1)}, f32[2048,1]{0,1:T(1,128)}, u32[]{:S(2)}) copy-start(f32[2048,1]{0,1:T(1,128)} %get-tuple-element.895) | copy-start | bytes 24580 | tf_op jit(solution)/shard_map/while
  159.6 5.8 %copy-start.1 = (f32[1024,2048]{1,0:T(8,128)S(1)}, f32[1024,2048]{1,0:T(8,128)}, u32[]{:S(2)}) copy-start(f32[1024,2048]{1,0:T(8,128)} %get-tuple-element.857) | copy-start | bytes 25165828 | tf_op jit(solution)/shard_map/while
  164.6 3.6 copy-start.12
  176.4 227.5 %copy-start.5 = (f32[2048,1,128]{2,0,1:T(8,128)S(1)}, f32[2048,1,128]{2,0,1:T(8,128)}, u32[]{:S(2)}) copy-start(f32[2048,1,128]{2,0,1:T(8,128)} %copy.28) | copy-start | bytes 3145732
  176.4 227.5 %copy-start.13 = (f32[2048,1]{0,1:T(1,128)S(1)}, f32[2048,1]{0,1:T(1,128)}, u32[]{:S(2)}) copy-start(f32[2048,1]{0,1:T(1,128)} %get-tuple-element.505) | copy-start | bytes 24580
  176.5 234.2 %copy-start.8 = (bf16[256,128]{1,0:T(8,128)(2,1)S(1)}, bf16[256,128]{1,0:T(8,128)(2,1)}, u32[]{:S(2)}) copy-start(bf16[256,128]{1,0:T(8,128)(2,1)} %param.24) | copy-start | bytes 196612
  176.5 234.2 %copy-start.14 = (f32[256,1]{0,1:T(1,128)S(1)}, f32[256,1]{0,1:T(1,128)}, u32[]{:S(2)}) copy-start(f32[256,1]{0,1:T(1,128)} %custom-call.9) | copy-start | bytes 3076
  176.5 234.2 %copy-start.17 = (f32[256,1]{0,1:T(1,128)S(1)}, f32[256,1]{0,1:T(1,128)}, u32[]{:S(2)}) copy-start(f32[256,1]{0,1:T(1,128)} %custom-call.10) | copy-start | bytes 3076
  182.0 6.3 %copy-start.2 = (f32[1024,2048]{1,0:T(8,128)S(1)}, f32[1024,2048]{1,0:T(8,128)}, u32[]{:S(2)}) copy-start(f32[1024,2048]{1,0:T(8,128)} %get-tuple-element.846) | copy-start | bytes 25165828 | tf_op jit(solution)/shard_map/while
  196.5 6.0 %copy-start.2 = (f32[1024,2048]{1,0:T(8,128)S(1)}, f32[1024,2048]{1,0:T(8,128)}, u32[]{:S(2)}) copy-start(f32[1024,2048]{1,0:T(8,128)} %get-tuple-element.846) | copy-start | bytes 25165828 | tf_op jit(solution)/shard_map/while
  210.8 6.1 %copy-start.2 = (f32[1024,2048]{1,0:T(8,128)S(1)}, f32[1024,2048]{1,0:T(8,128)}, u32[]{:S(2)}) copy-start(f32[1024,2048]{1,0:T(8,128)} %get-tuple-element.846) | copy-start | bytes 25165828 | tf_op jit(solution)/shard_map/while
  225.1 6.2 %copy-start.2 = (f32[1024,2048]{1,0:T(8,128)S(1)}, f32[1024,2048]{1,0:T(8,128)}, u32[]{:S(2)}) copy-start(f32[1024,2048]{1,0:T(8,128)} %get-tuple-element.846) | copy-start | bytes 25165828 | tf_op jit(solution)/shard_map/while
  239.5 6.0 %copy-start.2 = (f32[1024,2048]{1,0:T(8,128)S(1)}, f32[1024,2048]{1,0:T(8,128)}, u32[]{:S(2)}) copy-start(f32[1024,2048]{1,0:T(8,128)} %get-tuple-element.846) | copy-start | bytes 25165828 | tf_op jit(solution)/shard_map/while
  253.8 5.8 %copy-start.2 = (f32[1024,2048]{1,0:T(8,128)S(1)}, f32[1024,2048]{1,0:T(8,128)}, u32[]{:S(2)}) copy-start(f32[1024,2048]{1,0:T(8,128)} %get-tuple-element.846) | copy-start | bytes 25165828 | tf_op jit(solution)/shard_map/while
  267.8 5.8 %copy-start.2 = (f32[1024,2048]{1,0:T(8,128)S(1)}, f32[1024,2048]{1,0:T(8,128)}, u32[]{:S(2)}) copy-start(f32[1024,2048]{1,0:T(8,128)} %get-tuple-element.846) | copy-start | bytes 25165828 | tf_op jit(solution)/shard_map/while
  281.8 5.8 %copy-start.2 = (f32[1024,2048]{1,0:T(8,128)S(1)}, f32[1024,2048]{1,0:T(8,128)}, u32[]{:S(2)}) copy-start(f32[1024,2048]{1,0:T(8,128)} %get-tuple-element.846) | copy-start | bytes 25165828 | tf_op jit(solution)/shard_map/while
  295.8 5.8 %copy-start.2 = (f32[1024,2048]{1,0:T(8,128)S(1)}, f32[1024,2048]{1,0:T(8,128)}, u32[]{:S(2)}) copy-start(f32[1024,2048]{1,0:T(8,128)} %get-tuple-element.846) | copy-start | bytes 25165828 | tf_op jit(solution)/shard_map/while
  309.9 5.8 %copy-start.2 = (f32[1024,2048]{1,0:T(8,128)S(1)}, f32[1024,2048]{1,0:T(8,128)}, u32[]{:S(2)}) copy-start(f32[1024,2048]{1,0:T(8,128)} %get-tuple-element.846) | copy-start | bytes 25165828 | tf_op jit(solution)/shard_map/while
  323.9 5.8 %copy-start.2 = (f32[1024,2048]{1,0:T(8,128)S(1)}, f32[1024,2048]{1,0:T(8,128)}, u32[]{:S(2)}) copy-start(f32[1024,2048]{1,0:T(8,128)} %get-tuple-element.846) | copy-start | bytes 25165828 | tf_op jit(solution)/shard_map/while
  337.9 5.8 %copy-start.2 = (f32[1024,2048]{1,0:T(8,128)S(1)}, f32[1024,2048]{1,0:T(8,128)}, u32[]{:S(2)}) copy-start(f32[1024,2048]{1,0:T(8,128)} %get-tuple-element.846) | copy-start | bytes 25165828 | tf_op jit(solution)/shard_map/while
  351.9 5.8 %copy-start.2 = (f32[1024,2048]{1,0:T(8,128)S(1)}, f32[1024,2048]{1,0:T(8,128)}, u32[]{:S(2)}) copy-start(f32[1024,2048]{1,0:T(8,128)} %get-tuple-element.846) | copy-start | bytes 25165828 | tf_op jit(solution)/shard_map/while
  365.9 5.8 %copy-start.2 = (f32[1024,2048]{1,0:T(8,128)S(1)}, f32[1024,2048]{1,0:T(8,128)}, u32[]{:S(2)}) copy-start(f32[1024,2048]{1,0:T(8,128)} %get-tuple-element.846) | copy-start | bytes 25165828 | tf_op jit(solution)/shard_map/while
  379.9 5.8 %copy-start.2 = (f32[1024,2048]{1,0:T(8,128)S(1)}, f32[1024,2048]{1,0:T(8,128)}, u32[]{:S(2)}) copy-start(f32[1024,2048]{1,0:T(8,128)} %get-tuple-element.846) | copy-start | bytes 25165828 | tf_op jit(solution)/shard_map/while
  393.9 5.8 %copy-start.2 = (f32[1024,2048]{1,0:T(8,128)S(1)}, f32[1024,2048]{1,0:T(8,128)}, u32[]{:S(2)}) copy-start(f32[1024,2048]{1,0:T(8,128)} %get-tuple-element.846) | copy-start | bytes 25165828 | tf_op jit(solution)/shard_map/while
  406.4 52.7 %all-to-all-start.4 = ((bf16[16,128,128]{2,1,0:T(8,128)(2,1)}), bf16[16,128,128]{2,1,0:T(8,128)(2,1)S(1)}, u32[]{:S(2)}, u32[]{:S(2)}) async-start(bf16[16,128,128]{2,1,0:T(8,128)(2,1)} %bitcast.16), calls=%async_computation.4 | async-start | bytes 1048576 | tf_op jit(solution)/shard_map/all_to_all | solution.py:86
  410.7 46.9 %copy-start.20 = (f32[256,1]{0,1:T(1,128)S(1)}, f32[256,1]{0,1:T(1,128)}, u32[]{:S(2)}) copy-start(f32[256,1]{0,1:T(1,128)} %copy-done.19) | copy-start | bytes 3076
  456.9 0.6 copy-start.18
Sparse Core Ops, SparseCore 0:
  24.7 79.9 all-gather.3
  107.0 69.3 all-gather.5
  178.2 71.2 all-gather.7
where the time goes:
time: 480 us; the launch traced here: 473 us
  matrix products  198 us (41%)
  blocking collectives  104 us (22%)
  other arithmetic  98.9 us (21%)
  local copies, waits for them, and re-layouts  28.4 us (6%)
  waiting for transfers between devices  14.1 us (3%)
  between operations  14.1 us (3%)
  starting transfers between devices  13.7 us (3%)
    dot_general x36, matrix products, attend_block(): jnp.einsum('qhd,khd->qhk', queries, key_block, preferred_element_type=jnp...  119 us
    reduce_sum x36, other arithmetic, attend_block(): denominator = denominator * factor + jnp.sum(weights, axis=2)  93.6 us
    dot_general x36, matrix products, attend_block(): jnp.einsum('qhk,khd->qhd', rounded, value_block, preferred_element_type=j...  71.8 us
    all_gather x1, blocking collectives, local(): lax.all_gather(audio_k, 'seq', axis=0, tiled=True)  37.9 us
    all_gather x1, blocking collectives, local(): lax.all_gather(audio_v, 'seq', axis=0, tiled=True)  35.9 us
    all_to_all x1, blocking collectives, local(): lax.all_to_all(video_k, 'head', split_axis=1, concat_axis=0, tiled=True)  16.2 us
    while x80, local copies, waits for them, and re-layouts  15.1 us
    all_to_all x1, blocking collectives, local(): lax.all_to_all(video_v, 'head', split_axis=1, concat_axis=0, tiled=True)  14.1 us
  transfers between devices with their start and end apart: 6, of which 2 were waited for; matrix products, arithmetic and copies ran while one was open for 64% of the time, Pallas kernels for 0%

commit v1 on v0

v1 whole, which is shorter than its diff:
```python
import jax
import jax.numpy as jnp
from jax import lax
from jax.experimental import pallas as pl
from jax.experimental.pallas import tpu as pltpu
from jax.sharding import Mesh, PartitionSpec as P

BF16 = jnp.bfloat16
F32 = jnp.float32
B = 128
HEADS = 16
SCORE_SCALE = B**-0.5 * 1.4426950408889634
LARGEST_SUM = 1e30
Q_BLOCKS = 18
STEP_BLOCKS = 6
STEP = STEP_BLOCKS * B
STEPS = Q_BLOCKS // STEP_BLOCKS
ROWS = B + 16
VMEM = 60 << 20


def params():
    return pltpu.CompilerParams(vmem_limit_bytes=VMEM)


def cost(flops, bytes_accessed):
    return pl.CostEstimate(flops=int(flops), bytes_accessed=int(bytes_accessed), transcendentals=0)


def pack_video_kernel(q_ref, k_ref, v_ref, x_ref, out_ref):
    for head in range(HEADS):
        columns = slice(head * B, head * B + B)
        out_ref[head, 0] = k_ref[:, columns]
        out_ref[head, 1] = v_ref[:, columns].T
        out_ref[head, 2] = q_ref[:, columns].T
        out_ref[head, 3] = x_ref[:, columns].T


def pack_video(q, k, v, x):
    return pl.pallas_call(
        pack_video_kernel,
        out_shape=jax.ShapeDtypeStruct((HEADS, 4, B, B), BF16),
        compiler_params=params(),
    )(q, k, v, x)


def pack_audio_kernel(q_ref, k_ref, v_ref, x_ref, out_ref):
    for block in range(2):
        rows = slice(block * B, block * B + B)
        out_ref[block, 0] = k_ref[rows, :]
        out_ref[block, 1] = v_ref[rows, :].T
        out_ref[block, 2] = x_ref[rows, :].T
        out_ref[block, 3] = q_ref[rows, :].T


def pack_audio(q, k, v, x):
    return pl.pallas_call(
        pack_audio_kernel,
        out_shape=jax.ShapeDtypeStruct((2, 4, B, B), BF16),
        compiler_params=params(),
    )(q, k, v, x)


def unpack_kernel(video_ref, audio_ref, a_ref, b_ref, q_ref):
    for piece, out_ref in enumerate((a_ref, b_ref)):
        out_ref[0:8] = video_ref[piece * 8 : piece * 8 + 8, 0:2]
        out_ref[8] = audio_ref[piece, 0:2]
    for kind in range(2):
        q_ref[kind, 0:16] = video_ref[:, 2 + kind]
        q_ref[kind, 16:18] = audio_ref[:, 2 + kind]


def unpack(video, audio):
    piece = jax.ShapeDtypeStruct((9, 2, B, B), BF16)
    return pl.pallas_call(
        unpack_kernel,
        out_shape=(piece, piece, jax.ShapeDtypeStruct((2, Q_BLOCKS, B, B), BF16)),
        compiler_params=params(),
    )(video, audio)


def lanes(blocks):
    return jnp.concatenate([blocks[index] for index in range(blocks.shape[0])], axis=1)


def scores_of(keys, queries):
    return jnp.dot(keys, queries, preferred_element_type=F32) * SCORE_SCALE


def attend_step(first, state, pieces, audio, queries):
    part = slice(8, 9) if audio else slice(0, 8)
    scores = [
        scores_of(ref[part, 0].reshape(-1, B), queries) for ref in pieces
    ]
    if first:
        shift = jnp.max(scores[0][: 2 * B], axis=0, keepdims=True)
        sums, values = jnp.zeros((8, STEP), F32), jnp.zeros((B, STEP), F32)
    else:
        values, sums, shift = state
    for ref, score in zip(pieces, scores):
        weights = jnp.exp2(score - shift)
        sums = sums + jnp.sum(weights.reshape(-1, 8, STEP), axis=0)
        values = values + jnp.dot(
            lanes(ref[part, 1]), weights.astype(BF16), preferred_element_type=F32
        )
    return values, sums, shift


def attend_step_careful(state, pieces, audio, queries):
    for ref in pieces:

        def body(block, state, ref=ref):
            values, sums, shift = state
            scores = scores_of(ref[block, 0], queries)
            newest = jnp.maximum(shift, jnp.max(scores, axis=0, keepdims=True))
            factor = jnp.exp2(shift - newest)
            weights = jnp.exp2(scores - newest)
            sums = sums * factor + jnp.sum(weights.reshape(-1, 8, STEP), axis=0)
            values = values * factor + jnp.dot(
                ref[block, 1], weights.astype(BF16), preferred_element_type=F32
            )
            return values, sums, newest

        state = lax.fori_loop(8, 9, body, state) if audio else lax.fori_loop(0, 8, body, state)
    return state


def stage_kernel(first, offset, *refs):
    if first:
        own_ref, other_ref, a_ref, b_ref, out_ref = refs
    else:
        own_ref, other_ref, a_ref, b_ref, in_ref, out_ref = refs
    step = pl.program_id(0) + offset
    for kind in range(2):
        own, other = lanes(own_ref[kind]), lanes(other_ref[kind])
        queries = jnp.where(step < STEPS, own, other)
        pieces = (a_ref, b_ref)
        if first:
            state = None
        else:
            state = (in_ref[kind, 0:B], in_ref[kind, B : B + 8], in_ref[kind, B + 8 : B + 9])
        values, sums, shift = attend_step(first, state, pieces, kind == 1, queries)
        safe = jnp.max(sums) < LARGEST_SUM

        @pl.when(safe)
        def _():
            out_ref[kind, 0:B] = values
            out_ref[kind, B : B + 8] = sums
            out_ref[kind, B + 8 : B + 16] = jnp.broadcast_to(shift, (8, STEP))

        @pl.when(jnp.logical_not(safe))
        def _():
            if first:
                again = (jnp.zeros((B, STEP), F32), jnp.zeros((8, STEP), F32), shift)
            else:
                again = (in_ref[kind, 0:B], in_ref[kind, B : B + 8], in_ref[kind, B + 8 : B + 9])
            new_values, new_sums, new_shift = attend_step_careful(
                again, pieces, kind == 1, queries
            )
            out_ref[kind, 0:B] = new_values
            out_ref[kind, B : B + 8] = new_sums
            out_ref[kind, B + 8 : B + 16] = jnp.broadcast_to(new_shift, (8, STEP))


def stage(own, other, a, b, state, offset, steps):
    first = state is None
    query_block = (2, STEP_BLOCKS, B, B)
    piece_spec = pl.BlockSpec((9, 2, B, B), lambda i: (0, 0, 0, 0))
    in_specs = [
        pl.BlockSpec(query_block, lambda i: (0, jnp.minimum(i + offset, STEPS - 1), 0, 0)),
        pl.BlockSpec(query_block, lambda i: (0, jnp.maximum(i + offset - STEPS, 0), 0, 0)),
        piece_spec,
        piece_spec,
    ]
    operands = [own, other, a, b]
    if not first:
        in_specs.append(pl.BlockSpec((2, ROWS, STEP), lambda i: (0, 0, i + offset)))
        operands.append(state)

    def kernel(*refs):
        stage_kernel(first, offset, *refs)

    return pl.pallas_call(
        kernel,
        grid=(steps,),
        in_specs=in_specs,
        out_specs=pl.BlockSpec((2, ROWS, STEP), lambda i: (0, 0, i)),
        out_shape=jax.ShapeDtypeStruct((2, ROWS, steps * STEP), F32),
        compiler_params=params(),
        cost_estimate=cost(steps * STEP * 18 * B * 4 * B * 3, 4 << 20),
    )(*operands)


def merge_kernel(own_ref, other_ref, video_ref, audio_ref):
    total = None
    for kind in range(2):
        shift_own, shift_other = own_ref[kind, B + 8 : B + 9], other_ref[kind, B + 8 : B + 9]
        largest = jnp.maximum(shift_own, shift_other)
        factor_own, factor_other = jnp.exp2(shift_own - largest), jnp.exp2(shift_other - largest)
        sums = (
            jnp.sum(own_ref[kind, B : B + 8], axis=0, keepdims=True) * factor_own
            + jnp.sum(other_ref[kind, B : B + 8], axis=0, keepdims=True) * factor_other
        )
        values = own_ref[kind, 0:B] * (factor_own / sums) + other_ref[kind, 0:B] * (
            factor_other / sums
        )
        total = values if total is None else total + values
    for block in range(STEP_BLOCKS):
        piece = total[:, block * B : block * B + B].T.astype(BF16)
        video_ref[block] = piece
        audio_ref[block] = piece


def merge(own, other):
    spec = pl.BlockSpec((2, ROWS, STEP), lambda i: (0, 0, i))
    return pl.pallas_call(
        merge_kernel,
        grid=(STEPS,),
        in_specs=[spec, spec],
        out_specs=(
            pl.BlockSpec((STEP_BLOCKS, B, B), lambda i: (i, 0, 0)),
            pl.BlockSpec((STEP_BLOCKS, B, B), lambda i: (0, 0, 0)),
        ),
        out_shape=(
            jax.ShapeDtypeStruct((Q_BLOCKS, B, B), BF16),
            jax.ShapeDtypeStruct((STEP_BLOCKS, B, B), BF16),
        ),
        compiler_params=params(),
        cost_estimate=cost(0, 6 << 20),
    )(own, other)


def project_kernel(rows_ref, weight_ref, out_ref):
    out_ref[...] = jnp.dot(
        lanes(rows_ref[...]), weight_ref[...], preferred_element_type=F32
    ).astype(BF16)


def project(rows, weight):
    width = weight.shape[1]
    tile = 512
    return pl.pallas_call(
        project_kernel,
        grid=(width // tile,),
        in_specs=[
            pl.BlockSpec((HEADS, B, B), lambda i: (0, 0, 0)),
            pl.BlockSpec((HEADS * B, tile), lambda i: (0, i)),
        ],
        out_specs=pl.BlockSpec((B, tile), lambda i: (0, i)),
        out_shape=jax.ShapeDtypeStruct((B, width), BF16),
        compiler_params=params(),
        cost_estimate=cost(2 * B * HEADS * B * width, HEADS * B * width * 2),
    )(rows, weight)


def local(
    video_q, video_k, video_v, video_cross_q, audio_q, audio_k, audio_v, audio_cross_q, out_weight
):
    plane = ("yl", "x", "yh")
    trade = [
        (z * 4 + yh * 2 + core, z * 4 + core * 2 + yh)
        for z in range(4)
        for yh in range(2)
        for core in range(2)
    ]
    up = [(z, (z + 1) % 4) for z in range(4)]
    down = [(z, (z + 3) % 4) for z in range(4)]
    swap = [(0, 1), (1, 0)]

    weight = lax.all_gather(out_weight, ("yl", "x", "c"), axis=0, tiled=True)
    audio = lax.ppermute(
        pack_audio(audio_q, audio_k, audio_v, audio_cross_q), ("z", "yh", "c"), trade
    )
    video = lax.all_to_all(
        pack_video(video_q, video_k, video_v, video_cross_q),
        plane,
        split_axis=0,
        concat_axis=0,
        tiled=True,
    )
    own_a, own_b, own_q = unpack(video, audio)
    other_q = lax.ppermute(own_q, "c", swap)
    up_a, down_a = lax.ppermute(own_a, "z", up), lax.ppermute(own_a, "z", down)
    up_b, down_b = lax.ppermute(own_b, "z", up), lax.ppermute(own_b, "z", down)
    far_a, far_b = lax.ppermute(up_a, "z", up), lax.ppermute(down_b, "z", down)

    state = stage(own_q, other_q, own_a, own_b, None, 0, 2 * STEPS)
    state = stage(own_q, other_q, up_a, down_a, state, 0, 2 * STEPS)
    state = stage(own_q, other_q, up_b, down_b, state, 0, 2 * STEPS)
    given = lax.ppermute(
        stage(own_q, other_q, far_a, far_b, state, STEPS, STEPS), "c", swap
    )
    kept = stage(own_q, other_q, far_a, far_b, state, 0, STEPS)
    video_attn, audio_tail = merge(kept, given)
    rows = lax.all_to_all(video_attn[:HEADS], plane, split_axis=0, concat_axis=0, tiled=True)
    video_mixed = project(rows, weight)
    audio_attn = lax.ppermute(
        audio_tail[STEP_BLOCKS - 2 :].reshape(2 * B, B), ("z", "yh", "c"), trade
    )
    return video_mixed, audio_attn


def solution(mesh):
    fine = Mesh(mesh.devices.reshape(4, 2, 2, 4, 2), ("z", "yh", "yl", "x", "c"))
    seq, head = ("z", "yh"), ("yl", "x", "c")
    tokens = P(seq + head, None)
    tower = P(seq, head)
    return jax.shard_map(
        local,
        mesh=fine,
        in_specs=(tokens,) * 4 + (tower,) * 4 + (P(head, None),),
        out_specs=(tokens, tower),
        check_vma=False,
    )
```

time: 480 us -> 217 us (0.45)
  matrix products: 198 us -> 0 us
  blocking collectives: 104 us -> 0 us
  Pallas kernels: 0 us -> 101 us
  other arithmetic: 98.9 us -> 0 us
  waiting for transfers between devices: 14.1 us -> 70.2 us
  local copies, waits for them, and re-layouts: 28.4 us -> 9.79 us
  starting transfers between devices: 13.7 us -> 19.1 us
    dot_general x73 -> x0, matrix products: 198 us -> none  [the longest x36 119 us: attend_block(): jnp.einsum('qhd,khd->qhk', queries, key_block, preferred_element_type=jnp...]
    pallas_call x0 -> x10, Pallas kernels: none -> 101 us  [the longest x5 80.5 us: stage(): pl.pallas_call(kernel, grid=(steps,), in_specs=in_specs, out_specs=pl.Blo...]
    reduce_sum x36 -> x0, other arithmetic: 93.6 us -> none  [attend_block(): denominator = denominator * factor + jnp.sum(weights, axis=2)]
    all_gather x2 -> x0, blocking collectives: 73.8 us -> none  [the longest x1 37.9 us: local(): lax.all_gather(audio_k, 'seq', axis=0, tiled=True)]
    all_to_all x3 -> x2, waiting for transfers between devices: 6.63 us -> 57.2 us  [the longest x1 45.8 us: local(): lax.all_to_all(pack_video(video_q, video_k, video_v, video_cross_q), plan...]
    all_to_all x2 -> x0, blocking collectives: 30.3 us -> none  [the longest x1 16.2 us: local(): lax.all_to_all(video_k, 'head', split_axis=1, concat_axis=0, tiled=True)]
    while x84 -> x0, local copies, waits for them, and re-layouts: 18 us -> none
    ppermute x0 -> x10, waiting for transfers between devices: none -> 12.3 us  [the longest x1 12.2 us: local(): lax.ppermute(own_a, 'z', up)]
  transfers between devices with their start and end apart: 6 -> 13, of which waited for: 2 -> 3; matrix products, arithmetic and copies ran while one was open for 64% -> 1% of each run, Pallas kernels for 0% -> 43%
where the time goes in v1:
time: 217 us; the launch traced here: 214 us
  Pallas kernels  101 us (47%)
  waiting for transfers between devices  70.2 us (32%)
  starting transfers between devices  19.1 us (9%)
  between operations  14.1 us (6%)
  local copies, waits for them, and re-layouts  9.79 us (5%)
    pallas_call x5, Pallas kernels, stage(): pl.pallas_call(kernel, grid=(steps,), in_specs=in_specs, out_specs=pl.Blo...  80.5 us
    all_to_all x1, waiting for transfers between devices, local(): lax.all_to_all(pack_video(video_q, video_k, video_v, video_cross_q), plan...  45.8 us
    ppermute x1, waiting for transfers between devices, local(): lax.ppermute(own_a, 'z', up)  12.2 us
    all_to_all x1, waiting for transfers between devices, local(): lax.all_to_all(video_attn[:HEADS], plane, split_axis=0, concat_axis=0, ti...  11.5 us
    pallas_call x1, Pallas kernels, project(): pl.pallas_call(project_kernel, grid=(width // tile,), in_specs=[pl.BlockS...  7.97 us
    all_to_all x1, starting transfers between devices, local(): lax.all_to_all(pack_video(video_q, video_k, video_v, video_cross_q), plan...  7.03 us
    unnamed x19, local copies, waits for them, and re-layouts  7.01 us
  transfers between devices with their start and end apart: 13, of which 3 were waited for; matrix products, arithmetic and copies ran while one was open for 1% of the time, Pallas kernels for 43%

profile of v1, /device:TPU:64, one launch (start us, length us, event | category | flops | bytes accessed | tf_op | source)
XLA Modules:
  0.0 214.0 jit_solution(9515822419914849457)
XLA Ops:
  7.2 0.0 all-gather.2.cloned.1.call-start
  7.2 0.7 all-gather.2.cloned.1.call-update
  7.9 3.3 %shard_map.104 = bf16[16,4,128,128]{3,2,1,0:T(8,128)(2,1)} custom-call(bf16[128,2048]{1,0:T(8,128)(2,1)} %q_ref.2, bf16[128,2048]{1,0:T(8,128)(2,1)} %k_ref.2, bf16[128,2048]{1,0:T(8,128)(2,1)} %v_ref.2, bf16[128,2048]{1,0:T(8,128)(2,1)} %x_ref.2), custom_call_target="tpu_custom_call" | custom-call | tf_op jit(solution)/shard_map/pallas_call | solution.py:40
  11.2 7.0 %all-to-all-start = ((bf16[16,4,128,128]{3,2,1,0:T(8,128)(2,1)}), bf16[16,4,128,128]{3,2,1,0:T(8,128)(2,1)S(1)}, u32[]{:S(2)}, u32[]{:S(2)}) async-start(bf16[16,4,128,128]{3,2,1,0:T(8,128)(2,1)} %shard_map.104), calls=%async_computation | async-start | bytes 4194304 | tf_op jit(solution)/shard_map/all_to_all | solution.py:274
  18.3 1.7 shard_map.105
  20.0 1.6 collective-permute-start
  21.6 0.0 collective-permute-done.audio_ref
  21.6 45.8 %all-to-all-done.video_ref = bf16[16,4,128,128]{3,2,1,0:T(8,128)(2,1)S(1)} async-done(((bf16[16,4,128,128]{3,2,1,0:T(8,128)(2,1)}), bf16[16,4,128,128]{3,2,1,0:T(8,128)(2,1)S(1)}, u32[]{:S(2)}, u32[]{:S(2)}) %all-to-all-start) | async-done | bytes 2097184 | tf_op jit(solution)/shard_map/all_to_all | solution.py:274
  67.4 0.0 copy-done.3
  67.4 1.3 copy-done
  68.7 3.0 %shard_map.106 = (bf16[9,2,128,128]{3,2,1,0:T(8,128)(2,1)}, bf16[9,2,128,128]{3,2,1,0:T(8,128)(2,1)}, bf16[2,18,128,128]{3,2,1,0:T(8,128)(2,1)}) custom-call(bf16[16,4,128,128]{3,2,1,0:T(8,128)(2,1)} %copy-done, bf16[2,4,128,128]{3,2,1,0:T(8,128)(2,1)} %copy-done.3), custom_call_target="tpu_custom_call" | custom-call | tf_op jit(solution)/shard_map/pallas_call | solution.py:75
  71.8 0.0 collective-permute-start.1
  71.8 2.1 collective-permute-start.2
  73.8 0.0 collective-permute-start.4
  73.8 0.0 collective-permute-start.7
  73.8 2.1 collective-permute-start.6
  75.9 12.2 %collective-permute-done.2.refs_2_ = bf16[9,2,128,128]{3,2,1,0:T(8,128)(2,1)S(1)} collective-permute-done((bf16[9,2,128,128]{3,2,1,0:T(8,128)(2,1)}, bf16[9,2,128,128]{3,2,1,0:T(8,128)(2,1)S(1)}, u32[]{:S(2)}, u32[]{:S(2)}) %collective-permute-start.2) | collective-permute-done | bytes 589856 | tf_op jit(solution)/shard_map/ppermute | solution.py:283
  88.1 2.1 collective-permute-start.3
  90.2 0.0 collective-permute-done.4.refs_3_
  90.2 0.0 collective-permute-start.5
  90.2 0.0 collective-permute-done.1.refs_1_
  90.2 0.0 copy-start.4
  90.2 1.1 copy-done.4
  91.3 16.7 %shard_map.107.refs_4_ = f32[2,144,4608]{2,1,0:T(8,128)} custom-call(bf16[2,18,128,128]{3,2,1,0:T(8,128)(2,1)} %get-tuple-element.7.refs_0_, bf16[2,18,128,128]{3,2,1,0:T(8,128)(2,1)} %copy-done.4, bf16[9,2,128,128]{3,2,1,0:T(8,128)(2,1)} %get-tuple-element.8.refs_2_, bf16[9,2,128,128]{3,2,1,0:T(8,128)(2,1)} %get-tuple-element.9.refs_3_), custom_call_target="tpu_custom_call" | custom-call | flops 16307453952 | bytes 4194304 | tf_op jit(solution)/shard_map/pallas_call | solution.py:183
  108.0 0.0 copy-done.5
  108.0 0.0 collective-permute-done.7.refs_3_
  108.0 31.6 %shard_map.108.refs_4_ = f32[2,144,4608]{2,1,0:T(8,128)} custom-call(bf16[2,18,128,128]{3,2,1,0:T(8,128)(2,1)} %get-tuple-element.7.refs_0_, bf16[2,18,128,128]{3,2,1,0:T(8,128)(2,1)} %copy-done.4, bf16[9,2,128,128]{3,2,1,0:T(8,128)(2,1)} %copy-done.5, bf16[9,2,128,128]{3,2,1,0:T(8,128)(2,1)} %collective-permute-done.7.refs_3_, ...), custom_call_target="tpu_custom_call" | custom-call | flops 16307453952 | bytes 4194304 | tf_op jit(solution)/shard_map/pallas_call | solution.py:183
  139.7 0.0 collective-permute-done.6.refs_2_
  139.7 14.8 %shard_map.109.refs_4_ = f32[2,144,4608]{2,1,0:T(8,128)} custom-call(bf16[2,18,128,128]{3,2,1,0:T(8,128)(2,1)} %get-tuple-element.7.refs_0_, bf16[2,18,128,128]{3,2,1,0:T(8,128)(2,1)} %copy-done.4, bf16[9,2,128,128]{3,2,1,0:T(8,128)(2,1)} %collective-permute-done.6.refs_2_, bf16[9,2,128,128]{3,2,1,0:T(8,128)(2,1)} %copy-done.6, ...), custom_call_target="tpu_custom_call" | custom-call | flops 16307453952 | bytes 4194304 | tf_op jit(solution)/shard_map/pallas_call | solution.py:183
  154.4 0.0 collective-permute-done.3.refs_2_
  154.4 0.0 collective-permute-done.5.refs_3_
  154.4 0.8 copy-done.7
  155.2 0.8 copy-done.8
  156.1 8.7 %shard_map.111 = f32[2,144,2304]{2,1,0:T(8,128)} custom-call(bf16[2,18,128,128]{3,2,1,0:T(8,128)(2,1)} %get-tuple-element.7.refs_0_, bf16[2,18,128,128]{3,2,1,0:T(8,128)(2,1)} %copy-done.4, bf16[9,2,128,128]{3,2,1,0:T(8,128)(2,1)} %copy-done.7, bf16[9,2,128,128]{3,2,1,0:T(8,128)(2,1)} %copy-done.8, f32[2,144,4608]{2,1,0:T(8,128)} %shard_map.109.refs_4_), custom_call_target="tpu_custom_call" | custom-call | flops 8153726976 | bytes 4194304 | tf_op jit(solution)/shard_map/pallas_call | solution.py:183
  164.8 0.0 collective-permute-start.8
  164.8 8.7 %shard_map.110.own_ref = f32[2,144,2304]{2,1,0:T(8,128)} custom-call(bf16[2,18,128,128]{3,2,1,0:T(8,128)(2,1)} %get-tuple-element.7.refs_0_, bf16[2,18,128,128]{3,2,1,0:T(8,128)(2,1)} %copy-done.4, bf16[9,2,128,128]{3,2,1,0:T(8,128)(2,1)} %copy-done.7, bf16[9,2,128,128]{3,2,1,0:T(8,128)(2,1)} %copy-done.8, f32[2,144,4608]{2,1,0:T(8,128)} %shard_map.109.refs_4_), custom_call_target="tpu_custom_call" | custom-call | flops 8153726976 | bytes 4194304 | tf_op jit(solution)/shard_map/pallas_call | solution.py:183
  173.5 0.0 collective-permute-done.8.other_ref
  173.5 1.5 copy-done.1
  175.0 4.3 %shard_map.112 = (bf16[18,128,128]{2,1,0:T(8,128)(2,1)}, bf16[6,128,128]{2,1,0:T(8,128)(2,1)}) custom-call(f32[2,144,2304]{2,1,0:T(8,128)} %shard_map.110.own_ref, f32[2,144,2304]{2,1,0:T(8,128)} %copy-done.1), custom_call_target="tpu_custom_call" | custom-call | bytes 6291456 | tf_op jit(solution)/shard_map/pallas_call | solution.py:216
  179.2 1.9 slice.6
  181.1 3.6 %all-to-all-start.1 = ((bf16[16,128,128]{2,1,0:T(8,128)(2,1)}), bf16[16,128,128]{2,1,0:T(8,128)(2,1)S(1)}, u32[]{:S(2)}, u32[]{:S(2)}) async-start(bf16[16,128,128]{2,1,0:T(8,128)(2,1)} %slice.6), calls=%async_computation.1 | async-start | bytes 1048576 | tf_op jit(solution)/shard_map/all_to_all | solution.py:295
  184.7 0.8 slice.7
  185.6 0.7 collective-permute-start.9
  186.2 0.0 collective-permute-done.9
  186.2 11.5 %all-to-all-done.1.rows_ref = bf16[16,128,128]{2,1,0:T(8,128)(2,1)S(1)} async-done(((bf16[16,128,128]{2,1,0:T(8,128)(2,1)}), bf16[16,128,128]{2,1,0:T(8,128)(2,1)S(1)}, u32[]{:S(2)}, u32[]{:S(2)}) %all-to-all-start.1) | async-done | bytes 524320 | tf_op jit(solution)/shard_map/all_to_all | solution.py:295
  197.7 0.8 copy-done.2
  198.6 8.0 %shard_map.113 = bf16[128,3072]{1,0:T(8,128)(2,1)} custom-call(bf16[16,128,128]{2,1,0:T(8,128)(2,1)} %copy-done.2, bf16[2048,3072]{1,0:T(8,128)(2,1)} %all-gather.2.cloned.1.call-done.weight_ref), custom_call_target="tpu_custom_call" | custom-call | flops 1610612736 | bytes 12582912 | tf_op jit(solution)/shard_map/pallas_call | solution.py:242
  206.5 0.6 copy.12
  (10 shorter events, 0.0 us)
Async XLA Ops:
  7.2 190.6 %all-gather.2.cloned.1.call-start = ((), (), s32[]{:S(2)}) async-start(), calls=%async_computation.2 | async-start | bytes 13369344 | tf_op jit(solution)/shard_map/all_gather | solution.py:270
  11.2 56.2 %all-to-all-start = ((bf16[16,4,128,128]{3,2,1,0:T(8,128)(2,1)}), bf16[16,4,128,128]{3,2,1,0:T(8,128)(2,1)S(1)}, u32[]{:S(2)}, u32[]{:S(2)}) async-start(bf16[16,4,128,128]{3,2,1,0:T(8,128)(2,1)} %shard_map.104), calls=%async_computation | async-start | bytes 4194304 | tf_op jit(solution)/shard_map/all_to_all | solution.py:274
  20.0 1.6 collective-permute-start
  21.6 45.8 %copy-start.3 = (bf16[2,4,128,128]{3,2,1,0:T(8,128)(2,1)}, bf16[2,4,128,128]{3,2,1,0:T(8,128)(2,1)S(1)}, u32[]{:S(2)}) copy-start(bf16[2,4,128,128]{3,2,1,0:T(8,128)(2,1)S(1)} %collective-permute-done.audio_ref) | copy-start | bytes 786436
  67.4 1.3 copy-start
  71.8 18.5 %collective-permute-start.1 = (bf16[2,18,128,128]{3,2,1,0:T(8,128)(2,1)}, bf16[2,18,128,128]{3,2,1,0:T(8,128)(2,1)S(1)}, u32[]{:S(2)}, u32[]{:S(2)}) collective-permute-start(bf16[2,18,128,128]{3,2,1,0:T(8,128)(2,1)} %get-tuple-element.7.refs_0_), channel_id=1, source_target_pairs={{0,1},{1,0},{2,3},{3,2},{4,5},{5,4},{6,7},{7,6},{8,9},{9,8},{10,11... | collective-permute-start | bytes 3538952 | tf_op jit(solution)/shard_map/ppermute | solution.py:282
  71.8 16.3 %collective-permute-start.2 = (bf16[9,2,128,128]{3,2,1,0:T(8,128)(2,1)}, bf16[9,2,128,128]{3,2,1,0:T(8,128)(2,1)S(1)}, u32[]{:S(2)}, u32[]{:S(2)}) collective-permute-start(bf16[9,2,128,128]{3,2,1,0:T(8,128)(2,1)} %get-tuple-element.8.refs_2_), channel_id=1, source_target_pairs={{0,32},{32,64},{64,96},{96,0},{1,33},{33,65},{65,97},{97,1},{2,34}... | collective-permute-start | bytes 1769480 | tf_op jit(solution)/shard_map/ppermute | solution.py:283
  73.8 16.4 %collective-permute-start.4 = (bf16[9,2,128,128]{3,2,1,0:T(8,128)(2,1)}, bf16[9,2,128,128]{3,2,1,0:T(8,128)(2,1)S(1)}, u32[]{:S(2)}, u32[]{:S(2)}) collective-permute-start(bf16[9,2,128,128]{3,2,1,0:T(8,128)(2,1)} %get-tuple-element.9.refs_3_), channel_id=1, source_target_pairs={{0,96},{32,0},{64,32},{96,64},{1,97},{33,1},{65,33},{97,65},{2,98}... | collective-permute-start | bytes 1769480 | tf_op jit(solution)/shard_map/ppermute | solution.py:284
  73.8 34.2 %collective-permute-start.7 = (bf16[9,2,128,128]{3,2,1,0:T(8,128)(2,1)}, bf16[9,2,128,128]{3,2,1,0:T(8,128)(2,1)}, u32[]{:S(2)}, u32[]{:S(2)}) collective-permute-start(bf16[9,2,128,128]{3,2,1,0:T(8,128)(2,1)} %get-tuple-element.8.refs_2_), channel_id=1, source_target_pairs={{0,96},{32,0},{64,32},{96,64},{1,97},{33,1},{65,33},{97,65},{2,98}... | collective-permute-start | bytes 1769480 | tf_op jit(solution)/shard_map/ppermute | solution.py:283
  73.8 65.8 %collective-permute-start.6 = (bf16[9,2,128,128]{3,2,1,0:T(8,128)(2,1)}, bf16[9,2,128,128]{3,2,1,0:T(8,128)(2,1)}, u32[]{:S(2)}, u32[]{:S(2)}) collective-permute-start(bf16[9,2,128,128]{3,2,1,0:T(8,128)(2,1)} %get-tuple-element.9.refs_3_), channel_id=1, source_target_pairs={{0,32},{32,64},{64,96},{96,0},{1,33},{33,65},{65,97},{97,1},{2,34}... | collective-permute-start | bytes 1769480 | tf_op jit(solution)/shard_map/ppermute | solution.py:284
  88.1 19.9 %copy-start.5 = (bf16[9,2,128,128]{3,2,1,0:T(8,128)(2,1)}, bf16[9,2,128,128]{3,2,1,0:T(8,128)(2,1)S(1)}, u32[]{:S(2)}) copy-start(bf16[9,2,128,128]{3,2,1,0:T(8,128)(2,1)S(1)} %collective-permute-done.2.refs_2_) | copy-start | bytes 1769476
  88.1 66.3 %collective-permute-start.3 = (bf16[9,2,128,128]{3,2,1,0:T(8,128)(2,1)S(1)}, bf16[9,2,128,128]{3,2,1,0:T(8,128)(2,1)S(1)}, u32[]{:S(2)}, u32[]{:S(2)}) collective-permute-start(bf16[9,2,128,128]{3,2,1,0:T(8,128)(2,1)S(1)} %collective-permute-done.2.refs_2_), channel_id=1, source_target_pairs={{0,32},{32,64},{64,96},{96,0},{1,33},{33,65},{65,97},{97,1},{2,34}... | collective-permute-start | bytes 1769480 | tf_op jit(solution)/shard_map/ppermute | solution.py:285
  90.2 17.8 %copy-start.6 = (bf16[9,2,128,128]{3,2,1,0:T(8,128)(2,1)}, bf16[9,2,128,128]{3,2,1,0:T(8,128)(2,1)S(1)}, u32[]{:S(2)}) copy-start(bf16[9,2,128,128]{3,2,1,0:T(8,128)(2,1)S(1)} %collective-permute-done.4.refs_3_) | copy-start | bytes 1769476
  90.2 64.2 %collective-permute-start.5 = (bf16[9,2,128,128]{3,2,1,0:T(8,128)(2,1)S(1)}, bf16[9,2,128,128]{3,2,1,0:T(8,128)(2,1)S(1)}, u32[]{:S(2)}, u32[]{:S(2)}) collective-permute-start(bf16[9,2,128,128]{3,2,1,0:T(8,128)(2,1)S(1)} %collective-permute-done.4.refs_3_), channel_id=1, source_target_pairs={{0,96},{32,0},{64,32},{96,64},{1,97},{33,1},{65,33},{97,65},{2,98}... | collective-permute-start | bytes 1769480 | tf_op jit(solution)/shard_map/ppermute | solution.py:285
  90.2 1.1 copy-start.4
  154.4 0.8 copy-start.7
  155.2 0.8 copy-start.8
  164.8 8.7 %collective-permute-start.8 = (f32[2,144,2304]{2,1,0:T(8,128)}, f32[2,144,2304]{2,1,0:T(8,128)S(1)}, u32[]{:S(2)}, u32[]{:S(2)}) collective-permute-start(f32[2,144,2304]{2,1,0:T(8,128)} %shard_map.111), channel_id=1, source_target_pairs={{0,1},{1,0},{2,3},{3,2},{4,5},{5,4},{6,7},{7,6},{8,9},{9,8},{10,11... | collective-permute-start | bytes 7962632 | tf_op jit(solution)/shard_map/ppermute | solution.py:290
  173.5 1.5 copy-start.1
  181.1 16.6 %all-to-all-start.1 = ((bf16[16,128,128]{2,1,0:T(8,128)(2,1)}), bf16[16,128,128]{2,1,0:T(8,128)(2,1)S(1)}, u32[]{:S(2)}, u32[]{:S(2)}) async-start(bf16[16,128,128]{2,1,0:T(8,128)(2,1)} %slice.6), calls=%async_computation.1 | async-start | bytes 1048576 | tf_op jit(solution)/shard_map/all_to_all | solution.py:295
  185.6 0.7 collective-permute-start.9
  197.7 0.8 copy-start.2
Sparse Core Ops, SparseCore 0:
  9.7 96.8 all-gather.1

commit v2 on v1

v2 whole, which is shorter than its diff:
```python
import jax
import jax.numpy as jnp
from jax import lax
from jax.experimental import pallas as pl
from jax.experimental.pallas import tpu as pltpu
from jax.sharding import Mesh, PartitionSpec as P

BF16 = jnp.bfloat16
F32 = jnp.float32
B = 128
HEADS = 16
SCORE_SCALE = B**-0.5 * 1.4426950408889634
LARGEST_SUM = 1e30
Q_BLOCKS = 18
STEP_BLOCKS = 6
STEP = STEP_BLOCKS * B
STEPS = Q_BLOCKS // STEP_BLOCKS
ROWS = B + 16
VMEM = 24 << 20


def params():
    return pltpu.CompilerParams(vmem_limit_bytes=VMEM)


def cost(flops, bytes_accessed):
    return pl.CostEstimate(flops=int(flops), bytes_accessed=int(bytes_accessed), transcendentals=0)


def after(value, *others):
    return lax.optimization_barrier((value, *others))[0]


def pack_video_kernel(q_ref, k_ref, v_ref, x_ref, out_ref):
    for head in range(HEADS // 4):
        columns = slice(head * B, head * B + B)
        out_ref[head, 0] = k_ref[:, columns]
        out_ref[head, 1] = v_ref[:, columns].T
        out_ref[head, 2] = q_ref[:, columns].T
        out_ref[head, 3] = x_ref[:, columns].T


def pack_video(q, k, v, x):
    spec = pl.BlockSpec((B, 4 * B), lambda i: (0, i))
    return pl.pallas_call(
        pack_video_kernel,
        grid=(4,),
        in_specs=[spec] * 4,
        out_specs=pl.BlockSpec((4, 4, B, B), lambda i: (i, 0, 0, 0)),
        out_shape=jax.ShapeDtypeStruct((HEADS, 4, B, B), BF16),
        compiler_params=params(),
    )(q, k, v, x)


def pack_audio_kernel(q_ref, k_ref, v_ref, x_ref, keys_ref, queries_ref):
    for block in range(2):
        rows = slice(block * B, block * B + B)
        keys_ref[block, 0] = k_ref[rows, :]
        keys_ref[block, 1] = v_ref[rows, :].T
        queries_ref[0, block] = x_ref[rows, :].T
        queries_ref[1, block] = q_ref[rows, :].T


def pack_audio(q, k, v, x):
    shape = jax.ShapeDtypeStruct((2, 2, B, B), BF16)
    return pl.pallas_call(
        pack_audio_kernel,
        out_shape=(shape, shape),
        compiler_params=params(),
    )(q, k, v, x)


def unpack_kernel(video_ref, audio_ref, a_ref, b_ref, q_ref, x_ref):
    a_ref[...] = video_ref[0:8, 0:2]
    b_ref[...] = video_ref[8:16, 0:2]
    q_ref[0:16] = video_ref[:, 2]
    q_ref[16:18] = audio_ref[0]
    x_ref[0:16] = video_ref[:, 3]
    x_ref[16:18] = audio_ref[1]


def unpack(video, audio):
    piece = jax.ShapeDtypeStruct((8, 2, B, B), BF16)
    queries = jax.ShapeDtypeStruct((Q_BLOCKS, B, B), BF16)
    return pl.pallas_call(
        unpack_kernel,
        out_shape=(piece, piece, queries, queries),
        compiler_params=params(),
        cost_estimate=cost(0, 5 << 20),
    )(video, audio)


def lanes(blocks):
    return jnp.concatenate([blocks[index] for index in range(blocks.shape[0])], axis=1)


def scores_of(keys, queries):
    return jnp.dot(keys, queries, preferred_element_type=F32) * SCORE_SCALE


def sums_of(weights):
    return jnp.sum(weights.reshape(-1, 8, STEP), axis=0)


def attend_careful(state, pieces, queries):
    for ref in pieces:

        def body(block, state, ref=ref):
            values, sums, shift = state
            scores = scores_of(ref[block, 0], queries)
            newest = jnp.maximum(shift, jnp.max(scores, axis=0, keepdims=True))
            factor = jnp.exp2(shift - newest)
            weights = jnp.exp2(scores - newest)
            values = values * factor + jnp.dot(
                ref[block, 1], weights.astype(BF16), preferred_element_type=F32
            )
            return values, sums * factor + sums_of(weights), newest

        state = lax.fori_loop(0, ref.shape[0], body, state)
    return state


def store_state(out_ref, state):
    values, sums, shift = state
    out_ref[0:B] = values
    out_ref[B : B + 8] = sums
    out_ref[B + 8 : B + 16] = jnp.broadcast_to(shift, (8, STEP))


def stage_kernel(sides, first, piece_count, *refs):
    query_refs, refs = refs[:sides], refs[sides:]
    pieces, refs = refs[:piece_count], refs[piece_count:]
    state_refs, out_ref = refs[:-1], refs[-1]
    if sides == 2:
        own = pl.program_id(0) < STEPS
        queries = jnp.where(own, lanes(query_refs[0][...]), lanes(query_refs[1][...]))
    else:
        queries = lanes(query_refs[0][...])

    def load(rows):
        if len(state_refs) == 2:
            return jnp.where(own, state_refs[0][rows], state_refs[1][rows])
        return state_refs[0][rows]

    scores = [scores_of(ref[:, 0].reshape(-1, B), queries) for ref in pieces]
    if first:
        shift = jnp.max(scores[0][: 2 * B], axis=0, keepdims=True)
        before = (jnp.zeros((B, STEP), F32), jnp.zeros((8, STEP), F32), shift)
    else:
        before = (load(slice(0, B)), load(slice(B, B + 8)), load(slice(B + 8, B + 9)))
    values, sums, shift = before
    for ref, score in zip(pieces, scores):
        weights = jnp.exp2(score - shift)
        sums = sums + sums_of(weights)
        values = values + jnp.dot(
            lanes(ref[:, 1]), weights.astype(BF16), preferred_element_type=F32
        )
    store_state(out_ref, (values, sums, shift))

    @pl.when(jnp.logical_not(jnp.max(sums) < LARGEST_SUM))
    def _():
        if first:
            start = (jnp.zeros((B, STEP), F32), jnp.zeros((8, STEP), F32), shift)
        else:
            start = (load(slice(0, B)), load(slice(B, B + 8)), load(slice(B + 8, B + 9)))
        store_state(out_ref, attend_careful(start, pieces, queries))


def stage(queries, pieces, states=(), offset=0):
    sides = len(queries)
    block = (STEP_BLOCKS, B, B)
    own_index = lambda i: jnp.minimum(i, STEPS - 1)
    other_index = lambda i: jnp.maximum(i - STEPS, 0)
    if sides == 2:
        in_specs = [
            pl.BlockSpec(block, lambda i: (own_index(i), 0, 0)),
            pl.BlockSpec(block, lambda i: (other_index(i), 0, 0)),
        ]
    else:
        in_specs = [pl.BlockSpec(block, lambda i: (i, 0, 0))]
    keys = 0
    for piece in pieces:
        in_specs.append(pl.BlockSpec(piece.shape, lambda i: (0, 0, 0, 0)))
        keys += piece.shape[0] * B
    if len(states) == 2:
        in_specs.append(pl.BlockSpec((ROWS, STEP), lambda i: (0, own_index(i))))
        in_specs.append(pl.BlockSpec((ROWS, STEP), lambda i: (0, other_index(i))))
    elif len(states) == 1:
        in_specs.append(pl.BlockSpec((ROWS, STEP), lambda i: (0, i + offset)))

    def kernel(*refs):
        stage_kernel(sides, len(states) == 0, len(pieces), *refs)

    width = sides * Q_BLOCKS * B
    return pl.pallas_call(
        kernel,
        grid=(sides * STEPS,),
        in_specs=in_specs,
        out_specs=pl.BlockSpec((ROWS, STEP), lambda i: (0, i)),
        out_shape=jax.ShapeDtypeStruct((ROWS, width), F32),
        compiler_params=params(),
        cost_estimate=cost(width * keys * 4 * B * 2.5, 4 << 20),
    )(*queries, *pieces, *states)


def merge_kernel(own_ref, other_ref, cross_ref, video_ref, audio_ref):
    shift_own, shift_other = own_ref[B + 8 : B + 9], other_ref[B + 8 : B + 9]
    largest = jnp.maximum(shift_own, shift_other)
    factor_own, factor_other = jnp.exp2(shift_own - largest), jnp.exp2(shift_other - largest)
    sums = (
        jnp.sum(own_ref[B : B + 8], axis=0, keepdims=True) * factor_own
        + jnp.sum(other_ref[B : B + 8], axis=0, keepdims=True) * factor_other
    )
    factor_own, factor_other = factor_own / sums, factor_other / sums
    factor_cross = 1.0 / jnp.sum(cross_ref[B : B + 8], axis=0, keepdims=True)
    for block in range(Q_BLOCKS):
        part = slice(block * B, block * B + B)
        total = (
            own_ref[0:B, part] * factor_own[:, part]
            + other_ref[0:B, part] * factor_other[:, part]
            + cross_ref[0:B, part] * factor_cross[:, part]
        ).T.astype(BF16)
        if block < HEADS:
            video_ref[block] = total
        else:
            audio_ref[block - HEADS] = total


def merge(own, other, cross):
    spec = pl.BlockSpec((ROWS, Q_BLOCKS * B), lambda i: (0, 0))
    return pl.pallas_call(
        merge_kernel,
        grid=(1,),
        in_specs=[spec] * 3,
        out_specs=(
            pl.BlockSpec((HEADS, B, B), lambda i: (0, 0, 0)),
            pl.BlockSpec((2, B, B), lambda i: (0, 0, 0)),
        ),
        out_shape=(
            jax.ShapeDtypeStruct((HEADS, B, B), BF16),
            jax.ShapeDtypeStruct((2, B, B), BF16),
        ),
        compiler_params=params(),
        cost_estimate=cost(0, 6 << 20),
    )(own, other, cross)


def project_kernel(rows_ref, weight_ref, out_ref):
    out_ref[...] = jnp.dot(
        lanes(rows_ref[...]), weight_ref[...], preferred_element_type=F32
    ).astype(BF16)


def project(rows, weight):
    half = weight.shape[2]
    tile = 512
    tiles = half // tile
    return pl.pallas_call(
        project_kernel,
        grid=(2 * tiles,),
        in_specs=[
            pl.BlockSpec((HEADS, B, B), lambda i: (0, 0, 0)),
            pl.BlockSpec((None, HEADS * B, tile), lambda i: (i // tiles, 0, i % tiles)),
        ],
        out_specs=pl.BlockSpec((B, tile), lambda i: (0, i)),
        out_shape=jax.ShapeDtypeStruct((B, 2 * half), BF16),
        compiler_params=params(),
        cost_estimate=cost(4 * B * HEADS * B * half, HEADS * B * half * 4),
    )(rows, weight)


def local(
    video_q, video_k, video_v, video_cross_q, audio_q, audio_k, audio_v, audio_cross_q, out_weight
):
    plane = ("yl", "x", "yh")

    def trade(value, distance):
        pairs = [
            (z * 4 + yh * 2 + core, (z + distance) % 4 * 4 + core * 2 + yh)
            for z in range(4)
            for yh in range(2)
            for core in range(2)
        ]
        return lax.ppermute(value, ("z", "yh", "c"), pairs)

    def up(value):
        return lax.ppermute(value, "z", [(z, (z + 1) % 4) for z in range(4)])

    def down(value):
        return lax.ppermute(value, "z", [(z, (z + 3) % 4) for z in range(4)])

    def swap(value):
        return lax.ppermute(value, "c", [(0, 1), (1, 0)])

    video = lax.all_to_all(
        pack_video(video_q, video_k, video_v, video_cross_q),
        plane,
        split_axis=0,
        concat_axis=0,
        tiled=True,
    )
    audio_pair, audio_queries = pack_audio(audio_q, audio_k, audio_v, audio_cross_q)
    audio_queries = trade(audio_queries, 0)
    audio_own = jnp.concatenate([trade(audio_pair, distance) for distance in range(4)], axis=0)
    audio_other = swap(audio_own)

    half = out_weight.shape[1] // 2
    columns = lax.dynamic_slice_in_dim(out_weight, lax.axis_index("yh") * half, half, 1)
    weight = lax.all_gather(
        after(columns, video), ("yh", "yl", "x", "c"), axis=0, tiled=True
    ).reshape(2, HEADS * B, half)

    own_a, own_b, own_q, own_x = unpack(video, audio_queries)
    other_q = swap(own_q)
    up_a, down_b = up(own_a), down(own_b)
    own_state = stage([own_q], [own_a, own_b])
    up_b, down_a = up(after(own_b, own_state)), down(after(own_a, own_state))
    other_state = stage([other_q], [own_a, own_b])
    cross_state = stage([after(own_x, other_state)], [audio_own, audio_other])
    far_a, far_b = up(after(up_a, other_state)), down(after(down_b, other_state))
    state = stage([own_q, other_q], [up_a, down_b], [own_state, other_state])
    state = stage([own_q, other_q], [up_b, down_a], [state])
    given_state = stage([other_q], [far_a, far_b], [state], STEPS)
    given = swap(given_state)
    kept = stage([after(own_q, given_state)], [far_a, far_b], [state])
    video_attn, audio_attn = merge(kept, given, cross_state)
    rows = lax.all_to_all(video_attn, plane, split_axis=0, concat_axis=0, tiled=True)
    video_mixed = project(rows, weight)
    return video_mixed, trade(audio_attn.reshape(2 * B, B), 0)


def solution(mesh):
    fine = Mesh(mesh.devices.reshape(4, 2, 2, 4, 2), ("z", "yh", "yl", "x", "c"))
    seq, head = ("z", "yh"), ("yl", "x", "c")
    tokens = P(seq + head, None)
    tower = P(seq, head)
    return jax.shard_map(
        local,
        mesh=fine,
        in_specs=(tokens,) * 4 + (tower,) * 4 + (P(head, None),),
        out_specs=(tokens, tower),
        check_vma=False,
    )
```

time: 217 us -> 194 us (0.89); the launches traced: 214 us -> 193 us
  waiting for transfers between devices: 70.2 us -> 46.6 us
  starting transfers between devices: 19.1 us -> 37.8 us
  Pallas kernels: 101 us -> 82.8 us
    pallas_call x10 -> x12, Pallas kernels: 101 us -> 82.8 us  [the longest x7 76.1 us: stage(): pl.pallas_call(kernel, grid=(sides * STEPS,), in_specs=in_specs, out_spec...]
    ppermute x10 -> x15, starting transfers between devices: 8.5 us -> 22.9 us  [the longest x3 9.18 us: swap(): return lax.ppermute(value, 'c', [(0, 1), (1, 0)])]
    all_to_all x1, waiting for transfers between devices: 45.8 us -> 32 us  [local(): lax.all_to_all(pack_video(video_q, video_k, video_v, video_cross_q), plan...]
    ppermute x10 -> x15, waiting for transfers between devices: 12.3 us -> 5.24 us  [the longest x6 4.22 us: trade(): return lax.ppermute(value, ('z', 'yh', 'c'), pairs)]
    all_to_all x1, starting transfers between devices: 3.57 us -> 7.74 us  [local(): lax.all_to_all(video_attn, plane, split_axis=0, concat_axis=0, tiled=True)]
    unnamed x19 -> x26, local copies, waits for them, and re-layouts: 7.01 us -> 10.8 us
    slice x2 -> x0, local copies, waits for them, and re-layouts: 2.78 us -> none  [the longest x1 1.94 us: local(): video_attn[:HEADS]]
  transfers between devices with their start and end apart: 13 -> 18, of which waited for: 3 -> 5; matrix products, arithmetic and copies ran while one was open for 1% -> 0% of each run, Pallas kernels for 43% -> 40%
where the time goes in v2:
time: 194 us; the launch traced here: 193 us
  Pallas kernels  82.8 us (43%)
  waiting for transfers between devices  46.6 us (24%)
  starting transfers between devices  37.8 us (19%)
  between operations  14.3 us (7%)
  local copies, waits for them, and re-layouts  11.7 us (6%)
    pallas_call x7, Pallas kernels, stage(): pl.pallas_call(kernel, grid=(sides * STEPS,), in_specs=in_specs, out_spec...  76.1 us
    all_to_all x1, waiting for transfers between devices, local(): lax.all_to_all(pack_video(video_q, video_k, video_v, video_cross_q), plan...  32 us
    unnamed x26, local copies, waits for them, and re-layouts  10.8 us
    all_to_all x1, waiting for transfers between devices, local(): lax.all_to_all(video_attn, plane, split_axis=0, concat_axis=0, tiled=True)  9.36 us
    ppermute x3, starting transfers between devices, swap(): return lax.ppermute(value, 'c', [(0, 1), (1, 0)])  9.18 us
    all_to_all x1, starting transfers between devices, local(): lax.all_to_all(video_attn, plane, split_axis=0, concat_axis=0, tiled=True)  7.74 us
    all_to_all x1, starting transfers between devices, local(): lax.all_to_all(pack_video(video_q, video_k, video_v, video_cross_q), plan...  7.18 us
    ppermute x6, starting transfers between devices, trade(): return lax.ppermute(value, ('z', 'yh', 'c'), pairs)  5.24 us
  transfers between devices with their start and end apart: 18, of which 5 were waited for; matrix products, arithmetic and copies ran while one was open for 0% of the time, Pallas kernels for 40%

profile of v2, /device:TPU:64, one launch (start us, length us, event | category | flops | bytes accessed | tf_op | source)
XLA Modules:
  0.0 193.2 jit_solution(12884944250603291765)
XLA Ops:
  7.2 0.0 copy-start
  7.2 1.1 copy-done.3
  8.3 1.0 copy-done.4
  9.3 1.0 copy-done.5
  10.4 1.0 copy-done.6
  11.4 0.9 shard_map.104
  12.4 1.3 copy-done.2
  13.7 7.2 %all-to-all-start = ((bf16[16,4,128,128]{3,2,1,0:T(8,128)(2,1)}), bf16[16,4,128,128]{3,2,1,0:T(8,128)(2,1)S(1)}, u32[]{:S(2)}, u32[]{:S(2)}) async-start(bf16[16,4,128,128]{3,2,1,0:T(8,128)(2,1)} %copy-done.2), calls=%async_computation | async-start | bytes 4194304 | tf_op jit(solution)/shard_map/all_to_all | solution.py:295
  20.9 0.0 all-gather.2.cloned.1.call-start
  21.0 0.8 constant_dynamic-slice_fusion
  21.8 32.0 %all-to-all-done.video_ref = bf16[16,4,128,128]{3,2,1,0:T(8,128)(2,1)S(1)} async-done(((bf16[16,4,128,128]{3,2,1,0:T(8,128)(2,1)}), bf16[16,4,128,128]{3,2,1,0:T(8,128)(2,1)S(1)}, u32[]{:S(2)}, u32[]{:S(2)}) %all-to-all-start) | async-done | bytes 2097184 | tf_op jit(solution)/shard_map/all_to_all | solution.py:295
  53.7 0.0 all-gather.2.cloned.1.call-update
  53.8 0.1 shard_map.105
  53.9 0.7 collective-permute-start.9
  54.6 1.7 collective-permute-start.10
  56.3 0.0 collective-permute-start.11
  56.3 1.6 collective-permute-start.12
  57.8 0.7 collective-permute-start
  58.5 1.1 collective-permute-done.10
  59.7 3.1 %collective-permute-done.11 = bf16[2,2,128,128]{3,2,1,0:T(8,128)(2,1)S(1)} collective-permute-done((bf16[2,2,128,128]{3,2,1,0:T(8,128)(2,1)S(1)}, bf16[2,2,128,128]{3,2,1,0:T(8,128)(2,1)S(1)}, u32[]{:S(2)}, u32[]{:S(2)}) %collective-permute-start.11) | collective-permute-done | bytes 131104 | tf_op jit(solution)/shard_map/ppermute | solution.py:284
  62.8 0.1 shard_map.106
  63.0 9.0 %collective-permute-start.1 = (bf16[18,128,128]{2,1,0:T(8,128)(2,1)S(1)}, bf16[18,128,128]{2,1,0:T(8,128)(2,1)S(1)}, u32[]{:S(2)}, u32[]{:S(2)}) collective-permute-start(bf16[18,128,128]{2,1,0:T(8,128)(2,1)S(1)} %get-tuple-element.25.refs_0_), channel_id=1, source_target_pairs={{0,1},{1,0},{2,3},{3,2},{4,5},{5,4},{6,7},{7,6},{8,9},{9,8},{10,11... | collective-permute-start | bytes 1769480 | tf_op jit(solution)/shard_map/ppermute | solution.py:293
  72.0 0.0 collective-permute-done.12
  72.0 0.1 collective-permute-start.13
  72.1 1.3 collective-permute-start.2
  73.4 1.8 collective-permute-start.4
  75.2 5.3 %shard_map.108.refs_4_ = f32[144,2304]{1,0:T(8,128)S(1)} custom-call(bf16[18,128,128]{2,1,0:T(8,128)(2,1)S(1)} %get-tuple-element.25.refs_0_, bf16[8,2,128,128]{3,2,1,0:T(8,128)(2,1)S(1)} %get-tuple-element.24.refs_1_, bf16[8,2,128,128]{3,2,1,0:T(8,128)(2,1)S(1)} %get-tuple-element.23.refs_2_), custom_call_target="tpu_custom_call" | custom-call | flops 6039797760 | bytes 4194304 | tf_op jit(solution)/shard_map/pallas_call | solution.py:195
  80.5 2.0 %collective-permute-start.7 = (bf16[8,2,128,128]{3,2,1,0:T(8,128)(2,1)S(1)}, bf16[8,2,128,128]{3,2,1,0:T(8,128)(2,1)S(1)}, u32[]{:S(2)}, u32[]{:S(2)}) collective-permute-start(bf16[8,2,128,128]{3,2,1,0:T(8,128)(2,1)S(1)} %get-tuple-element.24.refs_1_), channel_id=1, source_target_pairs={{0,96},{32,0},{64,32},{96,64},{1,97},{33,1},{65,33},{97,65},{2,98}... | collective-permute-start | bytes 1572872 | tf_op jit(solution)/shard_map/ppermute | solution.py:290
  82.5 0.0 collective-permute-done.1.refs_0_.refs_1_
  82.5 0.1 collective-permute-start.6
  82.6 5.3 %shard_map.107.refs_5_ = f32[144,2304]{1,0:T(8,128)S(1)} custom-call(bf16[18,128,128]{2,1,0:T(8,128)(2,1)S(1)} %collective-permute-done.1.refs_0_.refs_1_, bf16[8,2,128,128]{3,2,1,0:T(8,128)(2,1)S(1)} %get-tuple-element.24.refs_1_, bf16[8,2,128,128]{3,2,1,0:T(8,128)(2,1)S(1)} %get-tuple-element.23.refs_2_), custom_call_target="tpu_custom_call" | custom-call | flops 6039797760 | bytes 4194304 | tf_op jit(solution)/shard_map/pallas_call | solution.py:195
  87.9 1.0 collective-permute-done.4.refs_3_
  88.9 1.0 collective-permute-start.5
  89.9 0.0 collective-permute-done.2.refs_2_
  89.9 2.2 %collective-permute-start.3 = (bf16[8,2,128,128]{3,2,1,0:T(8,128)(2,1)S(1)}, bf16[8,2,128,128]{3,2,1,0:T(8,128)(2,1)S(1)}, u32[]{:S(2)}, u32[]{:S(2)}) collective-permute-start(bf16[8,2,128,128]{3,2,1,0:T(8,128)(2,1)S(1)} %collective-permute-done.2.refs_2_), channel_id=1, source_target_pairs={{0,32},{32,64},{64,96},{96,0},{1,33},{33,65},{65,97},{97,1},{2,34}... | collective-permute-start | bytes 1572872 | tf_op jit(solution)/shard_map/ppermute | solution.py:287
  92.2 26.2 %shard_map.109.refs_4_ = f32[144,4608]{1,0:T(8,128)S(1)} custom-call(bf16[18,128,128]{2,1,0:T(8,128)(2,1)S(1)} %get-tuple-element.25.refs_0_, bf16[18,128,128]{2,1,0:T(8,128)(2,1)S(1)} %collective-permute-done.1.refs_0_.refs_1_, bf16[8,2,128,128]{3,2,1,0:T(8,128)(2,1)S(1)} %collective-permute-done.2.refs_2_, ...), custom_call_target="tpu_custom_call" | custom-call | flops 12079595520 | bytes 4194304 | tf_op jit(solution)/shard_map/pallas_call | solution.py:195
  118.4 9.2 %shard_map.110.refs_3_ = f32[144,4608]{1,0:T(8,128)S(1)} custom-call(bf16[18,128,128]{2,1,0:T(8,128)(2,1)S(1)} %get-tuple-element.25.refs_0_, bf16[18,128,128]{2,1,0:T(8,128)(2,1)S(1)} %collective-permute-done.1.refs_0_.refs_1_, bf16[8,2,128,128]{3,2,1,0:T(8,128)(2,1)S(1)} %collective-permute-done.6.refs_2_, ...), custom_call_target="tpu_custom_call" | custom-call | flops 12079595520 | bytes 4194304 | tf_op jit(solution)/shard_map/pallas_call | solution.py:195
  127.6 4.6 %shard_map.111 = f32[144,2304]{1,0:T(8,128)S(1)} custom-call(bf16[18,128,128]{2,1,0:T(8,128)(2,1)S(1)} %collective-permute-done.1.refs_0_.refs_1_, bf16[8,2,128,128]{3,2,1,0:T(8,128)(2,1)S(1)} %collective-permute-done.3.refs_1_, bf16[8,2,128,128]{3,2,1,0:T(8,128)(2,1)S(1)} %collective-permute-done.5.refs_2_, f32[144,4608]{1,0:T(8,128)S(1)} %shard_map.110.refs_3_), custom_call_target="tpu_custom_call" | custom-call | flops 6039797760 | bytes 4194304 | tf_op jit(solution)/shard_map/pallas_call | solution.py:195
  132.3 0.1 collective-permute-start.8
  132.4 20.8 %shard_map.113.cross_ref = f32[144,2304]{1,0:T(8,128)S(1)} custom-call(bf16[18,128,128]{2,1,0:T(8,128)(2,1)S(1)} %get-tuple-element.27.refs_0_, bf16[8,2,128,128]{3,2,1,0:T(8,128)(2,1)S(1)} %constant_dynamic-update-slice_fusion.refs_1_, bf16[8,2,128,128]{3,2,1,0:T(8,128)(2,1)S(1)} %collective-permute-done.13.refs_2_), custom_call_target="tpu_custom_call" | custom-call | flops 6039797760 | bytes 4194304 | tf_op jit(solution)/shard_map/pallas_call | solution.py:195
  153.2 4.6 %shard_map.112.own_ref = f32[144,2304]{1,0:T(8,128)S(1)} custom-call(bf16[18,128,128]{2,1,0:T(8,128)(2,1)S(1)} %get-tuple-element.25.refs_0_, bf16[8,2,128,128]{3,2,1,0:T(8,128)(2,1)S(1)} %collective-permute-done.3.refs_1_, bf16[8,2,128,128]{3,2,1,0:T(8,128)(2,1)S(1)} %collective-permute-done.5.refs_2_, f32[144,4608]{1,0:T(8,128)S(1)} %shard_map.110.refs_3_), custom_call_target="tpu_custom_call" | custom-call | flops 6039797760 | bytes 4194304 | tf_op jit(solution)/shard_map/pallas_call | solution.py:195
  157.8 1.2 shard_map.114
  159.0 7.7 %all-to-all-start.1 = ((bf16[16,128,128]{2,1,0:T(8,128)(2,1)}), bf16[16,128,128]{2,1,0:T(8,128)(2,1)S(1)}, u32[]{:S(2)}, u32[]{:S(2)}) async-start(bf16[16,128,128]{2,1,0:T(8,128)(2,1)} %get-tuple-element.29), calls=%async_computation.1 | async-start | bytes 1048576 | tf_op jit(solution)/shard_map/all_to_all | solution.py:327
  166.8 0.7 collective-permute-start.14
  167.4 9.4 %all-to-all-done.1.rows_ref = bf16[16,128,128]{2,1,0:T(8,128)(2,1)S(1)} async-done(((bf16[16,128,128]{2,1,0:T(8,128)(2,1)}), bf16[16,128,128]{2,1,0:T(8,128)(2,1)S(1)}, u32[]{:S(2)}, u32[]{:S(2)}) %all-to-all-start.1) | async-done | bytes 524320 | tf_op jit(solution)/shard_map/all_to_all | solution.py:327
  176.8 4.6 %copy-done.1 = bf16[4096,1536]{1,0:T(8,128)(2,1)S(1)} copy-done((bf16[4096,1536]{1,0:T(8,128)(2,1)S(1)}, bf16[4096,1536]{1,0:T(8,128)(2,1)}, u32[]{:S(2)}) %copy-start.1) | copy-done | bytes 12582936
  181.4 4.3 %shard_map.115 = bf16[128,3072]{1,0:T(8,128)(2,1)} custom-call(bf16[16,128,128]{2,1,0:T(8,128)(2,1)S(1)} %all-to-all-done.1.rows_ref, bf16[2,2048,1536]{2,1,0:T(8,128)(2,1)S(1)} %bitcast.2), custom_call_target="tpu_custom_call" | custom-call | flops 1610612736 | bytes 12582912 | tf_op jit(solution)/shard_map/pallas_call | solution.py:258
  185.7 0.6 copy.15
  (29 shorter events, 0.1 us)
Async XLA Ops:
  7.2 13.8 %copy-start = (bf16[128,3072]{1,0:T(8,128)(2,1)S(1)}, bf16[128,3072]{1,0:T(8,128)(2,1)}, u32[]{:S(2)}) copy-start(bf16[128,3072]{1,0:T(8,128)(2,1)} %param.17) | copy-start | bytes 2359300
  7.2 1.1 copy-start.3
  8.3 1.0 copy-start.4
  9.3 1.0 copy-start.5
  10.4 1.0 copy-start.6
  12.4 1.3 copy-start.2
  13.7 40.1 %copy-start.7 = (bf16[256,128]{1,0:T(8,128)(2,1)S(1)}, bf16[256,128]{1,0:T(8,128)(2,1)}, u32[]{:S(2)}) copy-start(bf16[256,128]{1,0:T(8,128)(2,1)} %q_ref.3) | copy-start | bytes 196612
  13.7 40.1 %copy-start.8 = (bf16[256,128]{1,0:T(8,128)(2,1)S(1)}, bf16[256,128]{1,0:T(8,128)(2,1)}, u32[]{:S(2)}) copy-start(bf16[256,128]{1,0:T(8,128)(2,1)} %k_ref.3) | copy-start | bytes 196612
  13.7 40.1 %copy-start.9 = (bf16[256,128]{1,0:T(8,128)(2,1)S(1)}, bf16[256,128]{1,0:T(8,128)(2,1)}, u32[]{:S(2)}) copy-start(bf16[256,128]{1,0:T(8,128)(2,1)} %v_ref.3) | copy-start | bytes 196612
  13.7 40.1 %copy-start.10 = (bf16[256,128]{1,0:T(8,128)(2,1)S(1)}, bf16[256,128]{1,0:T(8,128)(2,1)}, u32[]{:S(2)}) copy-start(bf16[256,128]{1,0:T(8,128)(2,1)} %x_ref.3) | copy-start | bytes 196612
  13.7 40.0 %all-to-all-start = ((bf16[16,4,128,128]{3,2,1,0:T(8,128)(2,1)}), bf16[16,4,128,128]{3,2,1,0:T(8,128)(2,1)S(1)}, u32[]{:S(2)}, u32[]{:S(2)}) async-start(bf16[16,4,128,128]{3,2,1,0:T(8,128)(2,1)} %copy-done.2), calls=%async_computation | async-start | bytes 4194304 | tf_op jit(solution)/shard_map/all_to_all | solution.py:295
  20.9 155.9 %all-gather.2.cloned.1.call-start = ((), (), s32[]{:S(2)}) async-start(), calls=%async_computation.2 | async-start | bytes 12976128 | tf_op jit(solution)/shard_map/all_gather | solution.py:309
  53.9 4.6 %collective-permute-start.9 = (bf16[2,2,128,128]{3,2,1,0:T(8,128)(2,1)S(1)}, bf16[2,2,128,128]{3,2,1,0:T(8,128)(2,1)S(1)}, u32[]{:S(2)}, u32[]{:S(2)}) collective-permute-start(bf16[2,2,128,128]{3,2,1,0:T(8,128)(2,1)S(1)} %get-tuple-element.28), channel_id=1, source_target_pairs={{0,0},{1,16},{16,1},{17,17},{32,32},{33,48},{48,33},{49,49},{64,64... | collective-permute-start | bytes 393224 | tf_op jit(solution)/shard_map/ppermute | solution.py:284
  54.6 5.0 %collective-permute-start.10 = (bf16[2,2,128,128]{3,2,1,0:T(8,128)(2,1)S(1)}, bf16[2,2,128,128]{3,2,1,0:T(8,128)(2,1)S(1)}, u32[]{:S(2)}, u32[]{:S(2)}) collective-permute-start(bf16[2,2,128,128]{3,2,1,0:T(8,128)(2,1)S(1)} %get-tuple-element.28), channel_id=1, source_target_pairs={{0,32},{1,48},{16,33},{17,49},{32,64},{33,80},{48,65},{49,81},{64,... | collective-permute-start | bytes 393224 | tf_op jit(solution)/shard_map/ppermute | solution.py:284
  56.3 6.5 %collective-permute-start.11 = (bf16[2,2,128,128]{3,2,1,0:T(8,128)(2,1)S(1)}, bf16[2,2,128,128]{3,2,1,0:T(8,128)(2,1)S(1)}, u32[]{:S(2)}, u32[]{:S(2)}) collective-permute-start(bf16[2,2,128,128]{3,2,1,0:T(8,128)(2,1)S(1)} %get-tuple-element.28), channel_id=1, source_target_pairs={{0,64},{1,80},{16,65},{17,81},{32,96},{33,112},{48,97},{49,113},{6... | collective-permute-start | bytes 393224 | tf_op jit(solution)/shard_map/ppermute | solution.py:284
  56.3 15.7 %collective-permute-start.12 = (bf16[2,2,128,128]{3,2,1,0:T(8,128)(2,1)S(1)}, bf16[2,2,128,128]{3,2,1,0:T(8,128)(2,1)S(1)}, u32[]{:S(2)}, u32[]{:S(2)}) collective-permute-start(bf16[2,2,128,128]{3,2,1,0:T(8,128)(2,1)S(1)} %get-tuple-element.28), channel_id=1, source_target_pairs={{0,96},{1,112},{16,97},{17,113},{32,0},{33,16},{48,1},{49,17},{64,... | collective-permute-start | bytes 393224 | tf_op jit(solution)/shard_map/ppermute | solution.py:284
  57.8 5.0 %collective-permute-start = (bf16[2,2,128,128]{3,2,1,0:T(8,128)(2,1)S(1)}, bf16[2,2,128,128]{3,2,1,0:T(8,128)(2,1)S(1)}, u32[]{:S(2)}, u32[]{:S(2)}) collective-permute-start(bf16[2,2,128,128]{3,2,1,0:T(8,128)(2,1)S(1)} %get-tuple-element.17), channel_id=1, source_target_pairs={{0,0},{1,16},{16,1},{17,17},{32,32},{33,48},{48,33},{49,49},{64,64... | collective-permute-start | bytes 393224 | tf_op jit(solution)/shard_map/ppermute | solution.py:284
  63.0 19.5 %collective-permute-start.1 = (bf16[18,128,128]{2,1,0:T(8,128)(2,1)S(1)}, bf16[18,128,128]{2,1,0:T(8,128)(2,1)S(1)}, u32[]{:S(2)}, u32[]{:S(2)}) collective-permute-start(bf16[18,128,128]{2,1,0:T(8,128)(2,1)S(1)} %get-tuple-element.25.refs_0_), channel_id=1, source_target_pairs={{0,1},{1,0},{2,3},{3,2},{4,5},{5,4},{6,7},{7,6},{8,9},{9,8},{10,11... | collective-permute-start | bytes 1769480 | tf_op jit(solution)/shard_map/ppermute | solution.py:293
  72.0 60.4 %collective-permute-start.13 = (bf16[8,2,128,128]{3,2,1,0:T(8,128)(2,1)S(1)}, bf16[8,2,128,128]{3,2,1,0:T(8,128)(2,1)S(1)}, u32[]{:S(2)}, u32[]{:S(2)}) collective-permute-start(bf16[8,2,128,128]{3,2,1,0:T(8,128)(2,1)S(1)} %constant_dynamic-update-slice_fusion.refs_1_), channel_id=1, source_target_pairs={{0,1},{1,0},{2,3},{3,2},{4,5},{5,4},{6,7},{7,6},{8,9},{9,8},{10,11... | collective-permute-start | bytes 1572872 | tf_op jit(solution)/shard_map/ppermute | solution.py:293
  72.1 17.8 %collective-permute-start.2 = (bf16[8,2,128,128]{3,2,1,0:T(8,128)(2,1)S(1)}, bf16[8,2,128,128]{3,2,1,0:T(8,128)(2,1)S(1)}, u32[]{:S(2)}, u32[]{:S(2)}) collective-permute-start(bf16[8,2,128,128]{3,2,1,0:T(8,128)(2,1)S(1)} %get-tuple-element.24.refs_1_), channel_id=1, source_target_pairs={{0,32},{32,64},{64,96},{96,0},{1,33},{33,65},{65,97},{97,1},{2,34}... | collective-permute-start | bytes 1572872 | tf_op jit(solution)/shard_map/ppermute | solution.py:287
  73.4 15.5 %collective-permute-start.4 = (bf16[8,2,128,128]{3,2,1,0:T(8,128)(2,1)S(1)}, bf16[8,2,128,128]{3,2,1,0:T(8,128)(2,1)S(1)}, u32[]{:S(2)}, u32[]{:S(2)}) collective-permute-start(bf16[8,2,128,128]{3,2,1,0:T(8,128)(2,1)S(1)} %get-tuple-element.23.refs_2_), channel_id=1, source_target_pairs={{0,96},{32,0},{64,32},{96,64},{1,97},{33,1},{65,33},{97,65},{2,98}... | collective-permute-start | bytes 1572872 | tf_op jit(solution)/shard_map/ppermute | solution.py:290
  80.5 37.9 %collective-permute-start.7 = (bf16[8,2,128,128]{3,2,1,0:T(8,128)(2,1)S(1)}, bf16[8,2,128,128]{3,2,1,0:T(8,128)(2,1)S(1)}, u32[]{:S(2)}, u32[]{:S(2)}) collective-permute-start(bf16[8,2,128,128]{3,2,1,0:T(8,128)(2,1)S(1)} %get-tuple-element.24.refs_1_), channel_id=1, source_target_pairs={{0,96},{32,0},{64,32},{96,64},{1,97},{33,1},{65,33},{97,65},{2,98}... | collective-permute-start | bytes 1572872 | tf_op jit(solution)/shard_map/ppermute | solution.py:290
  82.5 35.9 %collective-permute-start.6 = (bf16[8,2,128,128]{3,2,1,0:T(8,128)(2,1)S(1)}, bf16[8,2,128,128]{3,2,1,0:T(8,128)(2,1)S(1)}, u32[]{:S(2)}, u32[]{:S(2)}) collective-permute-start(bf16[8,2,128,128]{3,2,1,0:T(8,128)(2,1)S(1)} %get-tuple-element.23.refs_2_), channel_id=1, source_target_pairs={{0,32},{32,64},{64,96},{96,0},{1,33},{33,65},{65,97},{97,1},{2,34}... | collective-permute-start | bytes 1572872 | tf_op jit(solution)/shard_map/ppermute | solution.py:287
  88.9 38.7 %collective-permute-start.5 = (bf16[8,2,128,128]{3,2,1,0:T(8,128)(2,1)S(1)}, bf16[8,2,128,128]{3,2,1,0:T(8,128)(2,1)S(1)}, u32[]{:S(2)}, u32[]{:S(2)}) collective-permute-start(bf16[8,2,128,128]{3,2,1,0:T(8,128)(2,1)S(1)} %collective-permute-done.4.refs_3_), channel_id=1, source_target_pairs={{0,96},{32,0},{64,32},{96,64},{1,97},{33,1},{65,33},{97,65},{2,98}... | collective-permute-start | bytes 1572872 | tf_op jit(solution)/shard_map/ppermute | solution.py:290
  89.9 37.7 %collective-permute-start.3 = (bf16[8,2,128,128]{3,2,1,0:T(8,128)(2,1)S(1)}, bf16[8,2,128,128]{3,2,1,0:T(8,128)(2,1)S(1)}, u32[]{:S(2)}, u32[]{:S(2)}) collective-permute-start(bf16[8,2,128,128]{3,2,1,0:T(8,128)(2,1)S(1)} %collective-permute-done.2.refs_2_), channel_id=1, source_target_pairs={{0,32},{32,64},{64,96},{96,0},{1,33},{33,65},{65,97},{97,1},{2,34}... | collective-permute-start | bytes 1572872 | tf_op jit(solution)/shard_map/ppermute | solution.py:287
  132.3 25.5 %collective-permute-start.8 = (f32[144,2304]{1,0:T(8,128)S(1)}, f32[144,2304]{1,0:T(8,128)S(1)}, u32[]{:S(2)}, u32[]{:S(2)}) collective-permute-start(f32[144,2304]{1,0:T(8,128)S(1)} %shard_map.111), channel_id=1, source_target_pairs={{0,1},{1,0},{2,3},{3,2},{4,5},{5,4},{6,7},{7,6},{8,9},{9,8},{10,11... | collective-permute-start | bytes 3981320 | tf_op jit(solution)/shard_map/ppermute | solution.py:293
  159.0 17.8 %all-to-all-start.1 = ((bf16[16,128,128]{2,1,0:T(8,128)(2,1)}), bf16[16,128,128]{2,1,0:T(8,128)(2,1)S(1)}, u32[]{:S(2)}, u32[]{:S(2)}) async-start(bf16[16,128,128]{2,1,0:T(8,128)(2,1)} %get-tuple-element.29), calls=%async_computation.1 | async-start | bytes 1048576 | tf_op jit(solution)/shard_map/all_to_all | solution.py:327
  166.8 0.7 collective-permute-start.14
  176.8 4.6 %copy-start.1 = (bf16[4096,1536]{1,0:T(8,128)(2,1)S(1)}, bf16[4096,1536]{1,0:T(8,128)(2,1)}, u32[]{:S(2)}) copy-start(bf16[4096,1536]{1,0:T(8,128)(2,1)} %all-gather.2.cloned.1.call-done) | copy-start | bytes 37748740
Sparse Core Ops, SparseCore 0:
  53.9 63.4 all-gather.1

commit v3 on v2

--- a/solution.py
+++ b/solution.py
@@ -14,9 +14,13 @@
 Q_BLOCKS = 18
 STEP_BLOCKS = 6
 STEP = STEP_BLOCKS * B
+VIDEO = 8
 STEPS = Q_BLOCKS // STEP_BLOCKS
 ROWS = B + 16
 VMEM = 24 << 20
+PACK = 4
+PROJECT_AHEAD = 8
+PROJECT_ROWS = 512
 
 
 def params():
@@ -31,56 +35,84 @@
     return lax.optimization_barrier((value, *others))[0]
 
 
-def pack_video_kernel(q_ref, k_ref, v_ref, x_ref, out_ref):
-    for head in range(HEADS // 4):
-        columns = slice(head * B, head * B + B)
-        out_ref[head, 0] = k_ref[:, columns]
-        out_ref[head, 1] = v_ref[:, columns].T
-        out_ref[head, 2] = q_ref[:, columns].T
-        out_ref[head, 3] = x_ref[:, columns].T
+def pack_video_kernel(q_ref, k_ref, v_ref, x_ref, out_ref, rows, packed, in_semaphores, out_semaphores):
+    pieces = HEADS // PACK
+    ins, outs = [], []
+    for piece in range(pieces):
+        columns = pl.ds(piece * PACK * B, PACK * B)
+        ins.append(
+            [
+                pltpu.make_async_copy(
+                    ref.at[:, columns], rows.at[index, :, columns], in_semaphores.at[index, piece]
+                )
+                for index, ref in enumerate((k_ref, v_ref, q_ref, x_ref))
+            ]
+        )
+        heads = pl.ds(piece * PACK, PACK)
+        outs.append(
+            pltpu.make_async_copy(packed.at[heads], out_ref.at[heads], out_semaphores.at[piece])
+        )
+        for copy in ins[piece]:
+            copy.start()
+    for piece in range(pieces):
+        for copy in ins[piece]:
+            copy.wait()
+        for head in range(piece * PACK, (piece + 1) * PACK):
+            columns = slice(head * B, head * B + B)
+            packed[head, 0] = rows[0, :, columns]
+            for index in range(1, 4):
+                packed[head, index] = rows[index, :, columns].T
+        outs[piece].start()
+    for copy in outs:
+        copy.wait()
 
 
 def pack_video(q, k, v, x):
-    spec = pl.BlockSpec((B, 4 * B), lambda i: (0, i))
+    pieces = HEADS // PACK
+    any_space = pl.BlockSpec(memory_space=pl.ANY)
     return pl.pallas_call(
         pack_video_kernel,
-        grid=(4,),
-        in_specs=[spec] * 4,
-        out_specs=pl.BlockSpec((4, 4, B, B), lambda i: (i, 0, 0, 0)),
+        in_specs=[any_space] * 4,
+        out_specs=any_space,
         out_shape=jax.ShapeDtypeStruct((HEADS, 4, B, B), BF16),
+        scratch_shapes=[
+            pltpu.VMEM((4, B, HEADS * B), BF16),
+            pltpu.VMEM((HEADS, 4, B, B), BF16),
+            pltpu.SemaphoreType.DMA((4, pieces)),
+            pltpu.SemaphoreType.DMA((pieces,)),
+        ],
+        compiler_params=pltpu.CompilerParams(vmem_limit_bytes=62 << 20),
+    )(q, k, v, x)
+
+
+def pack_audio_kernel(q_ref, k_ref, v_ref, x_ref, out_ref):
+    for block in range(2):
+        rows = slice(block * B, block * B + B)
+        out_ref[block, 0] = k_ref[rows, :]
+        out_ref[block, 1] = v_ref[rows, :].T
+        out_ref[block, 2] = x_ref[rows, :].T
+        out_ref[block, 3] = q_ref[rows, :].T
+
+
+def pack_audio(q, k, v, x):
+    return pl.pallas_call(
+        pack_audio_kernel,
+        out_shape=jax.ShapeDtypeStruct((2, 4, B, B), BF16),
         compiler_params=params(),
     )(q, k, v, x)
 
 
-def pack_audio_kernel(q_ref, k_ref, v_ref, x_ref, keys_ref, queries_ref):
-    for block in range(2):
-        rows = slice(block * B, block * B + B)
-        keys_ref[block, 0] = k_ref[rows, :]
-        keys_ref[block, 1] = v_ref[rows, :].T
-        queries_ref[0, block] = x_ref[rows, :].T
-        queries_ref[1, block] = q_ref[rows, :].T
-
-
-def pack_audio(q, k, v, x):
-    shape = jax.ShapeDtypeStruct((2, 2, B, B), BF16)
-    return pl.pallas_call(
-        pack_audio_kernel,
-        out_shape=(shape, shape),
-        compiler_params=params(),
-    )(q, k, v, x)
-
-
 def unpack_kernel(video_ref, audio_ref, a_ref, b_ref, q_ref, x_ref):
-    a_ref[...] = video_ref[0:8, 0:2]
-    b_ref[...] = video_ref[8:16, 0:2]
-    q_ref[0:16] = video_ref[:, 2]
-    q_ref[16:18] = audio_ref[0]
-    x_ref[0:16] = video_ref[:, 3]
-    x_ref[16:18] = audio_ref[1]
+    for piece, out_ref in enumerate((a_ref, b_ref)):
+        out_ref[0:VIDEO] = video_ref[piece * VIDEO : (piece + 1) * VIDEO, 0:2]
+        out_ref[VIDEO] = audio_ref[piece, 0:2]
+    for index, out_ref in enumerate((q_ref, x_ref)):
+        out_ref[0:HEADS] = video_ref[:, 2 + index]
+        out_ref[HEADS:Q_BLOCKS] = audio_ref[:, 2 + index]
 
 
 def unpack(video, audio):
-    piece = jax.ShapeDtypeStruct((8, 2, B, B), BF16)
+    piece = jax.ShapeDtypeStruct((VIDEO + 1, 2, B, B), BF16)
     queries = jax.ShapeDtypeStruct((Q_BLOCKS, B, B), BF16)
     return pl.pallas_call(
         unpack_kernel,
@@ -88,6 +120,23 @@
         compiler_params=params(),
         cost_estimate=cost(0, 5 << 20),
     )(video, audio)
+
+
+def collect_kernel(*refs):
+    for index, ref in enumerate(refs[:-1]):
+        refs[-1][index] = ref[0]
+
+
+def collect_audio(pieces):
+    return pl.pallas_call(
+        collect_kernel,
+        grid=(1,),
+        in_specs=[pl.BlockSpec((1, 2, B, B), lambda i: (VIDEO, 0, 0, 0))] * len(pieces),
+        out_specs=pl.BlockSpec((len(pieces), 2, B, B), lambda i: (0, 0, 0, 0)),
+        out_shape=jax.ShapeDtypeStruct((len(pieces), 2, B, B), BF16),
+        compiler_params=params(),
+        cost_estimate=cost(0, 1 << 20),
+    )(*pieces)
 
 
 def lanes(blocks):
@@ -116,7 +165,7 @@
             )
             return values, sums * factor + sums_of(weights), newest
 
-        state = lax.fori_loop(0, ref.shape[0], body, state)
+        state = lax.fori_loop(0, VIDEO, body, state)
     return state
 
 
@@ -142,7 +191,7 @@
             return jnp.where(own, state_refs[0][rows], state_refs[1][rows])
         return state_refs[0][rows]
 
-    scores = [scores_of(ref[:, 0].reshape(-1, B), queries) for ref in pieces]
+    scores = [scores_of(ref[0:VIDEO, 0].reshape(-1, B), queries) for ref in pieces]
     if first:
         shift = jnp.max(scores[0][: 2 * B], axis=0, keepdims=True)
         before = (jnp.zeros((B, STEP), F32), jnp.zeros((8, STEP), F32), shift)
@@ -153,7 +202,7 @@
         weights = jnp.exp2(score - shift)
         sums = sums + sums_of(weights)
         values = values + jnp.dot(
-            lanes(ref[:, 1]), weights.astype(BF16), preferred_element_type=F32
+            lanes(ref[0:VIDEO, 1]), weights.astype(BF16), preferred_element_type=F32
         )
     store_state(out_ref, (values, sums, shift))
 
@@ -181,7 +230,7 @@
     keys = 0
     for piece in pieces:
         in_specs.append(pl.BlockSpec(piece.shape, lambda i: (0, 0, 0, 0)))
-        keys += piece.shape[0] * B
+        keys += VIDEO * B
     if len(states) == 2:
         in_specs.append(pl.BlockSpec((ROWS, STEP), lambda i: (0, own_index(i))))
         in_specs.append(pl.BlockSpec((ROWS, STEP), lambda i: (0, other_index(i))))
@@ -245,28 +294,65 @@
     )(own, other, cross)
 
 
-def project_kernel(rows_ref, weight_ref, out_ref):
-    out_ref[...] = jnp.dot(
-        lanes(rows_ref[...]), weight_ref[...], preferred_element_type=F32
-    ).astype(BF16)
-
-
-def project(rows, weight):
-    half = weight.shape[2]
-    tile = 512
-    tiles = half // tile
+def project_kernel(
+    rows_ref, weight_ref, audio_in_ref, out_ref, audio_out_ref, buffer, total, semaphores
+):
+    audio_out_ref[...] = audio_in_ref[...]
+    halves, depth, half = weight_ref.shape
+    pieces = depth // PROJECT_ROWS
+    copies = []
+    for side in range(halves):
+        for piece in range(pieces):
+            rows = pl.ds(piece * PROJECT_ROWS, PROJECT_ROWS)
+            copies.append(
+                pltpu.make_async_copy(
+                    weight_ref.at[side, rows],
+                    buffer.at[side, rows],
+                    semaphores.at[side * pieces + piece],
+                )
+            )
+    for copy in copies[:PROJECT_AHEAD]:
+        copy.start()
+    for side in range(halves):
+        columns = slice(side * half, side * half + half)
+        for piece in range(pieces):
+            now = side * pieces + piece
+            copies[now].wait()
+            if now + PROJECT_AHEAD < len(copies):
+                copies[now + PROJECT_AHEAD].start()
+            blocks = slice(piece * PROJECT_ROWS // B, (piece + 1) * PROJECT_ROWS // B)
+            part = jnp.dot(
+                lanes(rows_ref[blocks]),
+                buffer[side, piece * PROJECT_ROWS : (piece + 1) * PROJECT_ROWS],
+                preferred_element_type=F32,
+            )
+            if piece == 0:
+                total[...] = part
+            elif piece < pieces - 1:
+                total[...] += part
+            else:
+                out_ref[:, columns] = (total[...] + part).astype(BF16)
+
+
+def project(rows, weight, audio):
+    halves, depth, half = weight.shape
+    vmem = pl.BlockSpec(memory_space=pltpu.VMEM)
     return pl.pallas_call(
         project_kernel,
-        grid=(2 * tiles,),
-        in_specs=[
-            pl.BlockSpec((HEADS, B, B), lambda i: (0, 0, 0)),
-            pl.BlockSpec((None, HEADS * B, tile), lambda i: (i // tiles, 0, i % tiles)),
+        in_specs=[vmem, pl.BlockSpec(memory_space=pl.ANY), vmem],
+        out_specs=(vmem, vmem),
+        out_shape=(
+            jax.ShapeDtypeStruct((B, halves * half), BF16),
+            jax.ShapeDtypeStruct((2 * B, B), BF16),
+        ),
+        scratch_shapes=[
+            pltpu.VMEM(weight.shape, BF16),
+            pltpu.VMEM((B, half), F32),
+            pltpu.SemaphoreType.DMA((halves * depth // PROJECT_ROWS,)),
         ],
-        out_specs=pl.BlockSpec((B, tile), lambda i: (0, i)),
-        out_shape=jax.ShapeDtypeStruct((B, 2 * half), BF16),
-        compiler_params=params(),
-        cost_estimate=cost(4 * B * HEADS * B * half, HEADS * B * half * 4),
-    )(rows, weight)
+        compiler_params=pltpu.CompilerParams(vmem_limit_bytes=54 << 20),
+        cost_estimate=cost(2 * B * depth * halves * half, depth * halves * half * 2),
+    )(*(pltpu.with_memory_space_constraint(value, space) for value, space in ((rows, pltpu.VMEM), (weight, pltpu.HBM), (audio, pltpu.VMEM))))
 
 
 def local(
@@ -274,9 +360,9 @@
 ):
     plane = ("yl", "x", "yh")
 
-    def trade(value, distance):
+    def trade(value):
         pairs = [
-            (z * 4 + yh * 2 + core, (z + distance) % 4 * 4 + core * 2 + yh)
+            (z * 4 + yh * 2 + core, z * 4 + core * 2 + yh)
             for z in range(4)
             for yh in range(2)
             for core in range(2)
@@ -299,34 +385,33 @@
         concat_axis=0,
         tiled=True,
     )
-    audio_pair, audio_queries = pack_audio(audio_q, audio_k, audio_v, audio_cross_q)
-    audio_queries = trade(audio_queries, 0)
-    audio_own = jnp.concatenate([trade(audio_pair, distance) for distance in range(4)], axis=0)
-    audio_other = swap(audio_own)
-
+    audio = trade(pack_audio(audio_q, audio_k, audio_v, audio_cross_q))
+    own_a, own_b, own_q, own_x = unpack(video, audio)
     half = out_weight.shape[1] // 2
     columns = lax.dynamic_slice_in_dim(out_weight, lax.axis_index("yh") * half, half, 1)
     weight = lax.all_gather(
-        after(columns, video), ("yh", "yl", "x", "c"), axis=0, tiled=True
+        after(columns, own_q), ("yh", "yl", "x", "c"), axis=0, tiled=True
     ).reshape(2, HEADS * B, half)
 
-    own_a, own_b, own_q, own_x = unpack(video, audio_queries)
     other_q = swap(own_q)
     up_a, down_b = up(own_a), down(own_b)
     own_state = stage([own_q], [own_a, own_b])
     up_b, down_a = up(after(own_b, own_state)), down(after(own_a, own_state))
     other_state = stage([other_q], [own_a, own_b])
-    cross_state = stage([after(own_x, other_state)], [audio_own, audio_other])
     far_a, far_b = up(after(up_a, other_state)), down(after(down_b, other_state))
     state = stage([own_q, other_q], [up_a, down_b], [own_state, other_state])
     state = stage([own_q, other_q], [up_b, down_a], [state])
+    audio_own = collect_audio([own_a, own_b, up_a, up_b, down_a, down_b, far_a, far_b])
+    audio_other = swap(audio_own)
     given_state = stage([other_q], [far_a, far_b], [state], STEPS)
     given = swap(given_state)
+    cross_state = stage([after(own_x, given_state)], [audio_own, audio_other])
     kept = stage([after(own_q, given_state)], [far_a, far_b], [state])
     video_attn, audio_attn = merge(kept, given, cross_state)
-    rows = lax.all_to_all(video_attn, plane, split_axis=0, concat_axis=0, tiled=True)
-    video_mixed = project(rows, weight)
-    return video_mixed, trade(audio_attn.reshape(2 * B, B), 0)
+    rows = lax.all_to_all(
+        video_attn, plane, split_axis=0, concat_axis=0, tiled=True
+    )
+    return project(rows, weight, trade(audio_attn.reshape(2 * B, B)))
 
 
 def solution(mesh):

time: 194 us -> 170 us (0.88)
  starting transfers between devices: 37.8 us -> 23.2 us
  local copies, waits for them, and re-layouts: 11.7 us -> 0.85 us
  Pallas kernels: 82.8 us -> 87.9 us
  waiting for transfers between devices: 46.6 us -> 43.4 us
    unnamed x26 -> x10, local copies, waits for them, and re-layouts: 10.8 us -> 0.03 us
    ppermute x3, starting transfers between devices: 9.18 us -> 1.9 us  [swap(): return lax.ppermute(value, 'c', [(0, 1), (1, 0)])]
    ppermute x3, starting transfers between devices: 4.83 us -> 0.37 us  [down(): return lax.ppermute(value, 'z', [(z, (z + 3) % 4) for z in range(4)])]
    ppermute x6 -> x2, waiting for transfers between devices: 4.22 us -> 0.01 us  [trade(): return lax.ppermute(value, ('z', 'yh', 'c'), pairs)]
    ppermute x3, starting transfers between devices: 3.63 us -> 7.63 us  [up(): return lax.ppermute(value, 'z', [(z, (z + 1) % 4) for z in range(4)])]
    ppermute x6 -> x2, starting transfers between devices: 5.24 us -> 1.34 us  [trade(): return lax.ppermute(value, ('z', 'yh', 'c'), pairs)]
    pallas_call x3 -> x4, Pallas kernels: 5.37 us -> 8.94 us  [the longest x1 5.96 us: project(): pl.pallas_call(project_kernel, in_specs=[vmem, pl.BlockSpec(memory_space=...]
    all_to_all x1, starting transfers between devices: 7.74 us -> 4.72 us  [local(): lax.all_to_all(video_attn, plane, split_axis=0, concat_axis=0, tiled=True)]
  transfers between devices with their start and end apart: 18 -> 14, of which waited for: 5 -> 3; matrix products, arithmetic and copies ran while one was open for 0% -> 0% of each run, Pallas kernels for 40% -> 46%
where the time goes in v3:
time: 170 us
  Pallas kernels  87.9 us (52%)
  waiting for transfers between devices  43.4 us (26%)
  starting transfers between devices  23.2 us (14%)
  between operations  14.3 us (8%)
    pallas_call x7, Pallas kernels, stage(): pl.pallas_call(kernel, grid=(sides * STEPS,), in_specs=in_specs, out_spec...  76 us
    all_to_all x1, waiting for transfers between devices, local(): lax.all_to_all(pack_video(video_q, video_k, video_v, video_cross_q), plan...  33.4 us
    all_to_all x1, waiting for transfers between devices, local(): lax.all_to_all(video_attn, plane, split_axis=0, concat_axis=0, tiled=True)  9.36 us
    ppermute x3, starting transfers between devices, up(): return lax.ppermute(value, 'z', [(z, (z + 1) % 4) for z in range(4)])  7.63 us
    all_to_all x1, starting transfers between devices, local(): lax.all_to_all(pack_video(video_q, video_k, video_v, video_cross_q), plan...  7.23 us
    pallas_call x1, Pallas kernels, project(): pl.pallas_call(project_kernel, in_specs=[vmem, pl.BlockSpec(memory_space=...  5.96 us
    all_to_all x1, starting transfers between devices, local(): lax.all_to_all(video_attn, plane, split_axis=0, concat_axis=0, tiled=True)  4.72 us
  transfers between devices with their start and end apart: 14, of which 3 were waited for; matrix products, arithmetic and copies ran while one was open for 0% of the time, Pallas kernels for 46%

profile of v3, /device:TPU:64, one launch (start us, length us, event | category | flops | bytes accessed | tf_op | source)
XLA Modules:
  0.0 169.7 jit_solution(6264639039667085080)
XLA Ops:
  7.2 0.0 copy-start
  7.2 2.8 %shard_map.104 = bf16[16,4,128,128]{3,2,1,0:T(8,128)(2,1)} custom-call(bf16[128,2048]{1,0:T(8,128)(2,1)} %q_ref.2, bf16[128,2048]{1,0:T(8,128)(2,1)} %k_ref.2, bf16[128,2048]{1,0:T(8,128)(2,1)} %v_ref.2, bf16[128,2048]{1,0:T(8,128)(2,1)} %x_ref.2), custom_call_target="tpu_custom_call" | custom-call | tf_op jit(solution)/shard_map/pallas_call | solution.py:73
  10.0 0.0 copy-start.1
  10.0 0.0 copy-start.2
  10.1 0.0 copy-start.3
  10.1 0.0 copy-start.4
  10.1 7.2 %all-to-all-start = ((bf16[16,4,128,128]{3,2,1,0:T(8,128)(2,1)}), bf16[16,4,128,128]{3,2,1,0:T(8,128)(2,1)}, u32[]{:S(2)}, u32[]{:S(2)}) async-start(bf16[16,4,128,128]{3,2,1,0:T(8,128)(2,1)} %shard_map.104), calls=%async_computation | async-start | bytes 4194304 | tf_op jit(solution)/shard_map/all_to_all | solution.py:381
  17.3 0.0 all-gather.2.cloned.1.call-start
  17.4 0.0 copy-done.1
  17.4 0.0 copy-done.2
  17.4 0.1 shard_map.105
  17.5 0.7 collective-permute-start
  18.2 0.8 constant_dynamic-slice_fusion
  19.0 0.0 collective-permute-done.audio_ref
  19.0 33.4 %all-to-all-done.video_ref = bf16[16,4,128,128]{3,2,1,0:T(8,128)(2,1)} async-done(((bf16[16,4,128,128]{3,2,1,0:T(8,128)(2,1)}), bf16[16,4,128,128]{3,2,1,0:T(8,128)(2,1)}, u32[]{:S(2)}, u32[]{:S(2)}) %all-to-all-start) | async-done | bytes 2097184 | tf_op jit(solution)/shard_map/all_to_all | solution.py:381
  52.5 1.7 %shard_map.106 = (bf16[9,2,128,128]{3,2,1,0:T(8,128)(2,1)S(1)}, bf16[9,2,128,128]{3,2,1,0:T(8,128)(2,1)S(1)}, bf16[18,128,128]{2,1,0:T(8,128)(2,1)S(1)}, bf16[18,128,128]{2,1,0:T(8,128)(2,1)S(1)}) custom-call(bf16[16,4,128,128]{3,2,1,0:T(8,128)(2,1)} %all-to-all-done.video_ref, bf16[2,4,128,128]{3,2,1,0:T(8,128)(2,1)S(1)} %collective-permute-done.audio_ref), custom_call_target="tpu_custom_call" | custom-call | bytes 5242880 | tf_op jit(solution)/shard_map/pallas_call | solution.py:117
  54.2 0.0 all-gather.2.cloned.1.call-update
  54.2 1.2 collective-permute-start.1
  55.5 0.1 collective-permute-start.4
  55.6 1.9 %collective-permute-start.2 = (bf16[9,2,128,128]{3,2,1,0:T(8,128)(2,1)S(1)}, bf16[9,2,128,128]{3,2,1,0:T(8,128)(2,1)S(1)}, u32[]{:S(2)}, u32[]{:S(2)}) collective-permute-start(bf16[9,2,128,128]{3,2,1,0:T(8,128)(2,1)S(1)} %get-tuple-element.21.refs_1_.refs_0_), channel_id=1, source_target_pairs={{0,32},{32,64},{64,96},{96,0},{1,33},{33,65},{65,97},{97,1},{2,34}... | collective-permute-start | bytes 1769480 | tf_op jit(solution)/shard_map/ppermute | solution.py:373
  57.5 5.3 %shard_map.108.refs_4_ = f32[144,2304]{1,0:T(8,128)S(1)} custom-call(bf16[18,128,128]{2,1,0:T(8,128)(2,1)S(1)} %get-tuple-element.22.refs_0_, bf16[9,2,128,128]{3,2,1,0:T(8,128)(2,1)S(1)} %get-tuple-element.21.refs_1_.refs_0_, bf16[9,2,128,128]{3,2,1,0:T(8,128)(2,1)S(1)} %get-tuple-element.20.refs_2_.refs_1_), custom_call_target="tpu_custom_call" | custom-call | flops 6039797760 | bytes 4194304 | tf_op jit(solution)/shard_map/pallas_call | solution.py:244
  62.8 0.2 collective-permute-start.7
  63.0 2.8 %collective-permute-start.6 = (bf16[9,2,128,128]{3,2,1,0:T(8,128)(2,1)S(1)}, bf16[9,2,128,128]{3,2,1,0:T(8,128)(2,1)S(1)}, u32[]{:S(2)}, u32[]{:S(2)}) collective-permute-start(bf16[9,2,128,128]{3,2,1,0:T(8,128)(2,1)S(1)} %get-tuple-element.20.refs_2_.refs_1_), channel_id=1, source_target_pairs={{0,32},{32,64},{64,96},{96,0},{1,33},{33,65},{65,97},{97,1},{2,34}... | collective-permute-start | bytes 1769480 | tf_op jit(solution)/shard_map/ppermute | solution.py:373
  65.8 0.0 collective-permute-done.1.refs_0_.refs_1_
  65.8 5.3 %shard_map.107.refs_5_ = f32[144,2304]{1,0:T(8,128)S(1)} custom-call(bf16[18,128,128]{2,1,0:T(8,128)(2,1)S(1)} %collective-permute-done.1.refs_0_.refs_1_, bf16[9,2,128,128]{3,2,1,0:T(8,128)(2,1)S(1)} %get-tuple-element.21.refs_1_.refs_0_, bf16[9,2,128,128]{3,2,1,0:T(8,128)(2,1)S(1)} %get-tuple-element.20.refs_2_.refs_1_), custom_call_target="tpu_custom_call" | custom-call | flops 6039797760 | bytes 4194304 | tf_op jit(solution)/shard_map/pallas_call | solution.py:244
  71.1 0.6 collective-permute-done.4.refs_3_.refs_5_
  71.7 0.1 collective-permute-start.5
  71.8 0.0 collective-permute-done.2.refs_2_
  71.8 2.9 %collective-permute-start.3 = (bf16[9,2,128,128]{3,2,1,0:T(8,128)(2,1)S(1)}, bf16[9,2,128,128]{3,2,1,0:T(8,128)(2,1)S(1)}, u32[]{:S(2)}, u32[]{:S(2)}) collective-permute-start(bf16[9,2,128,128]{3,2,1,0:T(8,128)(2,1)S(1)} %collective-permute-done.2.refs_2_), channel_id=1, source_target_pairs={{0,32},{32,64},{64,96},{96,0},{1,33},{33,65},{65,97},{97,1},{2,34}... | collective-permute-start | bytes 1769480 | tf_op jit(solution)/shard_map/ppermute | solution.py:373
  74.7 26.2 %shard_map.109.refs_4_ = f32[144,4608]{1,0:T(8,128)S(1)} custom-call(bf16[18,128,128]{2,1,0:T(8,128)(2,1)S(1)} %get-tuple-element.22.refs_0_, bf16[18,128,128]{2,1,0:T(8,128)(2,1)S(1)} %collective-permute-done.1.refs_0_.refs_1_, bf16[9,2,128,128]{3,2,1,0:T(8,128)(2,1)S(1)} %collective-permute-done.2.refs_2_, ...), custom_call_target="tpu_custom_call" | custom-call | flops 12079595520 | bytes 4194304 | tf_op jit(solution)/shard_map/pallas_call | solution.py:244
  100.9 0.0 collective-permute-done.7.refs_3_.refs_4_
  100.9 0.0 collective-permute-done.6.refs_2_.refs_3_
  100.9 9.2 %shard_map.110.refs_3_ = f32[144,4608]{1,0:T(8,128)S(1)} custom-call(bf16[18,128,128]{2,1,0:T(8,128)(2,1)S(1)} %get-tuple-element.22.refs_0_, bf16[18,128,128]{2,1,0:T(8,128)(2,1)S(1)} %collective-permute-done.1.refs_0_.refs_1_, bf16[9,2,128,128]{3,2,1,0:T(8,128)(2,1)S(1)} %collective-permute-done.6.refs_2_.refs_3_, ...), custom_call_target="tpu_custom_call" | custom-call | flops 12079595520 | bytes 4194304 | tf_op jit(solution)/shard_map/pallas_call | solution.py:244
  110.1 0.0 collective-permute-done.5.refs_2_.refs_7_
  110.2 0.0 collective-permute-done.3.refs_1_.refs_6_
  110.2 4.6 %shard_map.111 = f32[144,2304]{1,0:T(8,128)S(1)} custom-call(bf16[18,128,128]{2,1,0:T(8,128)(2,1)S(1)} %collective-permute-done.1.refs_0_.refs_1_, bf16[9,2,128,128]{3,2,1,0:T(8,128)(2,1)S(1)} %collective-permute-done.3.refs_1_.refs_6_, bf16[9,2,128,128]{3,2,1,0:T(8,128)(2,1)S(1)} %collective-permute-done.5.refs_2_.refs_7_, f32[144,4608]{1,0:T(8,128)S(1)} %shard_map.110.refs_3_), custom_call_target="tpu_custom_call" | custom-call | flops 6039797760 | bytes 4194304 | tf_op jit(solution)/shard_map/pallas_call | solution.py:244
  114.8 0.1 collective-permute-start.8
  115.0 0.6 collective-permute-start.9
  115.5 4.6 %shard_map.112.own_ref = f32[144,2304]{1,0:T(8,128)S(1)} custom-call(bf16[18,128,128]{2,1,0:T(8,128)(2,1)S(1)} %get-tuple-element.22.refs_0_, bf16[9,2,128,128]{3,2,1,0:T(8,128)(2,1)S(1)} %collective-permute-done.3.refs_1_.refs_6_, bf16[9,2,128,128]{3,2,1,0:T(8,128)(2,1)S(1)} %collective-permute-done.5.refs_2_.refs_7_, f32[144,4608]{1,0:T(8,128)S(1)} %shard_map.110.refs_3_), custom_call_target="tpu_custom_call" | custom-call | flops 6039797760 | bytes 4194304 | tf_op jit(solution)/shard_map/pallas_call | solution.py:244
  120.2 0.0 collective-permute-done.9.refs_2_
  120.2 20.7 %shard_map.114.cross_ref = f32[144,2304]{1,0:T(8,128)S(1)} custom-call(bf16[18,128,128]{2,1,0:T(8,128)(2,1)S(1)} %get-tuple-element.24.refs_0_, bf16[8,2,128,128]{3,2,1,0:T(8,128)(2,1)S(1)} %shard_map.113.refs_1_, bf16[8,2,128,128]{3,2,1,0:T(8,128)(2,1)S(1)} %collective-permute-done.9.refs_2_), custom_call_target="tpu_custom_call" | custom-call | flops 6039797760 | bytes 4194304 | tf_op jit(solution)/shard_map/pallas_call | solution.py:244
  140.9 0.0 collective-permute-done.8.other_ref
  140.9 1.2 shard_map.115
  142.1 4.7 %all-to-all-start.1 = ((bf16[16,128,128]{2,1,0:T(8,128)(2,1)}), bf16[16,128,128]{2,1,0:T(8,128)(2,1)S(1)}, u32[]{:S(2)}, u32[]{:S(2)}) async-start(bf16[16,128,128]{2,1,0:T(8,128)(2,1)} %get-tuple-element.25), calls=%async_computation.1 | async-start | bytes 1048576 | tf_op jit(solution)/shard_map/all_to_all | solution.py:411
  146.8 0.7 collective-permute-start.10
  147.5 0.0 collective-permute-done.10.audio_in_ref
  147.5 9.4 %all-to-all-done.1.rows_ref = bf16[16,128,128]{2,1,0:T(8,128)(2,1)S(1)} async-done(((bf16[16,128,128]{2,1,0:T(8,128)(2,1)}), bf16[16,128,128]{2,1,0:T(8,128)(2,1)S(1)}, u32[]{:S(2)}, u32[]{:S(2)}) %all-to-all-start.1) | async-done | bytes 524320 | tf_op jit(solution)/shard_map/all_to_all | solution.py:411
  156.9 6.0 %shard_map.116 = (bf16[128,3072]{1,0:T(8,128)(2,1)}, bf16[256,128]{1,0:T(8,128)(2,1)}) custom-call(bf16[16,128,128]{2,1,0:T(8,128)(2,1)S(1)} %all-to-all-done.1.rows_ref, bf16[2,2048,1536]{2,1,0:T(8,128)(2,1)} %bitcast.3, bf16[256,128]{1,0:T(8,128)(2,1)S(1)} %collective-permute-done.10.audio_in_ref), custom_call_target="tpu_custom_call" | custom-call | flops 1610612736 | bytes 12582912 | tf_op jit(solution)/shard_map/pallas_call | solution.py:340
  (5 shorter events, 0.0 us)
Async XLA Ops:
  7.2 11.0 %copy-start = (bf16[128,3072]{1,0:T(8,128)(2,1)S(1)}, bf16[128,3072]{1,0:T(8,128)(2,1)}, u32[]{:S(2)}) copy-start(bf16[128,3072]{1,0:T(8,128)(2,1)} %param.17) | copy-start | bytes 2359300
  10.0 7.3 %copy-start.1 = (bf16[256,128]{1,0:T(8,128)(2,1)S(1)}, bf16[256,128]{1,0:T(8,128)(2,1)}, u32[]{:S(2)}) copy-start(bf16[256,128]{1,0:T(8,128)(2,1)} %q_ref.3) | copy-start | bytes 196612
  10.0 7.3 %copy-start.2 = (bf16[256,128]{1,0:T(8,128)(2,1)S(1)}, bf16[256,128]{1,0:T(8,128)(2,1)}, u32[]{:S(2)}) copy-start(bf16[256,128]{1,0:T(8,128)(2,1)} %k_ref.3) | copy-start | bytes 196612
  10.1 7.3 %copy-start.3 = (bf16[256,128]{1,0:T(8,128)(2,1)S(1)}, bf16[256,128]{1,0:T(8,128)(2,1)}, u32[]{:S(2)}) copy-start(bf16[256,128]{1,0:T(8,128)(2,1)} %v_ref.3) | copy-start | bytes 196612
  10.1 7.3 %copy-start.4 = (bf16[256,128]{1,0:T(8,128)(2,1)S(1)}, bf16[256,128]{1,0:T(8,128)(2,1)}, u32[]{:S(2)}) copy-start(bf16[256,128]{1,0:T(8,128)(2,1)} %x_ref.3) | copy-start | bytes 196612
  10.1 42.4 %all-to-all-start = ((bf16[16,4,128,128]{3,2,1,0:T(8,128)(2,1)}), bf16[16,4,128,128]{3,2,1,0:T(8,128)(2,1)}, u32[]{:S(2)}, u32[]{:S(2)}) async-start(bf16[16,4,128,128]{3,2,1,0:T(8,128)(2,1)} %shard_map.104), calls=%async_computation | async-start | bytes 4194304 | tf_op jit(solution)/shard_map/all_to_all | solution.py:381
  17.3 139.6 %all-gather.2.cloned.1.call-start = ((), (), s32[]{:S(2)}) async-start(), calls=%async_computation.2 | async-start | bytes 12976128 | tf_op jit(solution)/shard_map/all_gather | solution.py:392
  17.5 1.5 collective-permute-start
  54.2 11.6 %collective-permute-start.1 = (bf16[18,128,128]{2,1,0:T(8,128)(2,1)S(1)}, bf16[18,128,128]{2,1,0:T(8,128)(2,1)S(1)}, u32[]{:S(2)}, u32[]{:S(2)}) collective-permute-start(bf16[18,128,128]{2,1,0:T(8,128)(2,1)S(1)} %get-tuple-element.22.refs_0_), channel_id=1, source_target_pairs={{0,1},{1,0},{2,3},{3,2},{4,5},{5,4},{6,7},{7,6},{8,9},{9,8},{10,11... | collective-permute-start | bytes 1769480 | tf_op jit(solution)/shard_map/ppermute | solution.py:379
  55.5 16.2 %collective-permute-start.4 = (bf16[9,2,128,128]{3,2,1,0:T(8,128)(2,1)S(1)}, bf16[9,2,128,128]{3,2,1,0:T(8,128)(2,1)S(1)}, u32[]{:S(2)}, u32[]{:S(2)}) collective-permute-start(bf16[9,2,128,128]{3,2,1,0:T(8,128)(2,1)S(1)} %get-tuple-element.20.refs_2_.refs_1_), channel_id=1, source_target_pairs={{0,96},{32,0},{64,32},{96,64},{1,97},{33,1},{65,33},{97,65},{2,98}... | collective-permute-start | bytes 1769480 | tf_op jit(solution)/shard_map/ppermute | solution.py:376
  55.6 16.2 %collective-permute-start.2 = (bf16[9,2,128,128]{3,2,1,0:T(8,128)(2,1)S(1)}, bf16[9,2,128,128]{3,2,1,0:T(8,128)(2,1)S(1)}, u32[]{:S(2)}, u32[]{:S(2)}) collective-permute-start(bf16[9,2,128,128]{3,2,1,0:T(8,128)(2,1)S(1)} %get-tuple-element.21.refs_1_.refs_0_), channel_id=1, source_target_pairs={{0,32},{32,64},{64,96},{96,0},{1,33},{33,65},{65,97},{97,1},{2,34}... | collective-permute-start | bytes 1769480 | tf_op jit(solution)/shard_map/ppermute | solution.py:373
  62.8 38.1 %collective-permute-start.7 = (bf16[9,2,128,128]{3,2,1,0:T(8,128)(2,1)S(1)}, bf16[9,2,128,128]{3,2,1,0:T(8,128)(2,1)S(1)}, u32[]{:S(2)}, u32[]{:S(2)}) collective-permute-start(bf16[9,2,128,128]{3,2,1,0:T(8,128)(2,1)S(1)} %get-tuple-element.21.refs_1_.refs_0_), channel_id=1, source_target_pairs={{0,96},{32,0},{64,32},{96,64},{1,97},{33,1},{65,33},{97,65},{2,98}... | collective-permute-start | bytes 1769480 | tf_op jit(solution)/shard_map/ppermute | solution.py:376
  63.0 37.9 %collective-permute-start.6 = (bf16[9,2,128,128]{3,2,1,0:T(8,128)(2,1)S(1)}, bf16[9,2,128,128]{3,2,1,0:T(8,128)(2,1)S(1)}, u32[]{:S(2)}, u32[]{:S(2)}) collective-permute-start(bf16[9,2,128,128]{3,2,1,0:T(8,128)(2,1)S(1)} %get-tuple-element.20.refs_2_.refs_1_), channel_id=1, source_target_pairs={{0,32},{32,64},{64,96},{96,0},{1,33},{33,65},{65,97},{97,1},{2,34}... | collective-permute-start | bytes 1769480 | tf_op jit(solution)/shard_map/ppermute | solution.py:373
  71.7 38.5 %collective-permute-start.5 = (bf16[9,2,128,128]{3,2,1,0:T(8,128)(2,1)S(1)}, bf16[9,2,128,128]{3,2,1,0:T(8,128)(2,1)S(1)}, u32[]{:S(2)}, u32[]{:S(2)}) collective-permute-start(bf16[9,2,128,128]{3,2,1,0:T(8,128)(2,1)S(1)} %collective-permute-done.4.refs_3_.refs_5_), channel_id=1, source_target_pairs={{0,96},{32,0},{64,32},{96,64},{1,97},{33,1},{65,33},{97,65},{2,98}... | collective-permute-start | bytes 1769480 | tf_op jit(solution)/shard_map/ppermute | solution.py:376
  71.8 38.4 %collective-permute-start.3 = (bf16[9,2,128,128]{3,2,1,0:T(8,128)(2,1)S(1)}, bf16[9,2,128,128]{3,2,1,0:T(8,128)(2,1)S(1)}, u32[]{:S(2)}, u32[]{:S(2)}) collective-permute-start(bf16[9,2,128,128]{3,2,1,0:T(8,128)(2,1)S(1)} %collective-permute-done.2.refs_2_), channel_id=1, source_target_pairs={{0,32},{32,64},{64,96},{96,0},{1,33},{33,65},{65,97},{97,1},{2,34}... | collective-permute-start | bytes 1769480 | tf_op jit(solution)/shard_map/ppermute | solution.py:373
  114.8 26.1 %collective-permute-start.8 = (f32[144,2304]{1,0:T(8,128)S(1)}, f32[144,2304]{1,0:T(8,128)S(1)}, u32[]{:S(2)}, u32[]{:S(2)}) collective-permute-start(f32[144,2304]{1,0:T(8,128)S(1)} %shard_map.111), channel_id=1, source_target_pairs={{0,1},{1,0},{2,3},{3,2},{4,5},{5,4},{6,7},{7,6},{8,9},{9,8},{10,11... | collective-permute-start | bytes 3981320 | tf_op jit(solution)/shard_map/ppermute | solution.py:379
  115.0 5.2 %collective-permute-start.9 = (bf16[8,2,128,128]{3,2,1,0:T(8,128)(2,1)S(1)}, bf16[8,2,128,128]{3,2,1,0:T(8,128)(2,1)S(1)}, u32[]{:S(2)}, u32[]{:S(2)}) collective-permute-start(bf16[8,2,128,128]{3,2,1,0:T(8,128)(2,1)S(1)} %shard_map.113.refs_1_), channel_id=1, source_target_pairs={{0,1},{1,0},{2,3},{3,2},{4,5},{5,4},{6,7},{7,6},{8,9},{9,8},{10,11... | collective-permute-start | bytes 1572872 | tf_op jit(solution)/shard_map/ppermute | solution.py:379
  142.1 14.8 %all-to-all-start.1 = ((bf16[16,128,128]{2,1,0:T(8,128)(2,1)}), bf16[16,128,128]{2,1,0:T(8,128)(2,1)S(1)}, u32[]{:S(2)}, u32[]{:S(2)}) async-start(bf16[16,128,128]{2,1,0:T(8,128)(2,1)} %get-tuple-element.25), calls=%async_computation.1 | async-start | bytes 1048576 | tf_op jit(solution)/shard_map/all_to_all | solution.py:411
  146.8 0.7 collective-permute-start.10
Sparse Core Ops, SparseCore 0:
  54.4 64.8 all-gather.1

commit v4 on v3

--- a/solution.py
+++ b/solution.py
@@ -12,12 +12,13 @@
 SCORE_SCALE = B**-0.5 * 1.4426950408889634
 LARGEST_SUM = 1e30
 Q_BLOCKS = 18
-STEP_BLOCKS = 6
+STEP_BLOCKS = 9
 STEP = STEP_BLOCKS * B
 VIDEO = 8
 STEPS = Q_BLOCKS // STEP_BLOCKS
 ROWS = B + 16
 VMEM = 24 << 20
+STAGE_COST = 0.6
 PACK = 4
 PROJECT_AHEAD = 8
 PROJECT_ROWS = 512
@@ -102,21 +103,28 @@
     )(q, k, v, x)
 
 
-def unpack_kernel(video_ref, audio_ref, a_ref, b_ref, q_ref, x_ref):
-    for piece, out_ref in enumerate((a_ref, b_ref)):
-        out_ref[0:VIDEO] = video_ref[piece * VIDEO : (piece + 1) * VIDEO, 0:2]
-        out_ref[VIDEO] = audio_ref[piece, 0:2]
+def unpack_kernel(video_ref, audio_ref, a_ref, b_ref, audio_out_ref, q_ref, x_ref):
+    a_ref[...] = video_ref[0:VIDEO, 0:2]
+    b_ref[...] = video_ref[VIDEO : 2 * VIDEO, 0:2]
+    audio_out_ref[...] = audio_ref[:, 0:2]
     for index, out_ref in enumerate((q_ref, x_ref)):
         out_ref[0:HEADS] = video_ref[:, 2 + index]
         out_ref[HEADS:Q_BLOCKS] = audio_ref[:, 2 + index]
 
 
 def unpack(video, audio):
-    piece = jax.ShapeDtypeStruct((VIDEO + 1, 2, B, B), BF16)
-    queries = jax.ShapeDtypeStruct((Q_BLOCKS, B, B), BF16)
+    def blocks(*shape):
+        return jax.ShapeDtypeStruct((*shape, B, B), BF16)
+
     return pl.pallas_call(
         unpack_kernel,
-        out_shape=(piece, piece, queries, queries),
+        out_shape=(
+            blocks(VIDEO, 2),
+            blocks(VIDEO, 2),
+            blocks(2, 2),
+            blocks(Q_BLOCKS),
+            blocks(Q_BLOCKS),
+        ),
         compiler_params=params(),
         cost_estimate=cost(0, 5 << 20),
     )(video, audio)
@@ -124,16 +132,13 @@
 
 def collect_kernel(*refs):
     for index, ref in enumerate(refs[:-1]):
-        refs[-1][index] = ref[0]
+        refs[-1][2 * index : 2 * index + 2] = ref[...]
 
 
 def collect_audio(pieces):
     return pl.pallas_call(
         collect_kernel,
-        grid=(1,),
-        in_specs=[pl.BlockSpec((1, 2, B, B), lambda i: (VIDEO, 0, 0, 0))] * len(pieces),
-        out_specs=pl.BlockSpec((len(pieces), 2, B, B), lambda i: (0, 0, 0, 0)),
-        out_shape=jax.ShapeDtypeStruct((len(pieces), 2, B, B), BF16),
+        out_shape=jax.ShapeDtypeStruct((2 * len(pieces), 2, B, B), BF16),
         compiler_params=params(),
         cost_estimate=cost(0, 1 << 20),
     )(*pieces)
@@ -248,7 +253,7 @@
         out_specs=pl.BlockSpec((ROWS, STEP), lambda i: (0, i)),
         out_shape=jax.ShapeDtypeStruct((ROWS, width), F32),
         compiler_params=params(),
-        cost_estimate=cost(width * keys * 4 * B * 2.5, 4 << 20),
+        cost_estimate=cost(width * keys * 4 * B * STAGE_COST, 1 << 20),
     )(*queries, *pieces, *states)
 
 
@@ -369,11 +374,14 @@
         ]
         return lax.ppermute(value, ("z", "yh", "c"), pairs)
 
+    def round_z(value, distance):
+        return lax.ppermute(value, "z", [(z, (z + distance) % 4) for z in range(4)])
+
     def up(value):
-        return lax.ppermute(value, "z", [(z, (z + 1) % 4) for z in range(4)])
+        return round_z(value, 1)
 
     def down(value):
-        return lax.ppermute(value, "z", [(z, (z + 3) % 4) for z in range(4)])
+        return round_z(value, 3)
 
     def swap(value):
         return lax.ppermute(value, "c", [(0, 1), (1, 0)])
@@ -386,7 +394,7 @@
         tiled=True,
     )
     audio = trade(pack_audio(audio_q, audio_k, audio_v, audio_cross_q))
-    own_a, own_b, own_q, own_x = unpack(video, audio)
+    own_a, own_b, own_audio, own_q, own_x = unpack(video, audio)
     half = out_weight.shape[1] // 2
     columns = lax.dynamic_slice_in_dim(out_weight, lax.axis_index("yh") * half, half, 1)
     weight = lax.all_gather(
@@ -399,13 +407,15 @@
     up_b, down_a = up(after(own_b, own_state)), down(after(own_a, own_state))
     other_state = stage([other_q], [own_a, own_b])
     far_a, far_b = up(after(up_a, other_state)), down(after(down_b, other_state))
+    heard = [round_z(after(own_audio, own_state), distance) for distance in (1, 3, 2)]
     state = stage([own_q, other_q], [up_a, down_b], [own_state, other_state])
+    audio_own = collect_audio([after(own_audio, state)] + heard)
+    audio_other = swap(audio_own)
     state = stage([own_q, other_q], [up_b, down_a], [state])
-    audio_own = collect_audio([own_a, own_b, up_a, up_b, down_a, down_b, far_a, far_b])
-    audio_other = swap(audio_own)
+    cross_state = stage([after(own_x, state)], [audio_own, audio_other])
+    state = after(state, cross_state)
     given_state = stage([other_q], [far_a, far_b], [state], STEPS)
     given = swap(given_state)
-    cross_state = stage([after(own_x, given_state)], [audio_own, audio_other])
     kept = stage([after(own_q, given_state)], [far_a, far_b], [state])
     video_attn, audio_attn = merge(kept, given, cross_state)
     rows = lax.all_to_all(

time: 170 us -> 180 us (1.059)
  Pallas kernels: 87.9 us -> 92.7 us
  waiting for transfers between devices: 43.4 us -> 46.5 us
  starting transfers between devices: 23.2 us -> 25.8 us
    pallas_call x7, Pallas kernels: 76 us -> 80.8 us  [stage(): pl.pallas_call(kernel, grid=(sides * STEPS,), in_specs=in_specs, out_spec...]
    ppermute x6 -> x9, starting transfers between devices: 8.01 us -> 10.7 us  [round_z(): return lax.ppermute(value, 'z', [(z, (z + distance) % 4) for z in range(4)])]
    all_to_all x1, waiting for transfers between devices: 9.36 us -> 11.8 us  [local(): lax.all_to_all(video_attn, plane, split_axis=0, concat_axis=0, tiled=True)]
  transfers between devices with their start and end apart: 14 -> 17, of which waited for: 3 -> 3; matrix products, arithmetic and copies ran while one was open for 0% -> 0% of each run, Pallas kernels for 46% -> 46%
where the time goes in v4:
time: 180 us
  Pallas kernels  92.7 us (52%)
  waiting for transfers between devices  46.5 us (26%)
  starting transfers between devices  25.8 us (14%)
  between operations  14.3 us (8%)
    pallas_call x7, Pallas kernels, stage(): pl.pallas_call(kernel, grid=(sides * STEPS,), in_specs=in_specs, out_spec...  80.8 us
    all_to_all x1, waiting for transfers between devices, local(): lax.all_to_all(pack_video(video_q, video_k, video_v, video_cross_q), plan...  33.4 us
    all_to_all x1, waiting for transfers between devices, local(): lax.all_to_all(video_attn, plane, split_axis=0, concat_axis=0, tiled=True)  11.8 us
    ppermute x9, starting transfers between devices, round_z(): return lax.ppermute(value, 'z', [(z, (z + distance) % 4) for z in range(4)])  10.7 us
    all_to_all x1, starting transfers between devices, local(): lax.all_to_all(pack_video(video_q, video_k, video_v, video_cross_q), plan...  7.23 us
    pallas_call x1, Pallas kernels, project(): pl.pallas_call(project_kernel, in_specs=[vmem, pl.BlockSpec(memory_space=...  5.96 us
    all_to_all x1, starting transfers between devices, local(): lax.all_to_all(video_attn, plane, split_axis=0, concat_axis=0, tiled=True)  4.81 us
  transfers between devices with their start and end apart: 17, of which 3 were waited for; matrix products, arithmetic and copies ran while one was open for 0% of the time, Pallas kernels for 46%

profile of v4, /device:TPU:64, one launch (start us, length us, event | category | flops | bytes accessed | tf_op | source)
XLA Modules:
  0.0 180.1 jit_solution(14339409173146220185)
XLA Ops:
  7.2 0.0 copy-start
  7.2 2.8 %shard_map.104 = bf16[16,4,128,128]{3,2,1,0:T(8,128)(2,1)} custom-call(bf16[128,2048]{1,0:T(8,128)(2,1)} %q_ref.2, bf16[128,2048]{1,0:T(8,128)(2,1)} %k_ref.2, bf16[128,2048]{1,0:T(8,128)(2,1)} %v_ref.2, bf16[128,2048]{1,0:T(8,128)(2,1)} %x_ref.2), custom_call_target="tpu_custom_call" | custom-call | tf_op jit(solution)/shard_map/pallas_call | solution.py:74
  10.0 0.0 copy-start.1
  10.0 0.0 copy-start.2
  10.0 0.0 copy-start.3
  10.0 0.0 copy-start.4
  10.1 7.2 %all-to-all-start = ((bf16[16,4,128,128]{3,2,1,0:T(8,128)(2,1)}), bf16[16,4,128,128]{3,2,1,0:T(8,128)(2,1)}, u32[]{:S(2)}, u32[]{:S(2)}) async-start(bf16[16,4,128,128]{3,2,1,0:T(8,128)(2,1)} %shard_map.104), calls=%async_computation | async-start | bytes 4194304 | tf_op jit(solution)/shard_map/all_to_all | solution.py:389
  17.3 0.0 all-gather.2.cloned.1.call-start
  17.4 0.1 shard_map.105
  17.5 0.7 collective-permute-start
  18.2 0.8 constant_dynamic-slice_fusion
  19.0 0.0 collective-permute-done.audio_ref
  19.0 33.4 %all-to-all-done.video_ref = bf16[16,4,128,128]{3,2,1,0:T(8,128)(2,1)} async-done(((bf16[16,4,128,128]{3,2,1,0:T(8,128)(2,1)}), bf16[16,4,128,128]{3,2,1,0:T(8,128)(2,1)}, u32[]{:S(2)}, u32[]{:S(2)}) %all-to-all-start) | async-done | bytes 2097184 | tf_op jit(solution)/shard_map/all_to_all | solution.py:389
  52.5 1.7 shard_map.106
  54.2 0.0 all-gather.2.cloned.1.call-update
  54.2 1.2 collective-permute-start.1
  55.5 1.6 collective-permute-start.2
  57.1 0.4 collective-permute-start.4
  57.5 5.3 %shard_map.108.refs_4_ = f32[144,2304]{1,0:T(8,128)S(1)} custom-call(bf16[18,128,128]{2,1,0:T(8,128)(2,1)S(1)} %get-tuple-element.32.refs_0_, bf16[8,2,128,128]{3,2,1,0:T(8,128)(2,1)S(1)} %get-tuple-element.25.refs_1_, bf16[8,2,128,128]{3,2,1,0:T(8,128)(2,1)S(1)} %get-tuple-element.24.refs_2_), custom_call_target="tpu_custom_call" | custom-call | flops 1449551488 | bytes 1048576 | tf_op jit(solution)/shard_map/pallas_call | solution.py:249
  62.8 1.7 collective-permute-start.10
  64.5 0.5 collective-permute-start.8
  65.0 0.0 collective-permute-done.1.refs_0_.refs_1_
  65.0 1.5 collective-permute-start.9
  66.5 5.3 %shard_map.107.refs_5_ = f32[144,2304]{1,0:T(8,128)S(1)} custom-call(bf16[18,128,128]{2,1,0:T(8,128)(2,1)S(1)} %collective-permute-done.1.refs_0_.refs_1_, bf16[8,2,128,128]{3,2,1,0:T(8,128)(2,1)S(1)} %get-tuple-element.25.refs_1_, bf16[8,2,128,128]{3,2,1,0:T(8,128)(2,1)S(1)} %get-tuple-element.24.refs_2_), custom_call_target="tpu_custom_call" | custom-call | flops 1449551488 | bytes 1048576 | tf_op jit(solution)/shard_map/pallas_call | solution.py:249
  71.8 1.2 collective-permute-done.2.refs_2_
  73.1 0.3 collective-permute-start.7
  73.3 0.0 collective-permute-done.4.refs_3_
  73.3 2.6 %collective-permute-start.6 = (bf16[8,2,128,128]{3,2,1,0:T(8,128)(2,1)S(1)}, bf16[8,2,128,128]{3,2,1,0:T(8,128)(2,1)S(1)}, u32[]{:S(2)}, u32[]{:S(2)}) collective-permute-start(bf16[8,2,128,128]{3,2,1,0:T(8,128)(2,1)S(1)} %get-tuple-element.24.refs_2_), channel_id=1, source_target_pairs={{0,32},{32,64},{64,96},{96,0},{1,33},{33,65},{65,97},{97,1},{2,34}... | collective-permute-start | bytes 1572872 | tf_op jit(solution)/shard_map/ppermute | solution.py:378
  75.9 28.2 %shard_map.109.refs_4_ = f32[144,4608]{1,0:T(8,128)S(1)} custom-call(bf16[18,128,128]{2,1,0:T(8,128)(2,1)S(1)} %get-tuple-element.32.refs_0_, bf16[18,128,128]{2,1,0:T(8,128)(2,1)S(1)} %collective-permute-done.1.refs_0_.refs_1_, bf16[8,2,128,128]{3,2,1,0:T(8,128)(2,1)S(1)} %collective-permute-done.2.refs_2_, ...), custom_call_target="tpu_custom_call" | custom-call | flops 2899102976 | bytes 1048576 | tf_op jit(solution)/shard_map/pallas_call | solution.py:249
  104.0 0.0 collective-permute-done.10.refs_3_
  104.1 0.0 collective-permute-done.8.refs_1_
  104.1 0.0 collective-permute-done.9.refs_2_
  104.1 0.1 collective-permute-start.11
  104.2 0.1 collective-permute-start.5
  104.3 2.0 %collective-permute-start.3 = (bf16[8,2,128,128]{3,2,1,0:T(8,128)(2,1)S(1)}, bf16[8,2,128,128]{3,2,1,0:T(8,128)(2,1)S(1)}, u32[]{:S(2)}, u32[]{:S(2)}) collective-permute-start(bf16[8,2,128,128]{3,2,1,0:T(8,128)(2,1)S(1)} %collective-permute-done.2.refs_2_), channel_id=1, source_target_pairs={{0,32},{32,64},{64,96},{96,0},{1,33},{33,65},{65,97},{97,1},{2,34}... | collective-permute-start | bytes 1572872 | tf_op jit(solution)/shard_map/ppermute | solution.py:378
  106.3 0.0 collective-permute-done.7.refs_3_
  106.3 9.0 %shard_map.110.refs_3_ = f32[144,4608]{1,0:T(8,128)S(1)} custom-call(bf16[18,128,128]{2,1,0:T(8,128)(2,1)S(1)} %get-tuple-element.32.refs_0_, bf16[18,128,128]{2,1,0:T(8,128)(2,1)S(1)} %collective-permute-done.1.refs_0_.refs_1_, bf16[8,2,128,128]{3,2,1,0:T(8,128)(2,1)S(1)} %collective-permute-done.6.refs_2_, ...), custom_call_target="tpu_custom_call" | custom-call | flops 2899102976 | bytes 1048576 | tf_op jit(solution)/shard_map/pallas_call | solution.py:249
  115.3 24.1 %shard_map.112.cross_ref = f32[144,2304]{1,0:T(8,128)S(1)} custom-call(bf16[18,128,128]{2,1,0:T(8,128)(2,1)S(1)} %get-tuple-element.27.refs_0_, bf16[8,2,128,128]{3,2,1,0:T(8,128)(2,1)S(1)} %shard_map.111.refs_1_, bf16[8,2,128,128]{3,2,1,0:T(8,128)(2,1)S(1)} %collective-permute-done.11.refs_2_), custom_call_target="tpu_custom_call" | custom-call | flops 1449551488 | bytes 1048576 | tf_op jit(solution)/shard_map/pallas_call | solution.py:249
  139.5 0.0 collective-permute-done.5.refs_2_
  139.5 4.5 %shard_map.113 = f32[144,2304]{1,0:T(8,128)S(1)} custom-call(bf16[18,128,128]{2,1,0:T(8,128)(2,1)S(1)} %collective-permute-done.1.refs_0_.refs_1_, bf16[8,2,128,128]{3,2,1,0:T(8,128)(2,1)S(1)} %collective-permute-done.3.refs_1_, bf16[8,2,128,128]{3,2,1,0:T(8,128)(2,1)S(1)} %collective-permute-done.5.refs_2_, f32[144,4608]{1,0:T(8,128)S(1)} %shard_map.110.refs_3_), custom_call_target="tpu_custom_call" | custom-call | flops 1449551488 | bytes 1048576 | tf_op jit(solution)/shard_map/pallas_call | solution.py:249
  144.0 0.3 collective-permute-start.12
  144.3 4.5 %shard_map.114.own_ref = f32[144,2304]{1,0:T(8,128)S(1)} custom-call(bf16[18,128,128]{2,1,0:T(8,128)(2,1)S(1)} %get-tuple-element.32.refs_0_, bf16[8,2,128,128]{3,2,1,0:T(8,128)(2,1)S(1)} %collective-permute-done.3.refs_1_, bf16[8,2,128,128]{3,2,1,0:T(8,128)(2,1)S(1)} %collective-permute-done.5.refs_2_, f32[144,4608]{1,0:T(8,128)S(1)} %shard_map.110.refs_3_), custom_call_target="tpu_custom_call" | custom-call | flops 1449551488 | bytes 1048576 | tf_op jit(solution)/shard_map/pallas_call | solution.py:249
  148.8 1.2 shard_map.115
  150.0 4.8 %all-to-all-start.1 = ((bf16[16,128,128]{2,1,0:T(8,128)(2,1)}), bf16[16,128,128]{2,1,0:T(8,128)(2,1)S(1)}, u32[]{:S(2)}, u32[]{:S(2)}) async-start(bf16[16,128,128]{2,1,0:T(8,128)(2,1)} %get-tuple-element.33), calls=%async_computation.1 | async-start | bytes 1048576 | tf_op jit(solution)/shard_map/all_to_all | solution.py:421
  154.8 0.7 collective-permute-start.13
  155.5 0.0 collective-permute-done.13.audio_in_ref
  155.5 11.8 %all-to-all-done.1.rows_ref = bf16[16,128,128]{2,1,0:T(8,128)(2,1)S(1)} async-done(((bf16[16,128,128]{2,1,0:T(8,128)(2,1)}), bf16[16,128,128]{2,1,0:T(8,128)(2,1)S(1)}, u32[]{:S(2)}, u32[]{:S(2)}) %all-to-all-start.1) | async-done | bytes 524320 | tf_op jit(solution)/shard_map/all_to_all | solution.py:421
  167.3 6.0 %shard_map.116 = (bf16[128,3072]{1,0:T(8,128)(2,1)}, bf16[256,128]{1,0:T(8,128)(2,1)}) custom-call(bf16[16,128,128]{2,1,0:T(8,128)(2,1)S(1)} %all-to-all-done.1.rows_ref, bf16[2,2048,1536]{2,1,0:T(8,128)(2,1)} %bitcast.3, bf16[256,128]{1,0:T(8,128)(2,1)S(1)} %collective-permute-done.13.audio_in_ref), custom_call_target="tpu_custom_call" | custom-call | flops 1610612736 | bytes 12582912 | tf_op jit(solution)/shard_map/pallas_call | solution.py:345
  (11 shorter events, 0.1 us)
Async XLA Ops:
  7.2 11.0 %copy-start = (bf16[128,3072]{1,0:T(8,128)(2,1)S(1)}, bf16[128,3072]{1,0:T(8,128)(2,1)}, u32[]{:S(2)}) copy-start(bf16[128,3072]{1,0:T(8,128)(2,1)} %param.17) | copy-start | bytes 2359300
  10.0 7.3 %copy-start.1 = (bf16[256,128]{1,0:T(8,128)(2,1)S(1)}, bf16[256,128]{1,0:T(8,128)(2,1)}, u32[]{:S(2)}) copy-start(bf16[256,128]{1,0:T(8,128)(2,1)} %q_ref.3) | copy-start | bytes 196612
  10.0 7.3 %copy-start.2 = (bf16[256,128]{1,0:T(8,128)(2,1)S(1)}, bf16[256,128]{1,0:T(8,128)(2,1)}, u32[]{:S(2)}) copy-start(bf16[256,128]{1,0:T(8,128)(2,1)} %k_ref.3) | copy-start | bytes 196612
  10.0 7.3 %copy-start.3 = (bf16[256,128]{1,0:T(8,128)(2,1)S(1)}, bf16[256,128]{1,0:T(8,128)(2,1)}, u32[]{:S(2)}) copy-start(bf16[256,128]{1,0:T(8,128)(2,1)} %v_ref.3) | copy-start | bytes 196612
  10.0 7.3 %copy-start.4 = (bf16[256,128]{1,0:T(8,128)(2,1)S(1)}, bf16[256,128]{1,0:T(8,128)(2,1)}, u32[]{:S(2)}) copy-start(bf16[256,128]{1,0:T(8,128)(2,1)} %x_ref.3) | copy-start | bytes 196612
  10.1 42.4 %all-to-all-start = ((bf16[16,4,128,128]{3,2,1,0:T(8,128)(2,1)}), bf16[16,4,128,128]{3,2,1,0:T(8,128)(2,1)}, u32[]{:S(2)}, u32[]{:S(2)}) async-start(bf16[16,4,128,128]{3,2,1,0:T(8,128)(2,1)} %shard_map.104), calls=%async_computation | async-start | bytes 4194304 | tf_op jit(solution)/shard_map/all_to_all | solution.py:389
  17.3 150.0 %all-gather.2.cloned.1.call-start = ((), (), s32[]{:S(2)}) async-start(), calls=%async_computation.2 | async-start | bytes 12976128 | tf_op jit(solution)/shard_map/all_gather | solution.py:400
  17.5 1.5 collective-permute-start
  54.2 10.8 %collective-permute-start.1 = (bf16[18,128,128]{2,1,0:T(8,128)(2,1)S(1)}, bf16[18,128,128]{2,1,0:T(8,128)(2,1)S(1)}, u32[]{:S(2)}, u32[]{:S(2)}) collective-permute-start(bf16[18,128,128]{2,1,0:T(8,128)(2,1)S(1)} %get-tuple-element.32.refs_0_), channel_id=1, source_target_pairs={{0,1},{1,0},{2,3},{3,2},{4,5},{5,4},{6,7},{7,6},{8,9},{9,8},{10,11... | collective-permute-start | bytes 1769480 | tf_op jit(solution)/shard_map/ppermute | solution.py:387
  55.5 17.6 %collective-permute-start.2 = (bf16[8,2,128,128]{3,2,1,0:T(8,128)(2,1)S(1)}, bf16[8,2,128,128]{3,2,1,0:T(8,128)(2,1)S(1)}, u32[]{:S(2)}, u32[]{:S(2)}) collective-permute-start(bf16[8,2,128,128]{3,2,1,0:T(8,128)(2,1)S(1)} %get-tuple-element.25.refs_1_), channel_id=1, source_target_pairs={{0,32},{32,64},{64,96},{96,0},{1,33},{33,65},{65,97},{97,1},{2,34}... | collective-permute-start | bytes 1572872 | tf_op jit(solution)/shard_map/ppermute | solution.py:378
  57.1 16.2 %collective-permute-start.4 = (bf16[8,2,128,128]{3,2,1,0:T(8,128)(2,1)S(1)}, bf16[8,2,128,128]{3,2,1,0:T(8,128)(2,1)S(1)}, u32[]{:S(2)}, u32[]{:S(2)}) collective-permute-start(bf16[8,2,128,128]{3,2,1,0:T(8,128)(2,1)S(1)} %get-tuple-element.24.refs_2_), channel_id=1, source_target_pairs={{0,96},{32,0},{64,32},{96,64},{1,97},{33,1},{65,33},{97,65},{2,98}... | collective-permute-start | bytes 1572872 | tf_op jit(solution)/shard_map/ppermute | solution.py:378
  62.8 41.3 %collective-permute-start.10 = (bf16[2,2,128,128]{3,2,1,0:T(8,128)(2,1)S(1)}, bf16[2,2,128,128]{3,2,1,0:T(8,128)(2,1)S(1)}, u32[]{:S(2)}, u32[]{:S(2)}) collective-permute-start(bf16[2,2,128,128]{3,2,1,0:T(8,128)(2,1)S(1)} %get-tuple-element.30.refs_0_), channel_id=1, source_target_pairs={{0,64},{32,96},{64,0},{96,32},{1,65},{33,97},{65,1},{97,33},{2,66}... | collective-permute-start | bytes 393224 | tf_op jit(solution)/shard_map/ppermute | solution.py:378
  64.5 39.5 %collective-permute-start.8 = (bf16[2,2,128,128]{3,2,1,0:T(8,128)(2,1)S(1)}, bf16[2,2,128,128]{3,2,1,0:T(8,128)(2,1)S(1)}, u32[]{:S(2)}, u32[]{:S(2)}) collective-permute-start(bf16[2,2,128,128]{3,2,1,0:T(8,128)(2,1)S(1)} %get-tuple-element.30.refs_0_), channel_id=1, source_target_pairs={{0,32},{32,64},{64,96},{96,0},{1,33},{33,65},{65,97},{97,1},{2,34}... | collective-permute-start | bytes 393224 | tf_op jit(solution)/shard_map/ppermute | solution.py:378
  65.0 39.0 %collective-permute-start.9 = (bf16[2,2,128,128]{3,2,1,0:T(8,128)(2,1)S(1)}, bf16[2,2,128,128]{3,2,1,0:T(8,128)(2,1)S(1)}, u32[]{:S(2)}, u32[]{:S(2)}) collective-permute-start(bf16[2,2,128,128]{3,2,1,0:T(8,128)(2,1)S(1)} %get-tuple-element.30.refs_0_), channel_id=1, source_target_pairs={{0,96},{32,0},{64,32},{96,64},{1,97},{33,1},{65,33},{97,65},{2,98}... | collective-permute-start | bytes 393224 | tf_op jit(solution)/shard_map/ppermute | solution.py:378
  73.1 33.3 %collective-permute-start.7 = (bf16[8,2,128,128]{3,2,1,0:T(8,128)(2,1)S(1)}, bf16[8,2,128,128]{3,2,1,0:T(8,128)(2,1)S(1)}, u32[]{:S(2)}, u32[]{:S(2)}) collective-permute-start(bf16[8,2,128,128]{3,2,1,0:T(8,128)(2,1)S(1)} %get-tuple-element.25.refs_1_), channel_id=1, source_target_pairs={{0,96},{32,0},{64,32},{96,64},{1,97},{33,1},{65,33},{97,65},{2,98}... | collective-permute-start | bytes 1572872 | tf_op jit(solution)/shard_map/ppermute | solution.py:378
  73.3 33.0 %collective-permute-start.6 = (bf16[8,2,128,128]{3,2,1,0:T(8,128)(2,1)S(1)}, bf16[8,2,128,128]{3,2,1,0:T(8,128)(2,1)S(1)}, u32[]{:S(2)}, u32[]{:S(2)}) collective-permute-start(bf16[8,2,128,128]{3,2,1,0:T(8,128)(2,1)S(1)} %get-tuple-element.24.refs_2_), channel_id=1, source_target_pairs={{0,32},{32,64},{64,96},{96,0},{1,33},{33,65},{65,97},{97,1},{2,34}... | collective-permute-start | bytes 1572872 | tf_op jit(solution)/shard_map/ppermute | solution.py:378
  104.1 11.2 %collective-permute-start.11 = (bf16[8,2,128,128]{3,2,1,0:T(8,128)(2,1)S(1)}, bf16[8,2,128,128]{3,2,1,0:T(8,128)(2,1)S(1)}, u32[]{:S(2)}, u32[]{:S(2)}) collective-permute-start(bf16[8,2,128,128]{3,2,1,0:T(8,128)(2,1)S(1)} %shard_map.111.refs_1_), channel_id=1, source_target_pairs={{0,1},{1,0},{2,3},{3,2},{4,5},{5,4},{6,7},{7,6},{8,9},{9,8},{10,11... | collective-permute-start | bytes 1572872 | tf_op jit(solution)/shard_map/ppermute | solution.py:387
  104.2 35.2 %collective-permute-start.5 = (bf16[8,2,128,128]{3,2,1,0:T(8,128)(2,1)S(1)}, bf16[8,2,128,128]{3,2,1,0:T(8,128)(2,1)S(1)}, u32[]{:S(2)}, u32[]{:S(2)}) collective-permute-start(bf16[8,2,128,128]{3,2,1,0:T(8,128)(2,1)S(1)} %collective-permute-done.4.refs_3_), channel_id=1, source_target_pairs={{0,96},{32,0},{64,32},{96,64},{1,97},{33,1},{65,33},{97,65},{2,98}... | collective-permute-start | bytes 1572872 | tf_op jit(solution)/shard_map/ppermute | solution.py:378
  104.3 35.2 %collective-permute-start.3 = (bf16[8,2,128,128]{3,2,1,0:T(8,128)(2,1)S(1)}, bf16[8,2,128,128]{3,2,1,0:T(8,128)(2,1)S(1)}, u32[]{:S(2)}, u32[]{:S(2)}) collective-permute-start(bf16[8,2,128,128]{3,2,1,0:T(8,128)(2,1)S(1)} %collective-permute-done.2.refs_2_), channel_id=1, source_target_pairs={{0,32},{32,64},{64,96},{96,0},{1,33},{33,65},{65,97},{97,1},{2,34}... | collective-permute-start | bytes 1572872 | tf_op jit(solution)/shard_map/ppermute | solution.py:378
  144.0 4.8 %collective-permute-start.12 = (f32[144,2304]{1,0:T(8,128)S(1)}, f32[144,2304]{1,0:T(8,128)S(1)}, u32[]{:S(2)}, u32[]{:S(2)}) collective-permute-start(f32[144,2304]{1,0:T(8,128)S(1)} %shard_map.113), channel_id=1, source_target_pairs={{0,1},{1,0},{2,3},{3,2},{4,5},{5,4},{6,7},{7,6},{8,9},{9,8},{10,11... | collective-permute-start | bytes 3981320 | tf_op jit(solution)/shard_map/ppermute | solution.py:387
  150.0 17.3 %all-to-all-start.1 = ((bf16[16,128,128]{2,1,0:T(8,128)(2,1)}), bf16[16,128,128]{2,1,0:T(8,128)(2,1)S(1)}, u32[]{:S(2)}, u32[]{:S(2)}) async-start(bf16[16,128,128]{2,1,0:T(8,128)(2,1)} %get-tuple-element.33), calls=%async_computation.1 | async-start | bytes 1048576 | tf_op jit(solution)/shard_map/all_to_all | solution.py:421
  154.8 0.7 collective-permute-start.13
Sparse Core Ops, SparseCore 0:
  54.3 63.2 all-gather.1

commit v5 on v4

--- a/solution.py
+++ b/solution.py
@@ -11,6 +11,7 @@
 HEADS = 16
 SCORE_SCALE = B**-0.5 * 1.4426950408889634
 LARGEST_SUM = 1e30
+AUDIO = 2
 Q_BLOCKS = 18
 STEP_BLOCKS = 9
 STEP = STEP_BLOCKS * B
@@ -103,13 +104,27 @@
     )(q, k, v, x)
 
 
-def unpack_kernel(video_ref, audio_ref, a_ref, b_ref, audio_out_ref, q_ref, x_ref):
-    a_ref[...] = video_ref[0:VIDEO, 0:2]
-    b_ref[...] = video_ref[VIDEO : 2 * VIDEO, 0:2]
+def unpack_kernel(video_ref, audio_ref, a_ref, b_ref, audio_out_ref, q_ref, x_ref, semaphores):
+    first, second = pl.ds(0, VIDEO), pl.ds(VIDEO, VIDEO)
+    moves = (
+        (video_ref.at[first, pl.ds(0, 2)], a_ref),
+        (video_ref.at[second, pl.ds(0, 2)], b_ref),
+        (video_ref.at[first, 2], q_ref.at[first]),
+        (video_ref.at[second, 2], q_ref.at[second]),
+        (video_ref.at[first, 3], x_ref.at[first]),
+        (video_ref.at[second, 3], x_ref.at[second]),
+    )
+    copies = [
+        pltpu.make_async_copy(source, target, semaphores.at[index])
+        for index, (source, target) in enumerate(moves)
+    ]
+    for copy in copies:
+        copy.start()
     audio_out_ref[...] = audio_ref[:, 0:2]
-    for index, out_ref in enumerate((q_ref, x_ref)):
-        out_ref[0:HEADS] = video_ref[:, 2 + index]
-        out_ref[HEADS:Q_BLOCKS] = audio_ref[:, 2 + index]
+    q_ref[HEADS:Q_BLOCKS] = audio_ref[:, 2]
+    x_ref[HEADS:Q_BLOCKS] = audio_ref[:, 3]
+    for copy in copies:
+        copy.wait()
 
 
 def unpack(video, audio):
@@ -118,16 +133,19 @@
 
     return pl.pallas_call(
         unpack_kernel,
+        in_specs=[pl.BlockSpec(memory_space=pl.ANY), pl.BlockSpec(memory_space=pltpu.VMEM)],
+        out_specs=(pl.BlockSpec(memory_space=pltpu.VMEM),) * 5,
         out_shape=(
             blocks(VIDEO, 2),
             blocks(VIDEO, 2),
-            blocks(2, 2),
+            blocks(AUDIO, 2),
             blocks(Q_BLOCKS),
             blocks(Q_BLOCKS),
         ),
+        scratch_shapes=[pltpu.SemaphoreType.DMA((6,))],
         compiler_params=params(),
         cost_estimate=cost(0, 5 << 20),
-    )(video, audio)
+    )(pltpu.with_memory_space_constraint(video, pltpu.HBM), audio)
 
 
 def collect_kernel(*refs):

time: 180 us -> 180 us (level)
  no operation moved by 1% of the time
where the time goes in v5:
time: 180 us
  Pallas kernels  92.5 us (51%)
  waiting for transfers between devices  46.5 us (26%)
  starting transfers between devices  25.8 us (14%)
  between operations  14.3 us (8%)
    pallas_call x7, Pallas kernels, stage(): pl.pallas_call(kernel, grid=(sides * STEPS,), in_specs=in_specs, out_spec...  80.8 us
    all_to_all x1, waiting for transfers between devices, local(): lax.all_to_all(pack_video(video_q, video_k, video_v, video_cross_q), plan...  33.4 us
    all_to_all x1, waiting for transfers between devices, local(): lax.all_to_all(video_attn, plane, split_axis=0, concat_axis=0, tiled=True)  11.8 us
    ppermute x9, starting transfers between devices, round_z(): return lax.ppermute(value, 'z', [(z, (z + distance) % 4) for z in range(4)])  10.7 us
    all_to_all x1, starting transfers between devices, local(): lax.all_to_all(pack_video(video_q, video_k, video_v, video_cross_q), plan...  7.23 us
    pallas_call x1, Pallas kernels, project(): pl.pallas_call(project_kernel, in_specs=[vmem, pl.BlockSpec(memory_space=...  5.96 us
    all_to_all x1, starting transfers between devices, local(): lax.all_to_all(video_attn, plane, split_axis=0, concat_axis=0, tiled=True)  4.81 us
  transfers between devices with their start and end apart: 17, of which 3 were waited for; matrix products, arithmetic and copies ran while one was open for 0% of the time, Pallas kernels for 46%

profile of v5, /device:TPU:64, one launch (start us, length us, event | category | flops | bytes accessed | tf_op | source)
XLA Modules:
  0.0 179.9 jit_solution(3689375370274901986)
XLA Ops:
  7.2 0.0 copy-start
  7.2 2.8 %shard_map.104 = bf16[16,4,128,128]{3,2,1,0:T(8,128)(2,1)} custom-call(bf16[128,2048]{1,0:T(8,128)(2,1)} %q_ref.2, bf16[128,2048]{1,0:T(8,128)(2,1)} %k_ref.2, bf16[128,2048]{1,0:T(8,128)(2,1)} %v_ref.2, bf16[128,2048]{1,0:T(8,128)(2,1)} %x_ref.2), custom_call_target="tpu_custom_call" | custom-call | tf_op jit(solution)/shard_map/pallas_call | solution.py:75
  10.0 0.0 copy-start.1
  10.0 0.0 copy-start.2
  10.0 0.0 copy-start.3
  10.0 0.0 copy-start.4
  10.1 7.2 %all-to-all-start = ((bf16[16,4,128,128]{3,2,1,0:T(8,128)(2,1)}), bf16[16,4,128,128]{3,2,1,0:T(8,128)(2,1)}, u32[]{:S(2)}, u32[]{:S(2)}) async-start(bf16[16,4,128,128]{3,2,1,0:T(8,128)(2,1)} %shard_map.104), calls=%async_computation | async-start | bytes 4194304 | tf_op jit(solution)/shard_map/all_to_all | solution.py:407
  17.3 0.0 all-gather.2.cloned.1.call-start
  17.4 0.1 shard_map.105
  17.5 0.7 collective-permute-start
  18.2 0.8 constant_dynamic-slice_fusion
  19.0 0.0 collective-permute-done.audio_ref
  19.0 33.4 %all-to-all-done.video_ref = bf16[16,4,128,128]{3,2,1,0:T(8,128)(2,1)} async-done(((bf16[16,4,128,128]{3,2,1,0:T(8,128)(2,1)}), bf16[16,4,128,128]{3,2,1,0:T(8,128)(2,1)}, u32[]{:S(2)}, u32[]{:S(2)}) %all-to-all-start) | async-done | bytes 2097184 | tf_op jit(solution)/shard_map/all_to_all | solution.py:407
  52.5 1.6 shard_map.106
  54.0 0.0 all-gather.2.cloned.1.call-update
  54.0 1.2 collective-permute-start.1
  55.3 1.6 collective-permute-start.2
  56.9 0.4 collective-permute-start.4
  57.3 5.3 %shard_map.108.refs_4_ = f32[144,2304]{1,0:T(8,128)S(1)} custom-call(bf16[18,128,128]{2,1,0:T(8,128)(2,1)S(1)} %get-tuple-element.32.refs_0_, bf16[8,2,128,128]{3,2,1,0:T(8,128)(2,1)S(1)} %get-tuple-element.25.refs_1_, bf16[8,2,128,128]{3,2,1,0:T(8,128)(2,1)S(1)} %get-tuple-element.24.refs_2_), custom_call_target="tpu_custom_call" | custom-call | flops 1449551488 | bytes 1048576 | tf_op jit(solution)/shard_map/pallas_call | solution.py:267
  62.6 1.7 collective-permute-start.10
  64.3 0.5 collective-permute-start.8
  64.8 0.0 collective-permute-done.1.refs_0_.refs_1_
  64.9 1.5 collective-permute-start.9
  66.4 5.3 %shard_map.107.refs_5_ = f32[144,2304]{1,0:T(8,128)S(1)} custom-call(bf16[18,128,128]{2,1,0:T(8,128)(2,1)S(1)} %collective-permute-done.1.refs_0_.refs_1_, bf16[8,2,128,128]{3,2,1,0:T(8,128)(2,1)S(1)} %get-tuple-element.25.refs_1_, bf16[8,2,128,128]{3,2,1,0:T(8,128)(2,1)S(1)} %get-tuple-element.24.refs_2_), custom_call_target="tpu_custom_call" | custom-call | flops 1449551488 | bytes 1048576 | tf_op jit(solution)/shard_map/pallas_call | solution.py:267
  71.6 1.2 collective-permute-done.2.refs_2_
  72.9 0.3 collective-permute-start.7
  73.1 0.0 collective-permute-done.4.refs_3_
  73.1 2.6 %collective-permute-start.6 = (bf16[8,2,128,128]{3,2,1,0:T(8,128)(2,1)S(1)}, bf16[8,2,128,128]{3,2,1,0:T(8,128)(2,1)S(1)}, u32[]{:S(2)}, u32[]{:S(2)}) collective-permute-start(bf16[8,2,128,128]{3,2,1,0:T(8,128)(2,1)S(1)} %get-tuple-element.24.refs_2_), channel_id=1, source_target_pairs={{0,32},{32,64},{64,96},{96,0},{1,33},{33,65},{65,97},{97,1},{2,34}... | collective-permute-start | bytes 1572872 | tf_op jit(solution)/shard_map/ppermute | solution.py:396
  75.7 28.2 %shard_map.109.refs_4_ = f32[144,4608]{1,0:T(8,128)S(1)} custom-call(bf16[18,128,128]{2,1,0:T(8,128)(2,1)S(1)} %get-tuple-element.32.refs_0_, bf16[18,128,128]{2,1,0:T(8,128)(2,1)S(1)} %collective-permute-done.1.refs_0_.refs_1_, bf16[8,2,128,128]{3,2,1,0:T(8,128)(2,1)S(1)} %collective-permute-done.2.refs_2_, ...), custom_call_target="tpu_custom_call" | custom-call | flops 2899102976 | bytes 1048576 | tf_op jit(solution)/shard_map/pallas_call | solution.py:267
  103.9 0.0 collective-permute-done.10.refs_3_
  103.9 0.0 collective-permute-done.8.refs_1_
  103.9 0.1 collective-permute-start.11
  104.0 0.1 collective-permute-start.5
  104.1 2.0 %collective-permute-start.3 = (bf16[8,2,128,128]{3,2,1,0:T(8,128)(2,1)S(1)}, bf16[8,2,128,128]{3,2,1,0:T(8,128)(2,1)S(1)}, u32[]{:S(2)}, u32[]{:S(2)}) collective-permute-start(bf16[8,2,128,128]{3,2,1,0:T(8,128)(2,1)S(1)} %collective-permute-done.2.refs_2_), channel_id=1, source_target_pairs={{0,32},{32,64},{64,96},{96,0},{1,33},{33,65},{65,97},{97,1},{2,34}... | collective-permute-start | bytes 1572872 | tf_op jit(solution)/shard_map/ppermute | solution.py:396
  106.1 9.0 %shard_map.110.refs_3_ = f32[144,4608]{1,0:T(8,128)S(1)} custom-call(bf16[18,128,128]{2,1,0:T(8,128)(2,1)S(1)} %get-tuple-element.32.refs_0_, bf16[18,128,128]{2,1,0:T(8,128)(2,1)S(1)} %collective-permute-done.1.refs_0_.refs_1_, bf16[8,2,128,128]{3,2,1,0:T(8,128)(2,1)S(1)} %collective-permute-done.6.refs_2_, ...), custom_call_target="tpu_custom_call" | custom-call | flops 2899102976 | bytes 1048576 | tf_op jit(solution)/shard_map/pallas_call | solution.py:267
  115.2 0.0 collective-permute-done.11.refs_2_
  115.2 24.1 %shard_map.112.cross_ref = f32[144,2304]{1,0:T(8,128)S(1)} custom-call(bf16[18,128,128]{2,1,0:T(8,128)(2,1)S(1)} %get-tuple-element.27.refs_0_, bf16[8,2,128,128]{3,2,1,0:T(8,128)(2,1)S(1)} %shard_map.111.refs_1_, bf16[8,2,128,128]{3,2,1,0:T(8,128)(2,1)S(1)} %collective-permute-done.11.refs_2_), custom_call_target="tpu_custom_call" | custom-call | flops 1449551488 | bytes 1048576 | tf_op jit(solution)/shard_map/pallas_call | solution.py:267
  139.3 0.0 collective-permute-done.5.refs_2_
  139.3 4.5 %shard_map.113 = f32[144,2304]{1,0:T(8,128)S(1)} custom-call(bf16[18,128,128]{2,1,0:T(8,128)(2,1)S(1)} %collective-permute-done.1.refs_0_.refs_1_, bf16[8,2,128,128]{3,2,1,0:T(8,128)(2,1)S(1)} %collective-permute-done.3.refs_1_, bf16[8,2,128,128]{3,2,1,0:T(8,128)(2,1)S(1)} %collective-permute-done.5.refs_2_, f32[144,4608]{1,0:T(8,128)S(1)} %shard_map.110.refs_3_), custom_call_target="tpu_custom_call" | custom-call | flops 1449551488 | bytes 1048576 | tf_op jit(solution)/shard_map/pallas_call | solution.py:267
  143.8 0.3 collective-permute-start.12
  144.1 4.5 %shard_map.114.own_ref = f32[144,2304]{1,0:T(8,128)S(1)} custom-call(bf16[18,128,128]{2,1,0:T(8,128)(2,1)S(1)} %get-tuple-element.32.refs_0_, bf16[8,2,128,128]{3,2,1,0:T(8,128)(2,1)S(1)} %collective-permute-done.3.refs_1_, bf16[8,2,128,128]{3,2,1,0:T(8,128)(2,1)S(1)} %collective-permute-done.5.refs_2_, f32[144,4608]{1,0:T(8,128)S(1)} %shard_map.110.refs_3_), custom_call_target="tpu_custom_call" | custom-call | flops 1449551488 | bytes 1048576 | tf_op jit(solution)/shard_map/pallas_call | solution.py:267
  148.6 0.0 collective-permute-done.12.other_ref
  148.6 1.2 shard_map.115
  149.8 4.8 %all-to-all-start.1 = ((bf16[16,128,128]{2,1,0:T(8,128)(2,1)}), bf16[16,128,128]{2,1,0:T(8,128)(2,1)S(1)}, u32[]{:S(2)}, u32[]{:S(2)}) async-start(bf16[16,128,128]{2,1,0:T(8,128)(2,1)} %get-tuple-element.33), calls=%async_computation.1 | async-start | bytes 1048576 | tf_op jit(solution)/shard_map/all_to_all | solution.py:439
  154.6 0.7 collective-permute-start.13
  155.3 0.0 collective-permute-done.13.audio_in_ref
  155.3 11.8 %all-to-all-done.1.rows_ref = bf16[16,128,128]{2,1,0:T(8,128)(2,1)S(1)} async-done(((bf16[16,128,128]{2,1,0:T(8,128)(2,1)}), bf16[16,128,128]{2,1,0:T(8,128)(2,1)S(1)}, u32[]{:S(2)}, u32[]{:S(2)}) %all-to-all-start.1) | async-done | bytes 524320 | tf_op jit(solution)/shard_map/all_to_all | solution.py:439
  167.1 6.0 %shard_map.116 = (bf16[128,3072]{1,0:T(8,128)(2,1)}, bf16[256,128]{1,0:T(8,128)(2,1)}) custom-call(bf16[16,128,128]{2,1,0:T(8,128)(2,1)S(1)} %all-to-all-done.1.rows_ref, bf16[2,2048,1536]{2,1,0:T(8,128)(2,1)} %bitcast.3, bf16[256,128]{1,0:T(8,128)(2,1)S(1)} %collective-permute-done.13.audio_in_ref), custom_call_target="tpu_custom_call" | custom-call | flops 1610612736 | bytes 12582912 | tf_op jit(solution)/shard_map/pallas_call | solution.py:363
  (11 shorter events, 0.1 us)
Async XLA Ops:
  7.2 11.0 %copy-start = (bf16[128,3072]{1,0:T(8,128)(2,1)S(1)}, bf16[128,3072]{1,0:T(8,128)(2,1)}, u32[]{:S(2)}) copy-start(bf16[128,3072]{1,0:T(8,128)(2,1)} %param.17) | copy-start | bytes 2359300
  10.0 7.3 %copy-start.1 = (bf16[256,128]{1,0:T(8,128)(2,1)S(1)}, bf16[256,128]{1,0:T(8,128)(2,1)}, u32[]{:S(2)}) copy-start(bf16[256,128]{1,0:T(8,128)(2,1)} %q_ref.3) | copy-start | bytes 196612
  10.0 7.3 %copy-start.2 = (bf16[256,128]{1,0:T(8,128)(2,1)S(1)}, bf16[256,128]{1,0:T(8,128)(2,1)}, u32[]{:S(2)}) copy-start(bf16[256,128]{1,0:T(8,128)(2,1)} %k_ref.3) | copy-start | bytes 196612
  10.0 7.3 %copy-start.3 = (bf16[256,128]{1,0:T(8,128)(2,1)S(1)}, bf16[256,128]{1,0:T(8,128)(2,1)}, u32[]{:S(2)}) copy-start(bf16[256,128]{1,0:T(8,128)(2,1)} %v_ref.3) | copy-start | bytes 196612
  10.0 7.3 %copy-start.4 = (bf16[256,128]{1,0:T(8,128)(2,1)S(1)}, bf16[256,128]{1,0:T(8,128)(2,1)}, u32[]{:S(2)}) copy-start(bf16[256,128]{1,0:T(8,128)(2,1)} %x_ref.3) | copy-start | bytes 196612
  10.1 42.4 %all-to-all-start = ((bf16[16,4,128,128]{3,2,1,0:T(8,128)(2,1)}), bf16[16,4,128,128]{3,2,1,0:T(8,128)(2,1)}, u32[]{:S(2)}, u32[]{:S(2)}) async-start(bf16[16,4,128,128]{3,2,1,0:T(8,128)(2,1)} %shard_map.104), calls=%async_computation | async-start | bytes 4194304 | tf_op jit(solution)/shard_map/all_to_all | solution.py:407
  17.3 149.8 %all-gather.2.cloned.1.call-start = ((), (), s32[]{:S(2)}) async-start(), calls=%async_computation.2 | async-start | bytes 12976128 | tf_op jit(solution)/shard_map/all_gather | solution.py:418
  17.5 1.5 collective-permute-start
  54.0 10.8 %collective-permute-start.1 = (bf16[18,128,128]{2,1,0:T(8,128)(2,1)S(1)}, bf16[18,128,128]{2,1,0:T(8,128)(2,1)S(1)}, u32[]{:S(2)}, u32[]{:S(2)}) collective-permute-start(bf16[18,128,128]{2,1,0:T(8,128)(2,1)S(1)} %get-tuple-element.32.refs_0_), channel_id=1, source_target_pairs={{0,1},{1,0},{2,3},{3,2},{4,5},{5,4},{6,7},{7,6},{8,9},{9,8},{10,11... | collective-permute-start | bytes 1769480 | tf_op jit(solution)/shard_map/ppermute | solution.py:405
  55.3 17.6 %collective-permute-start.2 = (bf16[8,2,128,128]{3,2,1,0:T(8,128)(2,1)S(1)}, bf16[8,2,128,128]{3,2,1,0:T(8,128)(2,1)S(1)}, u32[]{:S(2)}, u32[]{:S(2)}) collective-permute-start(bf16[8,2,128,128]{3,2,1,0:T(8,128)(2,1)S(1)} %get-tuple-element.25.refs_1_), channel_id=1, source_target_pairs={{0,32},{32,64},{64,96},{96,0},{1,33},{33,65},{65,97},{97,1},{2,34}... | collective-permute-start | bytes 1572872 | tf_op jit(solution)/shard_map/ppermute | solution.py:396
  56.9 16.2 %collective-permute-start.4 = (bf16[8,2,128,128]{3,2,1,0:T(8,128)(2,1)S(1)}, bf16[8,2,128,128]{3,2,1,0:T(8,128)(2,1)S(1)}, u32[]{:S(2)}, u32[]{:S(2)}) collective-permute-start(bf16[8,2,128,128]{3,2,1,0:T(8,128)(2,1)S(1)} %get-tuple-element.24.refs_2_), channel_id=1, source_target_pairs={{0,96},{32,0},{64,32},{96,64},{1,97},{33,1},{65,33},{97,65},{2,98}... | collective-permute-start | bytes 1572872 | tf_op jit(solution)/shard_map/ppermute | solution.py:396
  62.6 41.3 %collective-permute-start.10 = (bf16[2,2,128,128]{3,2,1,0:T(8,128)(2,1)S(1)}, bf16[2,2,128,128]{3,2,1,0:T(8,128)(2,1)S(1)}, u32[]{:S(2)}, u32[]{:S(2)}) collective-permute-start(bf16[2,2,128,128]{3,2,1,0:T(8,128)(2,1)S(1)} %get-tuple-element.30.refs_0_), channel_id=1, source_target_pairs={{0,64},{32,96},{64,0},{96,32},{1,65},{33,97},{65,1},{97,33},{2,66}... | collective-permute-start | bytes 393224 | tf_op jit(solution)/shard_map/ppermute | solution.py:396
  64.3 39.6 %collective-permute-start.8 = (bf16[2,2,128,128]{3,2,1,0:T(8,128)(2,1)S(1)}, bf16[2,2,128,128]{3,2,1,0:T(8,128)(2,1)S(1)}, u32[]{:S(2)}, u32[]{:S(2)}) collective-permute-start(bf16[2,2,128,128]{3,2,1,0:T(8,128)(2,1)S(1)} %get-tuple-element.30.refs_0_), channel_id=1, source_target_pairs={{0,32},{32,64},{64,96},{96,0},{1,33},{33,65},{65,97},{97,1},{2,34}... | collective-permute-start | bytes 393224 | tf_op jit(solution)/shard_map/ppermute | solution.py:396
  64.9 39.0 %collective-permute-start.9 = (bf16[2,2,128,128]{3,2,1,0:T(8,128)(2,1)S(1)}, bf16[2,2,128,128]{3,2,1,0:T(8,128)(2,1)S(1)}, u32[]{:S(2)}, u32[]{:S(2)}) collective-permute-start(bf16[2,2,128,128]{3,2,1,0:T(8,128)(2,1)S(1)} %get-tuple-element.30.refs_0_), channel_id=1, source_target_pairs={{0,96},{32,0},{64,32},{96,64},{1,97},{33,1},{65,33},{97,65},{2,98}... | collective-permute-start | bytes 393224 | tf_op jit(solution)/shard_map/ppermute | solution.py:396
  72.9 33.3 %collective-permute-start.7 = (bf16[8,2,128,128]{3,2,1,0:T(8,128)(2,1)S(1)}, bf16[8,2,128,128]{3,2,1,0:T(8,128)(2,1)S(1)}, u32[]{:S(2)}, u32[]{:S(2)}) collective-permute-start(bf16[8,2,128,128]{3,2,1,0:T(8,128)(2,1)S(1)} %get-tuple-element.25.refs_1_), channel_id=1, source_target_pairs={{0,96},{32,0},{64,32},{96,64},{1,97},{33,1},{65,33},{97,65},{2,98}... | collective-permute-start | bytes 1572872 | tf_op jit(solution)/shard_map/ppermute | solution.py:396
  73.1 33.0 %collective-permute-start.6 = (bf16[8,2,128,128]{3,2,1,0:T(8,128)(2,1)S(1)}, bf16[8,2,128,128]{3,2,1,0:T(8,128)(2,1)S(1)}, u32[]{:S(2)}, u32[]{:S(2)}) collective-permute-start(bf16[8,2,128,128]{3,2,1,0:T(8,128)(2,1)S(1)} %get-tuple-element.24.refs_2_), channel_id=1, source_target_pairs={{0,32},{32,64},{64,96},{96,0},{1,33},{33,65},{65,97},{97,1},{2,34}... | collective-permute-start | bytes 1572872 | tf_op jit(solution)/shard_map/ppermute | solution.py:396
  103.9 11.2 %collective-permute-start.11 = (bf16[8,2,128,128]{3,2,1,0:T(8,128)(2,1)S(1)}, bf16[8,2,128,128]{3,2,1,0:T(8,128)(2,1)S(1)}, u32[]{:S(2)}, u32[]{:S(2)}) collective-permute-start(bf16[8,2,128,128]{3,2,1,0:T(8,128)(2,1)S(1)} %shard_map.111.refs_1_), channel_id=1, source_target_pairs={{0,1},{1,0},{2,3},{3,2},{4,5},{5,4},{6,7},{7,6},{8,9},{9,8},{10,11... | collective-permute-start | bytes 1572872 | tf_op jit(solution)/shard_map/ppermute | solution.py:405
  104.0 35.2 %collective-permute-start.5 = (bf16[8,2,128,128]{3,2,1,0:T(8,128)(2,1)S(1)}, bf16[8,2,128,128]{3,2,1,0:T(8,128)(2,1)S(1)}, u32[]{:S(2)}, u32[]{:S(2)}) collective-permute-start(bf16[8,2,128,128]{3,2,1,0:T(8,128)(2,1)S(1)} %collective-permute-done.4.refs_3_), channel_id=1, source_target_pairs={{0,96},{32,0},{64,32},{96,64},{1,97},{33,1},{65,33},{97,65},{2,98}... | collective-permute-start | bytes 1572872 | tf_op jit(solution)/shard_map/ppermute | solution.py:396
  104.1 35.2 %collective-permute-start.3 = (bf16[8,2,128,128]{3,2,1,0:T(8,128)(2,1)S(1)}, bf16[8,2,128,128]{3,2,1,0:T(8,128)(2,1)S(1)}, u32[]{:S(2)}, u32[]{:S(2)}) collective-permute-start(bf16[8,2,128,128]{3,2,1,0:T(8,128)(2,1)S(1)} %collective-permute-done.2.refs_2_), channel_id=1, source_target_pairs={{0,32},{32,64},{64,96},{96,0},{1,33},{33,65},{65,97},{97,1},{2,34}... | collective-permute-start | bytes 1572872 | tf_op jit(solution)/shard_map/ppermute | solution.py:396
  143.8 4.8 %collective-permute-start.12 = (f32[144,2304]{1,0:T(8,128)S(1)}, f32[144,2304]{1,0:T(8,128)S(1)}, u32[]{:S(2)}, u32[]{:S(2)}) collective-permute-start(f32[144,2304]{1,0:T(8,128)S(1)} %shard_map.113), channel_id=1, source_target_pairs={{0,1},{1,0},{2,3},{3,2},{4,5},{5,4},{6,7},{7,6},{8,9},{9,8},{10,11... | collective-permute-start | bytes 3981320 | tf_op jit(solution)/shard_map/ppermute | solution.py:405
  149.8 17.3 %all-to-all-start.1 = ((bf16[16,128,128]{2,1,0:T(8,128)(2,1)}), bf16[16,128,128]{2,1,0:T(8,128)(2,1)S(1)}, u32[]{:S(2)}, u32[]{:S(2)}) async-start(bf16[16,128,128]{2,1,0:T(8,128)(2,1)} %get-tuple-element.33), calls=%async_computation.1 | async-start | bytes 1048576 | tf_op jit(solution)/shard_map/all_to_all | solution.py:439
  154.6 0.7 collective-permute-start.13
Sparse Core Ops, SparseCore 0:
  54.2 63.2 all-gather.1
